TPU v7x, 128 devices: a whole 4x4x4 slice. The times are simulated.
128 devices in a mesh: rad: 8 (over z_lo, y), lat: 16 (over z_hi, x, core).
Axes of the slice: x: 4, y: 4, z: 4 (z_hi: 2, z_lo: 2; z = z_hi * 2 + z_lo), core: 2. Of those that a mesh axis runs over, the one named last changes fastest.
Arguments:
- physical: bfloat16 [256, 8, 256, 1536], P(None, None, 'rad', 'lat'), may hold values from -6 to 6
- pair_slot: int32 [128], replicated, may hold values from 0 to 127, each once
- legendre: bfloat16 [128, 1536, 1024], P('lat'), may hold values from -0.15625 to 0.15625
- spectral_state: bfloat16 [128, 8, 256, 1024], P('lat', None, None, 'rad'), may hold values from -6 to 6
- inverses: bfloat16 [4, 4, 256, 256], replicated, may hold values from -0.375 to 0.375
- block_index: int32 [128, 1024], P('lat', 'rad'), may hold values from 0 to 3
Outputs:
- new_state: bfloat16 [128, 8, 256, 1024], P('lat', None, None, 'rad')
Inputs may be any that keep to these rules, and one draw needn't show every extreme that they name: `pair_slot`: each slot is taken by exactly one pair.
All inputs are finite; a program needn't handle non-finite values.
Results may differ from a plain program's by a relative error of at most 0.0053.
Values may be sent and summed in bfloat16 or wider, within the bound.
No kernel may reach another device: no remote copies, remote signals or barrier semaphores. Data moves between devices by JAX's collectives and lax.ppermute only.
A program may use at most 192 MiB of HBM per device.

v0:
```python
import jax
import jax.numpy as jnp
from jax import lax
from jax.sharding import PartitionSpec as P


def transform(lat_whole, tables, lengths):
    per_dev = tables.shape[0]
    grouped = lat_whole.reshape((per_dev, 2) + lat_whole.shape[1:])
    low_part = jnp.einsum(
        "scrn,snj->scrj", grouped[:, 0], tables, preferred_element_type=jnp.float32
    )
    high_part = jnp.einsum(
        "scrn,snj->scrj", grouped[:, 1], tables, preferred_element_type=jnp.float32
    )
    column = jnp.arange(tables.shape[2], dtype=jnp.int32)
    chosen = column[None, None, None, :] < lengths[:, None, None, None]
    return jnp.where(chosen, low_part, high_part).astype(jnp.bfloat16)


def settle(spectral, spectral_state, inverses, block_index):
    right_side = (spectral_state.astype(jnp.float32) + 0.5 * spectral.astype(jnp.float32)).astype(
        jnp.bfloat16
    )
    results = []
    for potential in range(inverses.shape[0]):
        pot_part = right_side[:, 2 * potential : 2 * potential + 2]
        summed = jnp.zeros(pot_part.shape, jnp.float32)
        for group in range(inverses.shape[1]):
            masked = jnp.where(
                (block_index == group)[:, None, None, :], pot_part, jnp.zeros((), jnp.bfloat16)
            )
            summed = summed + jnp.einsum(
                "ab,scbj->scaj",
                inverses[potential, group],
                masked,
                preferred_element_type=jnp.float32,
            )
        results.append(summed)
    return jnp.concatenate(results, axis=1).astype(jnp.bfloat16)


def on_device(physical, pair_slot, legendre, spectral_state, inverses, block_index):
    pair_count = pair_slot.shape[0]
    per_dev = legendre.shape[0]
    degrees = legendre.shape[2]
    slot_ids = jnp.arange(pair_count, dtype=jnp.int32)
    matches = pair_slot[None, :] == slot_ids[:, None]
    owners = jnp.sum(jnp.where(matches, slot_ids[None, :], 0), axis=1)
    row_order = (2 * owners[:, None] + jnp.arange(2, dtype=jnp.int32)[None, :]).reshape(-1)
    ordered = jnp.take(physical, row_order, axis=0)
    local_slots = lax.axis_index("lat") * per_dev + jnp.arange(per_dev, dtype=jnp.int32)
    local_owners = jnp.take(owners, local_slots)
    stride = degrees // 2 // pair_count
    lengths = degrees - (1 + local_owners * stride)
    lat_whole = lax.all_to_all(ordered, "lat", split_axis=0, concat_axis=3, tiled=True)
    spectral = transform(lat_whole, legendre, lengths)
    shells = lax.all_to_all(spectral, "rad", split_axis=3, concat_axis=2, tiled=True)
    return settle(shells, spectral_state, inverses, block_index)


def solution(mesh):
    in_specs = (
        P(None, None, "rad", "lat"),
        P(),
        P("lat", None, None),
        P("lat", None, None, "rad"),
        P(),
        P("lat", "rad"),
    )
    out_specs = P("lat", None, None, "rad")
    return jax.shard_map(
        on_device, mesh=mesh, in_specs=in_specs, out_specs=out_specs, check_vma=False
    )
```

profile of v0, /device:TPU:74, one launch (start us, length us, event | category | flops | bytes accessed | tf_op | source)
XLA Modules:
  0.0 549.8 jit_solution(12415396060383862266)
XLA Ops:
  0.0 0.8 select_reduce_fusion
  0.8 0.1 iota_add_fusion
  0.9 0.1 add.171
  1.0 0.1 add.168
  1.2 22.0 %copy.70 = bf16[256,8,32,96]{3,2,1,0:T(8,128)(2,1)} copy(bf16[256,8,32,96]{0,3,2,1:T(8,128)(2,1)} %param.6) | data formatting | bytes 25165824 | tf_op args[0]
  23.2 15.5 %gather_fusion.1 = bf16[256,8,32,96]{3,2,1,0:T(8,128)(2,1)} fusion(bf16[256,8,32,96]{3,2,1,0:T(8,128)(2,1)} %copy.70, s32[1024]{0:T(1024)S(1)} %pad_clamp_fusion), kind=kCustom, calls=%fused_computation.1 | custom fusion | bytes 25166848 | tf_op jit(solution)/shard_map/jit(_take)/gather | solution.py:51
  38.7 14.2 %broadcast_select_fusion = bf16[256,8,32,96]{3,2,1,0:T(8,128)(2,1)} fusion(bf16[256,8,32,96]{3,2,1,0:T(8,128)(2,1)} %gather_fusion.1, pred[256]{0:T(512)(128)(4,1)S(1)} %compare_and_fusion), kind=kLoop, calls=%fused_computation.7 | loop fusion | flops 6291456 | bytes 25166080 | tf_op jit(solution)/shard_map/jit(_take)/select_n | solution.py:51
  52.9 7.3 %all-to-all-start = ((bf16[256,8,32,96]{3,2,1,0:T(8,128)(2,1)}), bf16[256,8,32,96]{3,2,1,0:T(8,128)(2,1)}, u32[]{:S(2)}, u32[]{:S(2)}) async-start(bf16[256,8,32,96]{3,2,1,0:T(8,128)(2,1)} %broadcast_select_fusion), calls=%async_computation | async-start | bytes 33554432 | tf_op jit(solution)/shard_map/all_to_all | solution.py:56
  60.2 0.6 gather_fusion
  60.9 0.1 iota_compare_fusion.1
  60.9 224.8 %all-to-all-done = bf16[256,8,32,96]{3,2,1,0:T(8,128)(2,1)} async-done(((bf16[256,8,32,96]{3,2,1,0:T(8,128)(2,1)}), bf16[256,8,32,96]{3,2,1,0:T(8,128)(2,1)}, u32[]{:S(2)}, u32[]{:S(2)}) %all-to-all-start) | async-done | bytes 12582944 | tf_op jit(solution)/shard_map/all_to_all | solution.py:56
  285.7 18.5 %copy.71 = bf16[16,8,32,16,96]{4,3,2,1,0:T(8,128)(2,1)} copy(bf16[16,8,32,16,96]{4,2,1,0,3:T(8,128)(2,1)} %bitcast.3) | data formatting | bytes 25165824 | tf_op jit(solution)/shard_map/all_to_all | solution.py:56
  304.2 27.9 %reshape.117 = bf16[8,2,8,32,1536]{4,3,2,1,0:T(8,128)(2,1)} reshape(bf16[16,8,32,16,96]{4,3,2,1,0:T(8,128)(2,1)} %copy.71) | data formatting | bytes 25165824 | tf_op jit(solution)/shard_map/reshape | solution.py:9
  332.2 17.3 %fusion = bf16[8,8,32,1024]{3,2,1,0:T(8,128)(2,1)} fusion(bf16[8,1536,1024]{2,1,0:T(8,128)(2,1)} %param.8, bf16[8,2,8,32,1536]{4,3,2,1,0:T(8,128)(2,1)} %reshape.117), kind=kOutput, calls=%fused_computation.3 | convolution fusion | flops 6442450944 | bytes 35651584 | tf_op jit(solution)/shard_map/scrn,snj->scrj/dot_general | solution.py:13
  349.5 18.0 %select_convert_fusion = bf16[8,8,32,1024]{3,2,1,0:T(8,128)(2,1)} fusion(bf16[8,8,32,1024]{3,2,1,0:T(8,128)(2,1)} %fusion, pred[8,1024]{1,0:T(8,128)(4,1)S(1)} %iota_compare_fusion.1, bf16[8,1536,1024]{2,1,0:T(8,128)(2,1)} %param.8, bf16[8,2,8,32,1536]{4,3,2,1,0:T(8,128)(2,1)} %reshape.117), kind=kOutput, calls=%fused_computation.10 | convolution fusion | flops 6444548096 | bytes 39854080 | tf_op jit(solution)/shard_map/scrn,snj->scrj/dot_general | solution.py:10
  367.5 23.1 %copy.74 = bf16[8,8,32,1024]{2,1,0,3:T(8,128)(2,1)} copy(bf16[8,8,32,1024]{3,2,1,0:T(8,128)(2,1)} %select_convert_fusion) | data formatting | bytes 8388608 | tf_op jit(solution)/shard_map/convert_element_type | solution.py:18
  390.6 18.7 %reshape.151 = bf16[8,2,131072]{2,1,0:T(2,128)(2,1)} reshape(bf16[1024,8,8,32]{3,2,1,0:T(8,128)(2,1)} %bitcast.160) | data formatting | bytes 8388608
  409.3 0.0 copy-start.1
  409.3 6.1 %all-to-all-start.1 = ((bf16[8,2,131072]{2,1,0:T(2,128)(2,1)}), bf16[8,2,131072]{2,1,0:T(2,128)(2,1)}, u32[]{:S(2)}, u32[]{:S(2)}) async-start(bf16[8,2,131072]{2,1,0:T(2,128)(2,1)} %reshape.151), calls=%async_computation.1 | async-start | bytes 8388608 | tf_op jit(solution)/shard_map/all_to_all | solution.py:58
  415.4 0.0 copy-done.1
  415.4 58.7 %all-to-all-done.1 = bf16[8,2,131072]{2,1,0:T(2,128)(2,1)} async-done(((bf16[8,2,131072]{2,1,0:T(2,128)(2,1)}), bf16[8,2,131072]{2,1,0:T(2,128)(2,1)}, u32[]{:S(2)}, u32[]{:S(2)}) %all-to-all-start.1) | async-done | bytes 4194336 | tf_op jit(solution)/shard_map/all_to_all | solution.py:58
  474.1 12.4 %reshape.152 = bf16[1024,8,8,32]{3,2,1,0:T(8,128)(2,1)} reshape(bf16[8,2,131072]{2,1,0:T(2,128)(2,1)} %all-to-all-done.1) | data formatting | bytes 8388608
  486.5 18.8 %convert_multiply_fusion = f32[8,8,32,1024]{2,1,0,3:T(8,128)} fusion(bf16[1024,8,8,32]{3,2,1,0:T(8,128)(2,1)} %reshape.152), kind=kLoop, calls=%fused_computation.2 | loop fusion | flops 4194304 | bytes 12582912 | tf_op jit(solution)/shard_map/mul | solution.py:22
  505.3 21.8 %copy.75 = f32[8,8,8,32,128]{4,3,2,1,0:T(8,128)} copy(f32[8,8,8,32,128]{3,1,0,4,2:T(8,128)} %bitcast.159) | data formatting | bytes 16777216 | tf_op jit(solution)/shard_map/mul | solution.py:22
  527.1 0.0 copy-start
  527.1 6.0 %fusion.4 = bf16[8,8,256,128]{3,2,1,0:T(8,128)(2,1)S(1)} fusion(f32[8,8,8,32,128]{4,3,2,1,0:T(8,128)} %copy.75, bf16[8,8,256,128]{3,2,1,0:T(8,128)(2,1)} %param.9), kind=kLoop, calls=%fused_computation.9 | loop fusion | flops 6291456 | bytes 16777216 | tf_op jit(solution)/shard_map/convert_element_type | solution.py:22
  533.1 0.0 copy-done
  533.1 0.5 fusion.33
  533.6 0.5 fusion.26
  534.1 0.5 fusion.35
  534.6 0.5 fusion.28
  535.1 0.5 fusion.37
  535.6 0.5 fusion.30
  536.1 0.5 fusion.19
  536.5 0.5 fusion.21
  537.0 0.5 fusion.23
  537.5 0.5 fusion.14
  538.0 0.5 fusion.16
  538.5 0.5 fusion.12
  539.0 0.5 fusion.7
  539.6 0.5 fusion.8
  540.1 0.5 fusion.9
  540.6 0.5 fusion.10
  541.2 2.2 pad_maximum_fusion
  543.4 6.4 %copy.92 = bf16[8,8,256,128]{3,2,1,0:T(8,128)(2,1)} copy(bf16[8,8,256,128]{2,3,1,0:T(8,128)(2,1)} %pad_maximum_fusion) | data formatting | bytes 8388608 | tf_op jit(solution)/shard_map/concatenate | solution.py:40
  (8 shorter events, 0.1 us)
Async XLA Ops:
  52.9 232.8 %all-to-all-start = ((bf16[256,8,32,96]{3,2,1,0:T(8,128)(2,1)}), bf16[256,8,32,96]{3,2,1,0:T(8,128)(2,1)}, u32[]{:S(2)}, u32[]{:S(2)}) async-start(bf16[256,8,32,96]{3,2,1,0:T(8,128)(2,1)} %broadcast_select_fusion), calls=%async_computation | async-start | bytes 33554432 | tf_op jit(solution)/shard_map/all_to_all | solution.py:56
  409.3 6.1 %copy-start.1 = (s32[8,128]{1,0:T(8,128)S(1)}, s32[8,128]{1,0:T(8,128)}, u32[]{:S(2)}) copy-start(s32[8,128]{1,0:T(8,128)} %param.11) | copy-start | bytes 12292
  409.3 64.8 %all-to-all-start.1 = ((bf16[8,2,131072]{2,1,0:T(2,128)(2,1)}), bf16[8,2,131072]{2,1,0:T(2,128)(2,1)}, u32[]{:S(2)}, u32[]{:S(2)}) async-start(bf16[8,2,131072]{2,1,0:T(2,128)(2,1)} %reshape.151), calls=%async_computation.1 | async-start | bytes 8388608 | tf_op jit(solution)/shard_map/all_to_all | solution.py:58
  527.1 6.0 %copy-start = (bf16[4,4,256,256]{3,2,1,0:T(8,128)(2,1)S(1)}, bf16[4,4,256,256]{3,2,1,0:T(8,128)(2,1)}, u32[]{:S(2)}) copy-start(bf16[4,4,256,256]{3,2,1,0:T(8,128)(2,1)} %param.10) | copy-start | bytes 6291460
where the time goes:
time: 555 us; the launch traced here: 550 us
  waiting for transfers between devices  283 us (51%)
  local copies, waits for them, and re-layouts  167 us (30%)
  matrix products  43.3 us (8%)
  other arithmetic  42.2 us (8%)
  starting transfers between devices  13.4 us (2%)
    all_to_all x1, waiting for transfers between devices, on_device(): lax.all_to_all(ordered, 'lat', split_axis=0, concat_axis=3, tiled=True)  225 us
    all_to_all x1, waiting for transfers between devices, on_device(): lax.all_to_all(spectral, 'rad', split_axis=3, concat_axis=2, tiled=True)  58.7 us
    unnamed x7, local copies, waits for them, and re-layouts  53.1 us
    reshape x1, local copies, waits for them, and re-layouts, transform(): grouped = lat_whole.reshape((per_dev, 2) + lat_whole.shape[1:])  27.9 us
    convert_element_type x1, local copies, waits for them, and re-layouts, transform(): return jnp.where(chosen, low_part, high_part).astype(jnp.bfloat16)  23.1 us
    mul x1, local copies, waits for them, and re-layouts, settle(): 0.5 * spectral.astype(jnp.float32)  21.8 us
    mul x1, other arithmetic, settle(): 0.5 * spectral.astype(jnp.float32)  18.8 us
    all_to_all x1, local copies, waits for them, and re-layouts, on_device(): lax.all_to_all(ordered, 'lat', split_axis=0, concat_axis=3, tiled=True)  18.5 us
  transfers between devices with their start and end apart: 2, of which 2 were waited for; matrix products, arithmetic and copies ran while one was open for 0% of the time, Pallas kernels for 0%

commit v1 on v0

v1 whole, which is shorter than its diff:
```python
import functools

import jax
import jax.numpy as jnp
from jax import lax
from jax.experimental import pallas as pl
from jax.experimental.pallas import tpu as pltpu
from jax.sharding import PartitionSpec as P

ZS, Y = 2, 4
CHUNKS = (2, 2, 2, 1, 1)
STEP = 16
BF16, F32 = jnp.bfloat16, jnp.float32


def prep_kernel(starts, key_ref, x_ref, *refs):
    outs, (pick, wide, tall) = refs[: len(starts)], refs[len(starts) :]
    rows, step, orders = x_ref.shape
    per_dev = sum(n for _, n in starts)

    @pl.when(pl.program_id(0) == 0)
    def _():
        at = 0
        for first, n in starts:
            count = 16 * n * 2
            i = lax.broadcasted_iota(jnp.int32, (count, orders), 0)
            dest, rest = i // (2 * n), i % (2 * n)
            target = dest * (2 * per_dev) + 2 * first + rest
            hit = key_ref[...] == target
            pick[at : at + count, :] = jnp.where(hit, 1.0, 0.0).astype(BF16)
            at += count

    for lane in range(2):
        cols = slice(lane * 128, (lane + 1) * 128)
        wide[lane] = x_ref[:, :, cols].astype(F32).reshape(rows * step, 128)

    def body(n, carry):
        one = [wide[lane, pl.ds(n, rows, stride=step), :].astype(BF16) for lane in range(2)]
        moved = lax.dot_general(
            pick[...],
            jnp.concatenate(one, axis=1),
            (((1,), (1,)), ((), ())),
            preferred_element_type=F32,
        )
        for lane in range(2):
            cols = slice(lane * 128, (lane + 1) * 128)
            tall[lane, pl.ds(n, orders, stride=step), :] = moved[:, cols]
        return carry

    lax.fori_loop(0, step, body, 0)
    at = 0
    for out, (_, n) in zip(outs, starts):
        count = 16 * n * 2
        for lane in range(2):
            cols = slice(lane * 128, (lane + 1) * 128)
            part = tall[lane, at * step : (at + count) * step, :].astype(BF16)
            out[:, :, :, :, cols] = part.reshape(out.shape[:4] + (128,))
        at += count


def prep(physical, pair_slot, starts):
    orders, chans, radii, lats = physical.shape
    rows = chans * radii
    x = jnp.transpose(physical, (1, 2, 3, 0)).reshape(rows, lats, orders)
    key = (2 * pair_slot[:, None] + jnp.arange(2, dtype=jnp.int32)[None, :]).reshape(1, orders)
    return pl.pallas_call(
        functools.partial(prep_kernel, starts),
        grid=(lats // STEP,),
        in_specs=[
            pl.BlockSpec((1, orders), lambda b: (0, 0)),
            pl.BlockSpec((rows, STEP, orders), lambda b: (0, b, 0)),
        ],
        out_specs=[
            pl.BlockSpec((16, n, 2, STEP, rows), lambda b: (0, 0, 0, b, 0)) for _, n in starts
        ],
        out_shape=[jax.ShapeDtypeStruct((16, n, 2, lats, rows), BF16) for _, n in starts],
        scratch_shapes=[
            pltpu.VMEM((orders, orders), BF16),
            pltpu.VMEM((2, rows * STEP, 128), F32),
            pltpu.VMEM((2, orders * STEP, 128), F32),
        ],
        compiler_params=pltpu.CompilerParams(vmem_limit_bytes=48 << 20),
        cost_estimate=pl.CostEstimate(
            flops=2 * rows * lats * orders * orders,
            bytes_accessed=4 * rows * lats * orders,
            transcendentals=0,
        ),
        name="prep",
    )(key, x)


def transform_kernel(meta_ref, got_ref, table_ref, *refs):
    outs, full = refs[:8], refs[8]
    slot = pl.program_id(0)
    half = table_ref.shape[2] // 2
    depth = table_ref.shape[1]
    rows = got_ref.shape[4]
    low_in = got_ref[:, 0, 0].reshape(depth, rows)
    high_in = got_ref[:, 0, 1].reshape(depth, rows)
    length = meta_ref[9 + slot]
    dims = (((0,), (0,)), ((), ()))
    left = table_ref[0, :, :half]
    right = table_ref[0, :, half:]
    full[:, :half] = lax.dot_general(low_in, left, dims, preferred_element_type=F32).astype(BF16)
    low = lax.dot_general(low_in, right, dims, preferred_element_type=F32)
    high = lax.dot_general(high_in, right, dims, preferred_element_type=F32)
    column = half + lax.broadcasted_iota(jnp.int32, low.shape, 1)
    full[:, half:] = jnp.where(column < length, low, high).astype(BF16)
    for k in range(8):
        at = pl.multiple_of(meta_ref[1 + k] * 128, 128)
        outs[k][0, 0] = full[:, pl.ds(at, 128)]


def transform(got, legendre, meta, first):
    srcs, count, _, lats, rows = got.shape
    degrees = legendre.shape[2]
    depth = srcs // 2 * lats
    shape = (2, count, rows, 128)
    return pl.pallas_call(
        transform_kernel,
        grid_spec=pltpu.PrefetchScalarGridSpec(
            num_scalar_prefetch=1,
            grid=(count, 2),
            in_specs=[
                pl.BlockSpec(
                    (srcs // 2, 1, 2, lats, rows), lambda s, t, m: (t ^ m[0], s, 0, 0, 0)
                ),
                pl.BlockSpec((1, depth, degrees), lambda s, t, m: (first + s, t ^ m[0], 0)),
            ],
            out_specs=[pl.BlockSpec((1, 1, rows, 128), lambda s, t, m: (t, s, 0, 0))] * 8,
            scratch_shapes=[pltpu.VMEM((rows, degrees), BF16)],
        ),
        out_shape=[jax.ShapeDtypeStruct(shape, BF16)] * 8,
        compiler_params=pltpu.CompilerParams(vmem_limit_bytes=48 << 20),
        cost_estimate=pl.CostEstimate(
            flops=3 * 2 * count * rows * depth * degrees,
            bytes_accessed=4 * count * (2 * depth * rows * 2 + depth * degrees + rows * degrees),
            transcendentals=0,
        ),
        name="transform",
    )(meta, got, legendre)


def settle_kernel(first, meta_ref, *refs):
    parts = refs[:8]
    state_ref, index_ref, inv_ref = refs[8:11]
    out_ref, side = refs[-2], refs[-1]
    zl, y = meta_ref[0], meta_ref[1]
    radii = 32
    for ky in range(Y):
        near, far = parts[ky], parts[Y + ky]
        y_from = lax.rem(y + (Y - ky), Y)
        for t in range(2):
            at = pl.multiple_of(((zl ^ t) * Y + y_from) * radii, radii)
            for c in range(8):
                rows = slice(c * radii, (c + 1) * radii)
                total = near[t, 0, rows, :].astype(F32) + far[1 - t, 0, rows, :].astype(F32)
                value = state_ref[0, c, pl.ds(at, radii), :].astype(F32) + 0.5 * total
                lanes = slice((c % 2) * 128, (c % 2) * 128 + 128)
                side[c // 2, pl.ds(at, radii), lanes] = value.astype(BF16)
    row = index_ref[pl.ds(first + pl.program_id(0), 1), :]
    row = jnp.concatenate([row, row], axis=1)
    for q in range(4):
        acc = None
        for g in range(4):
            one = jnp.dot(inv_ref[q, g], side[q], preferred_element_type=F32)
            acc = one if acc is None else jnp.where(row == g, one, acc)
        acc = acc.astype(BF16)
        out_ref[0, 2 * q] = acc[:, :128]
        out_ref[0, 2 * q + 1] = acc[:, 128:]


def settle(parts, state, inverses, index, meta, first, so_far):
    count = parts[0].shape[1]
    block = pl.BlockSpec((2, 1) + parts[0].shape[2:], lambda s, m: (0, s, 0, 0))
    operands = [meta, *parts, state, index, inverses]
    in_specs = [block] * 8 + [
        pl.BlockSpec((1,) + state.shape[1:], lambda s, m: (first + s, 0, 0, 0)),
        pl.BlockSpec(index.shape, lambda s, m: (0, 0)),
        pl.BlockSpec(inverses.shape, lambda s, m: (0, 0, 0, 0)),
    ]
    aliases = {}
    if so_far is not None:
        operands.append(so_far)
        in_specs.append(pl.BlockSpec(memory_space=pl.ANY))
        aliases = {len(operands) - 1: 0}
    return pl.pallas_call(
        functools.partial(settle_kernel, first),
        grid_spec=pltpu.PrefetchScalarGridSpec(
            num_scalar_prefetch=1,
            grid=(count,),
            in_specs=in_specs,
            out_specs=pl.BlockSpec((1,) + state.shape[1:], lambda s, m: (first + s, 0, 0, 0)),
            scratch_shapes=[pltpu.VMEM((4, 256, 256), BF16)],
        ),
        out_shape=jax.ShapeDtypeStruct(state.shape, BF16),
        input_output_aliases=aliases,
        compiler_params=pltpu.CompilerParams(vmem_limit_bytes=48 << 20),
        cost_estimate=pl.CostEstimate(
            flops=2 * count * 16 * 256 * 256 * 256,
            bytes_accessed=count * (2 << 20) + (2 << 20),
            transcendentals=0,
        ),
        name="settle",
    )(*operands)


def flip_groups():
    groups = []
    for y in range(Y):
        for zl in range(ZS):
            groups.append([((zl ^ (l // 8)) * Y + y) * 16 + l for l in range(16)])
    return groups


def rad_targets(kz, ky):
    return [(i, ((i // Y) ^ kz) * Y + (i % Y + ky) % Y) for i in range(ZS * Y)]


def on_device(physical, pair_slot, legendre, spectral_state, inverses, block_index):
    pair_count = pair_slot.shape[0]
    per_dev, _, degrees = legendre.shape
    starts, first = [], 0
    for n in CHUNKS:
        starts.append((first, n))
        first += n
    sends = prep(physical, pair_slot, tuple(starts))

    lat, rad = lax.axis_index("lat"), lax.axis_index("rad")
    zl, y = rad // Y, rad % Y
    slots = lat * per_dev + jnp.arange(per_dev, dtype=jnp.int32)
    matches = pair_slot[None, :] == slots[:, None]
    owners = jnp.sum(jnp.where(matches, jnp.arange(pair_count, dtype=jnp.int32), 0), axis=1)
    stride = degrees // 2 // pair_count
    lengths = degrees - (1 + owners * stride)
    hops = jnp.arange(8, dtype=jnp.int32)
    blocks = (zl ^ (hops // Y)) * Y + (y + hops) % Y
    place = jnp.stack([zl, y]).astype(jnp.int32)

    out = None
    for send, (first, n) in zip(sends, starts):
        got = lax.all_to_all(
            send, ("rad", "lat"), 0, 0, tiled=True, axis_index_groups=flip_groups()
        )
        meta = jnp.concatenate(
            [(lat // 8)[None], blocks, lengths[first : first + n]]
        ).astype(jnp.int32)
        parts = transform(got, legendre, meta, first)
        moved = [parts[0]] + [
            lax.ppermute(parts[k], "rad", rad_targets(k // Y, k % Y)) for k in range(1, 8)
        ]
        out = settle(moved, spectral_state, inverses, block_index, place, first, out)
    return out


def solution(mesh):
    in_specs = (
        P(None, None, "rad", "lat"),
        P(),
        P("lat", None, None),
        P("lat", None, None, "rad"),
        P(),
        P("lat", "rad"),
    )
    out_specs = P("lat", None, None, "rad")
    return jax.shard_map(
        on_device, mesh=mesh, in_specs=in_specs, out_specs=out_specs, check_vma=False
    )
```

time: 555 us -> 345 us (0.62)
  waiting for transfers between devices: 283 us -> 15.8 us
  local copies, waits for them, and re-layouts: 167 us -> 17.8 us
  blocking collectives: 0 us -> 135 us
  Pallas kernels: 0 us -> 94.1 us
  starting transfers between devices: 13.4 us -> 75.7 us
  matrix products: 43.3 us -> 0 us
  other arithmetic: 42.2 us -> 2.5 us
    all_to_all x2 -> x1, waiting for transfers between devices: 283 us -> 0.01 us  [on_device(): lax.all_to_all(send, ('rad', 'lat'), 0, 0, tiled=True, axis_index_groups=...]
    all_to_all x0 -> x4, blocking collectives: none -> 135 us  [on_device(): lax.all_to_all(send, ('rad', 'lat'), 0, 0, tiled=True, axis_index_groups=...]
    pallas_call x0 -> x11, Pallas kernels: none -> 94.1 us  [the longest x1 44.1 us: prep(): pl.pallas_call(functools.partial(prep_kernel, starts), grid=(lats // STEP...]
    ppermute x0 -> x35, starting transfers between devices: none -> 68.7 us  [on_device(): lax.ppermute(parts[k], 'rad', rad_targets(k // Y, k % Y))]
    dot_general x18 -> x0, matrix products: 43.3 us -> none  [the longest x1 18 us: transform(): jnp.einsum('scrn,snj->scrj', grouped[:, 0], tables, preferred_element_typ...]
    unnamed x7 -> x118, local copies, waits for them, and re-layouts: 53.1 us -> 16.9 us
    reshape x1 -> x0, local copies, waits for them, and re-layouts: 27.9 us -> none  [transform(): grouped = lat_whole.reshape((per_dev, 2) + lat_whole.shape[1:])]
    convert_element_type x1 -> x0, local copies, waits for them, and re-layouts: 23.1 us -> none  [transform(): return jnp.where(chosen, low_part, high_part).astype(jnp.bfloat16)]
  transfers between devices with their start and end apart: 2 -> 36, of which waited for: 2 -> 1; matrix products, arithmetic and copies ran while one was open for 0% -> 1% of each run, Pallas kernels for 0% -> 14%
where the time goes in v1:
time: 345 us; the launch traced here: 341 us
  blocking collectives  135 us (39%)
  Pallas kernels  94.1 us (27%)
  starting transfers between devices  75.7 us (22%)
  local copies, waits for them, and re-layouts  17.8 us (5%)
  waiting for transfers between devices  15.8 us (5%)
    all_to_all x4, blocking collectives, on_device(): lax.all_to_all(send, ('rad', 'lat'), 0, 0, tiled=True, axis_index_groups=...  135 us
    ppermute x35, starting transfers between devices, on_device(): lax.ppermute(parts[k], 'rad', rad_targets(k // Y, k % Y))  68.7 us
    pallas_call x1, Pallas kernels, prep(): pl.pallas_call(functools.partial(prep_kernel, starts), grid=(lats // STEP...  44.1 us
    pallas_call x5, Pallas kernels, transform(): pl.pallas_call(transform_kernel, grid_spec=pltpu.PrefetchScalarGridSpec(n...  29.7 us
    pallas_call x5, Pallas kernels, settle(): pl.pallas_call(functools.partial(settle_kernel, first), grid_spec=pltpu.P...  20.3 us
    unnamed x118, local copies, waits for them, and re-layouts  16.9 us
    ppermute x35, waiting for transfers between devices, on_device(): lax.ppermute(parts[k], 'rad', rad_targets(k // Y, k % Y))  15.8 us
    all_to_all x1, starting transfers between devices, on_device(): lax.all_to_all(send, ('rad', 'lat'), 0, 0, tiled=True, axis_index_groups=...  6.97 us
  transfers between devices with their start and end apart: 36, of which 1 were waited for; matrix products, arithmetic and copies ran while one was open for 1% of the time, Pallas kernels for 14%

profile of v1, /device:TPU:74, one launch (start us, length us, event | category | flops | bytes accessed | tf_op | source)
XLA Modules:
  0.0 341.4 jit_solution(156342505715972312)
XLA Ops:
  0.0 0.7 broadcast_multiply_fusion
  0.9 44.1 %prep.1 = (bf16[16,2,2,96,256]{4,3,2,1,0:T(8,128)(2,1)}, bf16[16,2,2,96,256]{4,3,2,1,0:T(8,128)(2,1)}, bf16[16,2,2,96,256]{4,3,2,1,0:T(8,128)(2,1)}, bf16[16,1,2...) custom-call(s32[1,256]{1,0:T(1,128)S(1)} %add.69.key_ref, bf16[256,96,256]{2,1,0:T(8,128)(2,1)} %bitcast.6), custom_call_target="tpu_custom_call" | custom-call | flops 3221225472 | bytes 25165824 | tf_op jit(solution)/shard_map/prep/pallas_call | solution.py:66
  45.0 24.8 %all_to_all.25.got_ref = bf16[16,1,2,96,256]{4,3,2,1,0:T(8,128)(2,1)} all-to-all(bf16[16,1,2,96,256]{4,3,2,1,0:T(8,128)(2,1)S(1)} %get-tuple-element.50), channel_id=1, replica_groups={{0,1,2,3,4,5,6,7,72,73,74,75,76,77,78,79},{64,65,66,67,68,69,70,71,8,9,..., dimensions={0} | all-to-all | bytes 3145728 | tf_op jit(solution)/shard_map/all_to_all | solution.py:242
  69.9 25.4 %all_to_all.26.got_ref = bf16[16,1,2,96,256]{4,3,2,1,0:T(8,128)(2,1)} all-to-all(bf16[16,1,2,96,256]{4,3,2,1,0:T(8,128)(2,1)S(1)} %get-tuple-element.59), channel_id=1, replica_groups={{0,1,2,3,4,5,6,7,72,73,74,75,76,77,78,79},{64,65,66,67,68,69,70,71,8,9,..., dimensions={0} | all-to-all | bytes 3145728 | tf_op jit(solution)/shard_map/all_to_all | solution.py:242
  95.3 42.6 %all_to_all.27.got_ref = bf16[16,2,2,96,256]{4,3,2,1,0:T(8,128)(2,1)} all-to-all(bf16[16,2,2,96,256]{4,3,2,1,0:T(8,128)(2,1)S(1)} %copy-done.57), channel_id=1, replica_groups={{0,1,2,3,4,5,6,7,72,73,74,75,76,77,78,79},{64,65,66,67,68,69,70,71,8,9,..., dimensions={0} | all-to-all | bytes 6291456 | tf_op jit(solution)/shard_map/all_to_all | solution.py:242
  137.8 42.3 %all_to_all.28.got_ref = bf16[16,2,2,96,256]{4,3,2,1,0:T(8,128)(2,1)} all-to-all(bf16[16,2,2,96,256]{4,3,2,1,0:T(8,128)(2,1)S(1)} %copy-done.56), channel_id=1, replica_groups={{0,1,2,3,4,5,6,7,72,73,74,75,76,77,78,79},{64,65,66,67,68,69,70,71,8,9,..., dimensions={0} | all-to-all | bytes 6291456 | tf_op jit(solution)/shard_map/all_to_all | solution.py:242
  180.1 7.0 %all-to-all-start.2 = ((bf16[16,2,2,96,256]{4,3,2,1,0:T(8,128)(2,1)}), bf16[16,2,2,96,256]{4,3,2,1,0:T(8,128)(2,1)S(1)}, u32[]{:S(2)}, u32[]{:S(2)}) async-start(bf16[16,2,2,96,256]{4,3,2,1,0:T(8,128)(2,1)} %get-tuple-element.68), calls=%async_computation.2 | async-start | bytes 6291456 | tf_op jit(solution)/shard_map/all_to_all | solution.py:242
  187.3 0.7 fusion.5
  188.0 1.4 pad_add_fusion.3
  189.6 1.4 copy-done.4
  191.0 4.2 %transform.6 = (bf16[2,1,256,128]{3,2,1,0:T(8,128)(2,1)S(1)}, bf16[2,1,256,128]{3,2,1,0:T(8,128)(2,1)S(1)}, bf16[2,1,256,128]{3,2,1,0:T(8,128)(2,1)S(1)}, bf16[2...) custom-call(s32[10]{0:T(128)S(1)} %get-tuple-element.101.meta_ref, ...), custom_call_target="tpu_custom_call" | custom-call | flops 1207959552 | bytes 7340032 | tf_op jit(solution)/shard_map/transform/pallas_call | solution.py:119
  195.2 1.6 collective-permute-start.7
  196.8 1.0 collective-permute-start.8
  197.8 2.4 collective-permute-start.9
  200.2 7.7 %collective-permute-start.10 = (bf16[2,1,256,128]{3,2,1,0:T(8,128)(2,1)S(1)}, bf16[2,1,256,128]{3,2,1,0:T(8,128)(2,1)S(1)}, u32[]{:S(2)}, u32[]{:S(2)}) collective-permute-start(bf16[2,1,256,128]{3,2,1,0:T(8,128)(2,1)S(1)} %get-tuple-element.64), channel_id=1, source_target_pairs={{0,64},{16,80},{32,96},{48,112},{64,0},{80,16},{96,32},{112,48},{1... | collective-permute-start | bytes 393224 | tf_op jit(solution)/shard_map/ppermute | solution.py:250
  207.9 7.2 %transform.9 = (bf16[2,2,256,128]{3,2,1,0:T(8,128)(2,1)S(1)}, bf16[2,2,256,128]{3,2,1,0:T(8,128)(2,1)S(1)}, bf16[2,2,256,128]{3,2,1,0:T(8,128)(2,1)S(1)}, bf16[2...) custom-call(s32[11]{0:T(128)S(1)} %get-tuple-element.95.meta_ref, ...), custom_call_target="tpu_custom_call" | custom-call | flops 2415919104 | bytes 14680064 | tf_op jit(solution)/shard_map/transform/pallas_call | solution.py:119
  215.0 0.7 copy-done.5
  215.9 4.2 %transform.5 = (bf16[2,1,256,128]{3,2,1,0:T(8,128)(2,1)S(1)}, bf16[2,1,256,128]{3,2,1,0:T(8,128)(2,1)S(1)}, bf16[2,1,256,128]{3,2,1,0:T(8,128)(2,1)S(1)}, bf16[2...) custom-call(s32[10]{0:T(128)S(1)} %get-tuple-element.102.meta_ref, ...), custom_call_target="tpu_custom_call" | custom-call | flops 1207959552 | bytes 7340032 | tf_op jit(solution)/shard_map/transform/pallas_call | solution.py:119
  220.8 0.6 copy-done.46
  223.4 0.6 copy-done.54
  224.0 0.6 copy-done.21
  224.7 4.8 %collective-permute-start.12 = (bf16[2,1,256,128]{3,2,1,0:T(8,128)(2,1)S(1)}, bf16[2,1,256,128]{3,2,1,0:T(8,128)(2,1)S(1)}, u32[]{:S(2)}, u32[]{:S(2)}) collective-permute-start(bf16[2,1,256,128]{3,2,1,0:T(8,128)(2,1)S(1)} %get-tuple-element.66), channel_id=1, source_target_pairs={{0,96},{16,112},{32,64},{48,80},{64,32},{80,48},{96,0},{112,16},{1... | collective-permute-start | bytes 393224 | tf_op jit(solution)/shard_map/ppermute | solution.py:250
  229.5 0.7 copy-done.23
  230.1 1.4 collective-permute-start.13
  231.5 0.7 copy-done.25
  232.3 0.7 copy-done.27
  232.9 2.6 collective-permute-start.1
  235.5 0.7 copy-done.35
  236.1 1.0 collective-permute-start.29
  237.7 2.3 collective-permute-start.30
  240.0 0.6 copy-done.31
  240.7 2.1 collective-permute-start.31
  242.8 0.7 copy-done.33
  243.7 6.9 %collective-permute-start.33 = (bf16[2,2,256,128]{3,2,1,0:T(8,128)(2,1)S(1)}, bf16[2,2,256,128]{3,2,1,0:T(8,128)(2,1)S(1)}, u32[]{:S(2)}, u32[]{:S(2)}) collective-permute-start(bf16[2,2,256,128]{3,2,1,0:T(8,128)(2,1)S(1)} %get-tuple-element.93), channel_id=1, source_target_pairs={{0,96},{16,112},{32,64},{48,80},{64,32},{80,48},{96,0},{112,16},{1... | collective-permute-start | bytes 786440 | tf_op jit(solution)/shard_map/ppermute | solution.py:250
  250.6 7.2 %transform.8 = (bf16[2,2,256,128]{3,2,1,0:T(8,128)(2,1)S(1)}, bf16[2,2,256,128]{3,2,1,0:T(8,128)(2,1)}, bf16[2,2,256,128]{3,2,1,0:T(8,128)(2,1)}, bf16[2,2,256,1...) custom-call(s32[11]{0:T(128)S(1)} %get-tuple-element.96.meta_ref, ...), custom_call_target="tpu_custom_call" | custom-call | flops 2415919104 | bytes 14680064 | tf_op jit(solution)/shard_map/transform/pallas_call | solution.py:119
  257.8 0.7 copy-done.40
  258.5 0.7 copy-done.42
  259.2 0.7 copy-done.44
  259.9 0.7 copy-done.9
  260.6 0.7 copy-done.11
  261.3 3.5 %collective-permute-start.21 = (bf16[2,2,256,128]{3,2,1,0:T(8,128)(2,1)}, bf16[2,2,256,128]{3,2,1,0:T(8,128)(2,1)}, u32[]{:S(2)}, u32[]{:S(2)}) collective-permute-start(bf16[2,2,256,128]{3,2,1,0:T(8,128)(2,1)} %get-tuple-element.79), channel_id=1, source_target_pairs={{0,16},{16,32},{32,48},{48,0},{64,80},{80,96},{96,112},{112,64},{1... | collective-permute-start | bytes 786440 | tf_op jit(solution)/shard_map/ppermute | solution.py:250
  264.8 0.7 copy-done.13
  265.5 0.7 copy-done.15
  266.2 2.1 collective-permute-start.23
  268.3 0.7 copy-done.17
  269.1 6.9 %transform.7 = (bf16[2,2,256,128]{3,2,1,0:T(8,128)(2,1)S(1)}, bf16[2,2,256,128]{3,2,1,0:T(8,128)(2,1)S(1)}, bf16[2,2,256,128]{3,2,1,0:T(8,128)(2,1)S(1)}, bf16[2...) custom-call(s32[11]{0:T(128)S(1)} %get-tuple-element.97.meta_ref, ...), custom_call_target="tpu_custom_call" | custom-call | flops 2415919104 | bytes 14680064 | tf_op jit(solution)/shard_map/transform/pallas_call | solution.py:119
  276.1 1.5 collective-permute-start.25
  277.5 4.2 %collective-permute-start.26 = (bf16[2,2,256,128]{3,2,1,0:T(8,128)(2,1)S(1)}, bf16[2,2,256,128]{3,2,1,0:T(8,128)(2,1)S(1)}, u32[]{:S(2)}, u32[]{:S(2)}) collective-permute-start(bf16[2,2,256,128]{3,2,1,0:T(8,128)(2,1)S(1)} %copy-done.43), channel_id=1, source_target_pairs={{0,96},{16,112},{32,64},{48,80},{64,32},{80,48},{96,0},{112,16},{1... | collective-permute-start | bytes 786440 | tf_op jit(solution)/shard_map/ppermute | solution.py:250
  281.7 0.8 collective-permute-start.27
  282.6 2.6 collective-permute-start.14
  285.2 15.7 %collective-permute-done.24.refs_4_ = bf16[2,2,256,128]{3,2,1,0:T(8,128)(2,1)} collective-permute-done((bf16[2,2,256,128]{3,2,1,0:T(8,128)(2,1)}, bf16[2,2,256,128]{3,2,1,0:T(8,128)(2,1)}, u32[]{:S(2)}, u32[]{:S(2)}) %collective-permute-start.24) | collective-permute-done | bytes 262176 | tf_op jit(solution)/shard_map/ppermute | solution.py:250
  300.9 3.7 %collective-permute-start.16 = (bf16[2,2,256,128]{3,2,1,0:T(8,128)(2,1)S(1)}, bf16[2,2,256,128]{3,2,1,0:T(8,128)(2,1)S(1)}, u32[]{:S(2)}, u32[]{:S(2)}) collective-permute-start(bf16[2,2,256,128]{3,2,1,0:T(8,128)(2,1)S(1)} %get-tuple-element.72), channel_id=1, source_target_pairs={{0,48},{16,0},{32,16},{48,32},{64,112},{80,64},{96,80},{112,96},{1... | collective-permute-start | bytes 786440 | tf_op jit(solution)/shard_map/ppermute | solution.py:250
  304.6 3.0 collective-permute-start.18
  307.6 1.5 collective-permute-start.19
  309.0 5.1 %collective-permute-start.20 = (bf16[2,2,256,128]{3,2,1,0:T(8,128)(2,1)S(1)}, bf16[2,2,256,128]{3,2,1,0:T(8,128)(2,1)S(1)}, u32[]{:S(2)}, u32[]{:S(2)}) collective-permute-start(bf16[2,2,256,128]{3,2,1,0:T(8,128)(2,1)S(1)} %get-tuple-element.76), channel_id=1, source_target_pairs={{0,112},{16,64},{32,80},{48,96},{64,48},{80,0},{96,16},{112,32},{1... | collective-permute-start | bytes 786440 | tf_op jit(solution)/shard_map/ppermute | solution.py:250
  314.3 4.5 %settle.5.refs_11_ = bf16[8,8,256,128]{3,2,1,0:T(8,128)(2,1)} custom-call(s32[2]{0:T(128)S(1)} %pad_add_fusion.meta_ref, bf16[2,2,256,128]{3,2,1,0:T(8,128)(2,1)S(1)} %copy-done.6, bf16[2,2,256,128]{3,2,1,0:T(8,128)(2,1)S(1)} %copy-done.8, bf16[2,2,256,128]{3,2,1,0:T(8,128)(2,1)S(1)} %copy-done.10, bf16[2,2,256,128]{3,2,1,0:T(8,128)(2,1)S(1)} %copy-done.12, ...), custom_call_target="tpu_custom_call" | custom-call | flops 1073741824 | bytes 6291456 | tf_op jit(solution)/shard_map/settle/pallas_call | solution.py:187
  318.8 4.7 %settle.6.refs_11_ = bf16[8,8,256,128]{3,2,1,0:T(8,128)(2,1)} custom-call(s32[2]{0:T(128)S(1)} %pad_add_fusion.meta_ref, bf16[2,2,256,128]{3,2,1,0:T(8,128)(2,1)S(1)} %get-tuple-element.78.refs_0_, bf16[2,2,256,128]{3,2,1,0:T(8,128)(2,1)} %collective-permute-done.21.refs_1_, ...), custom_call_target="tpu_custom_call", output_to_operand_aliasing={{}: (12, {})} | custom-call | flops 1073741824 | bytes 6291456 | tf_op jit(solution)/shard_map/settle/pallas_call | solution.py:187
  323.6 1.4 collective-permute-start.3
  325.0 2.1 collective-permute-start.4
  327.0 2.2 collective-permute-start.5
  329.2 0.9 collective-permute-start.6
  330.1 4.5 %settle.7.refs_11_ = bf16[8,8,256,128]{3,2,1,0:T(8,128)(2,1)} custom-call(s32[2]{0:T(128)S(1)} %pad_add_fusion.meta_ref, bf16[2,2,256,128]{3,2,1,0:T(8,128)(2,1)S(1)} %get-tuple-element.69.refs_0_, bf16[2,2,256,128]{3,2,1,0:T(8,128)(2,1)S(1)} %collective-permute-done.14.refs_1_, ...), custom_call_target="tpu_custom_call", output_to_operand_aliasing={{}: (12, {})} | custom-call | flops 1073741824 | bytes 6291456 | tf_op jit(solution)/shard_map/settle/pallas_call | solution.py:187
  334.7 3.4 settle.8.refs_11_
  338.1 3.4 settle.9
  (153 shorter events, 4.7 us)
Async XLA Ops:
  45.0 50.2 %copy-start.57 = (bf16[16,2,2,96,256]{4,3,2,1,0:T(8,128)(2,1)S(1)}, bf16[16,2,2,96,256]{4,3,2,1,0:T(8,128)(2,1)}, u32[]{:S(2)}) copy-start(bf16[16,2,2,96,256]{4,3,2,1,0:T(8,128)(2,1)} %get-tuple-element.77) | copy-start | bytes 9437188
  95.3 42.6 %copy-start.56 = (bf16[16,2,2,96,256]{4,3,2,1,0:T(8,128)(2,1)S(1)}, bf16[16,2,2,96,256]{4,3,2,1,0:T(8,128)(2,1)}, u32[]{:S(2)}) copy-start(bf16[16,2,2,96,256]{4,3,2,1,0:T(8,128)(2,1)} %get-tuple-element.86) | copy-start | bytes 9437188
  180.1 7.0 %copy-start.58 = (s32[128]{0:T(128)S(1)}, s32[128]{0:T(128)}, u32[]{:S(2)}) copy-start(s32[128]{0:T(128)} %param.7) | copy-start | bytes 1540
  180.1 88.9 %all-to-all-start.2 = ((bf16[16,2,2,96,256]{4,3,2,1,0:T(8,128)(2,1)}), bf16[16,2,2,96,256]{4,3,2,1,0:T(8,128)(2,1)S(1)}, u32[]{:S(2)}, u32[]{:S(2)}) async-start(bf16[16,2,2,96,256]{4,3,2,1,0:T(8,128)(2,1)} %get-tuple-element.68), calls=%async_computation.2 | async-start | bytes 6291456 | tf_op jit(solution)/shard_map/all_to_all | solution.py:242
  191.0 16.9 %copy-start.2 = (bf16[16,2,2,96,256]{4,3,2,1,0:T(8,128)(2,1)S(1)}, bf16[16,2,2,96,256]{4,3,2,1,0:T(8,128)(2,1)}, u32[]{:S(2)}) copy-start(bf16[16,2,2,96,256]{4,3,2,1,0:T(8,128)(2,1)} %all_to_all.28.got_ref) | copy-start | bytes 9437188
  195.2 20.6 %collective-permute-start.7 = (bf16[2,1,256,128]{3,2,1,0:T(8,128)(2,1)S(1)}, bf16[2,1,256,128]{3,2,1,0:T(8,128)(2,1)S(1)}, u32[]{:S(2)}, u32[]{:S(2)}) collective-permute-start(bf16[2,1,256,128]{3,2,1,0:T(8,128)(2,1)S(1)} %get-tuple-element.61), channel_id=1, source_target_pairs={{0,16},{16,32},{32,48},{48,0},{64,80},{80,96},{96,112},{112,64},{1... | collective-permute-start | bytes 393224 | tf_op jit(solution)/shard_map/ppermute | solution.py:250
  196.8 27.2 %collective-permute-start.8 = (bf16[2,1,256,128]{3,2,1,0:T(8,128)(2,1)S(1)}, bf16[2,1,256,128]{3,2,1,0:T(8,128)(2,1)S(1)}, u32[]{:S(2)}, u32[]{:S(2)}) collective-permute-start(bf16[2,1,256,128]{3,2,1,0:T(8,128)(2,1)S(1)} %get-tuple-element.62), channel_id=1, source_target_pairs={{0,32},{16,48},{32,0},{48,16},{64,96},{80,112},{96,64},{112,80},{1... | collective-permute-start | bytes 393224 | tf_op jit(solution)/shard_map/ppermute | solution.py:250
  197.8 31.7 %collective-permute-start.9 = (bf16[2,1,256,128]{3,2,1,0:T(8,128)(2,1)S(1)}, bf16[2,1,256,128]{3,2,1,0:T(8,128)(2,1)S(1)}, u32[]{:S(2)}, u32[]{:S(2)}) collective-permute-start(bf16[2,1,256,128]{3,2,1,0:T(8,128)(2,1)S(1)} %get-tuple-element.63), channel_id=1, source_target_pairs={{0,48},{16,0},{32,16},{48,32},{64,112},{80,64},{96,80},{112,96},{1... | collective-permute-start | bytes 393224 | tf_op jit(solution)/shard_map/ppermute | solution.py:250
  200.2 31.4 %collective-permute-start.10 = (bf16[2,1,256,128]{3,2,1,0:T(8,128)(2,1)S(1)}, bf16[2,1,256,128]{3,2,1,0:T(8,128)(2,1)S(1)}, u32[]{:S(2)}, u32[]{:S(2)}) collective-permute-start(bf16[2,1,256,128]{3,2,1,0:T(8,128)(2,1)S(1)} %get-tuple-element.64), channel_id=1, source_target_pairs={{0,64},{16,80},{32,96},{48,112},{64,0},{80,16},{96,32},{112,48},{1... | collective-permute-start | bytes 393224 | tf_op jit(solution)/shard_map/ppermute | solution.py:250
  207.8 24.4 %collective-permute-start.11 = (bf16[2,1,256,128]{3,2,1,0:T(8,128)(2,1)S(1)}, bf16[2,1,256,128]{3,2,1,0:T(8,128)(2,1)S(1)}, u32[]{:S(2)}, u32[]{:S(2)}) collective-permute-start(bf16[2,1,256,128]{3,2,1,0:T(8,128)(2,1)S(1)} %get-tuple-element.65), channel_id=1, source_target_pairs={{0,80},{16,96},{32,112},{48,64},{64,16},{80,32},{96,48},{112,0},{1... | collective-permute-start | bytes 393224 | tf_op jit(solution)/shard_map/ppermute | solution.py:250
  207.9 8.1 %copy-start.3 = (bf16[16,1,2,96,256]{4,3,2,1,0:T(8,128)(2,1)S(1)}, bf16[16,1,2,96,256]{4,3,2,1,0:T(8,128)(2,1)}, u32[]{:S(2)}) copy-start(bf16[16,1,2,96,256]{4,3,2,1,0:T(8,128)(2,1)} %all_to_all.25.got_ref) | copy-start | bytes 4718596
  215.7 28.0 %collective-permute-start.28 = (bf16[2,2,256,128]{3,2,1,0:T(8,128)(2,1)S(1)}, bf16[2,2,256,128]{3,2,1,0:T(8,128)(2,1)S(1)}, u32[]{:S(2)}, u32[]{:S(2)}) collective-permute-start(bf16[2,2,256,128]{3,2,1,0:T(8,128)(2,1)S(1)} %get-tuple-element.88), channel_id=1, source_target_pairs={{0,16},{16,32},{32,48},{48,0},{64,80},{80,96},{96,112},{112,64},{1... | collective-permute-start | bytes 786440 | tf_op jit(solution)/shard_map/ppermute | solution.py:250
  215.9 34.7 %copy-start.1 = (bf16[16,2,2,96,256]{4,3,2,1,0:T(8,128)(2,1)S(1)}, bf16[16,2,2,96,256]{4,3,2,1,0:T(8,128)(2,1)}, u32[]{:S(2)}) copy-start(bf16[16,2,2,96,256]{4,3,2,1,0:T(8,128)(2,1)} %all_to_all.27.got_ref) | copy-start | bytes 9437188
  224.7 10.8 %collective-permute-start.12 = (bf16[2,1,256,128]{3,2,1,0:T(8,128)(2,1)S(1)}, bf16[2,1,256,128]{3,2,1,0:T(8,128)(2,1)S(1)}, u32[]{:S(2)}, u32[]{:S(2)}) collective-permute-start(bf16[2,1,256,128]{3,2,1,0:T(8,128)(2,1)S(1)} %get-tuple-element.66), channel_id=1, source_target_pairs={{0,96},{16,112},{32,64},{48,80},{64,32},{80,48},{96,0},{112,16},{1... | collective-permute-start | bytes 393224 | tf_op jit(solution)/shard_map/ppermute | solution.py:250
  230.1 7.0 %collective-permute-start.13 = (bf16[2,1,256,128]{3,2,1,0:T(8,128)(2,1)S(1)}, bf16[2,1,256,128]{3,2,1,0:T(8,128)(2,1)S(1)}, u32[]{:S(2)}, u32[]{:S(2)}) collective-permute-start(bf16[2,1,256,128]{3,2,1,0:T(8,128)(2,1)S(1)} %get-tuple-element.67), channel_id=1, source_target_pairs={{0,112},{16,64},{32,80},{48,96},{64,48},{80,0},{96,16},{112,32},{1... | collective-permute-start | bytes 393224 | tf_op jit(solution)/shard_map/ppermute | solution.py:250
  232.2 7.8 %collective-permute-start = (bf16[2,1,256,128]{3,2,1,0:T(8,128)(2,1)S(1)}, bf16[2,1,256,128]{3,2,1,0:T(8,128)(2,1)S(1)}, u32[]{:S(2)}, u32[]{:S(2)}) collective-permute-start(bf16[2,1,256,128]{3,2,1,0:T(8,128)(2,1)S(1)} %get-tuple-element.52), channel_id=1, source_target_pairs={{0,16},{16,32},{32,48},{48,0},{64,80},{80,96},{96,112},{112,64},{1... | collective-permute-start | bytes 393224 | tf_op jit(solution)/shard_map/ppermute | solution.py:250
  232.9 9.9 %collective-permute-start.1 = (bf16[2,1,256,128]{3,2,1,0:T(8,128)(2,1)S(1)}, bf16[2,1,256,128]{3,2,1,0:T(8,128)(2,1)S(1)}, u32[]{:S(2)}, u32[]{:S(2)}) collective-permute-start(bf16[2,1,256,128]{3,2,1,0:T(8,128)(2,1)S(1)} %get-tuple-element.53), channel_id=1, source_target_pairs={{0,32},{16,48},{32,0},{48,16},{64,96},{80,112},{96,64},{112,80},{1... | collective-permute-start | bytes 393224 | tf_op jit(solution)/shard_map/ppermute | solution.py:250
  236.1 23.8 %collective-permute-start.29 = (bf16[2,2,256,128]{3,2,1,0:T(8,128)(2,1)S(1)}, bf16[2,2,256,128]{3,2,1,0:T(8,128)(2,1)S(1)}, u32[]{:S(2)}, u32[]{:S(2)}) collective-permute-start(bf16[2,2,256,128]{3,2,1,0:T(8,128)(2,1)S(1)} %get-tuple-element.89), channel_id=1, source_target_pairs={{0,32},{16,48},{32,0},{48,16},{64,96},{80,112},{96,64},{112,80},{1... | collective-permute-start | bytes 786440 | tf_op jit(solution)/shard_map/ppermute | solution.py:250
  237.7 22.8 %collective-permute-start.30 = (bf16[2,2,256,128]{3,2,1,0:T(8,128)(2,1)S(1)}, bf16[2,2,256,128]{3,2,1,0:T(8,128)(2,1)S(1)}, u32[]{:S(2)}, u32[]{:S(2)}) collective-permute-start(bf16[2,2,256,128]{3,2,1,0:T(8,128)(2,1)S(1)} %get-tuple-element.90), channel_id=1, source_target_pairs={{0,48},{16,0},{32,16},{48,32},{64,112},{80,64},{96,80},{112,96},{1... | collective-permute-start | bytes 786440 | tf_op jit(solution)/shard_map/ppermute | solution.py:250
  240.7 24.1 %collective-permute-start.31 = (bf16[2,2,256,128]{3,2,1,0:T(8,128)(2,1)S(1)}, bf16[2,2,256,128]{3,2,1,0:T(8,128)(2,1)S(1)}, u32[]{:S(2)}, u32[]{:S(2)}) collective-permute-start(bf16[2,2,256,128]{3,2,1,0:T(8,128)(2,1)S(1)} %get-tuple-element.91), channel_id=1, source_target_pairs={{0,64},{16,80},{32,96},{48,112},{64,0},{80,16},{96,32},{112,48},{1... | collective-permute-start | bytes 786440 | tf_op jit(solution)/shard_map/ppermute | solution.py:250
  243.5 22.0 %collective-permute-start.32 = (bf16[2,2,256,128]{3,2,1,0:T(8,128)(2,1)S(1)}, bf16[2,2,256,128]{3,2,1,0:T(8,128)(2,1)S(1)}, u32[]{:S(2)}, u32[]{:S(2)}) collective-permute-start(bf16[2,2,256,128]{3,2,1,0:T(8,128)(2,1)S(1)} %get-tuple-element.92), channel_id=1, source_target_pairs={{0,80},{16,96},{32,112},{48,64},{64,16},{80,32},{96,48},{112,0},{1... | collective-permute-start | bytes 786440 | tf_op jit(solution)/shard_map/ppermute | solution.py:250
  243.7 14.1 %copy-start.7 = (bf16[2,2,256,128]{3,2,1,0:T(8,128)(2,1)}, bf16[2,2,256,128]{3,2,1,0:T(8,128)(2,1)S(1)}, u32[]{:S(2)}) copy-start(bf16[2,2,256,128]{3,2,1,0:T(8,128)(2,1)S(1)} %collective-permute-done.28.refs_1_) | copy-start | bytes 786436
  243.7 24.6 %collective-permute-start.33 = (bf16[2,2,256,128]{3,2,1,0:T(8,128)(2,1)S(1)}, bf16[2,2,256,128]{3,2,1,0:T(8,128)(2,1)S(1)}, u32[]{:S(2)}, u32[]{:S(2)}) collective-permute-start(bf16[2,2,256,128]{3,2,1,0:T(8,128)(2,1)S(1)} %get-tuple-element.93), channel_id=1, source_target_pairs={{0,96},{16,112},{32,64},{48,80},{64,32},{80,48},{96,0},{112,16},{1... | collective-permute-start | bytes 786440 | tf_op jit(solution)/shard_map/ppermute | solution.py:250
  260.6 15.5 %collective-permute-start.34 = (bf16[2,2,256,128]{3,2,1,0:T(8,128)(2,1)}, bf16[2,2,256,128]{3,2,1,0:T(8,128)(2,1)}, u32[]{:S(2)}, u32[]{:S(2)}) collective-permute-start(bf16[2,2,256,128]{3,2,1,0:T(8,128)(2,1)} %get-tuple-element.94), channel_id=1, source_target_pairs={{0,112},{16,64},{32,80},{48,96},{64,48},{80,0},{96,16},{112,32},{1... | collective-permute-start | bytes 786440 | tf_op jit(solution)/shard_map/ppermute | solution.py:250
  261.3 16.2 %collective-permute-start.21 = (bf16[2,2,256,128]{3,2,1,0:T(8,128)(2,1)}, bf16[2,2,256,128]{3,2,1,0:T(8,128)(2,1)}, u32[]{:S(2)}, u32[]{:S(2)}) collective-permute-start(bf16[2,2,256,128]{3,2,1,0:T(8,128)(2,1)} %get-tuple-element.79), channel_id=1, source_target_pairs={{0,16},{16,32},{32,48},{48,0},{64,80},{80,96},{96,112},{112,64},{1... | collective-permute-start | bytes 786440 | tf_op jit(solution)/shard_map/ppermute | solution.py:250
  265.5 16.2 %collective-permute-start.22 = (bf16[2,2,256,128]{3,2,1,0:T(8,128)(2,1)}, bf16[2,2,256,128]{3,2,1,0:T(8,128)(2,1)}, u32[]{:S(2)}, u32[]{:S(2)}) collective-permute-start(bf16[2,2,256,128]{3,2,1,0:T(8,128)(2,1)} %get-tuple-element.80), channel_id=1, source_target_pairs={{0,32},{16,48},{32,0},{48,16},{64,96},{80,112},{96,64},{112,80},{1... | collective-permute-start | bytes 786440 | tf_op jit(solution)/shard_map/ppermute | solution.py:250
  266.2 16.4 %collective-permute-start.23 = (bf16[2,2,256,128]{3,2,1,0:T(8,128)(2,1)}, bf16[2,2,256,128]{3,2,1,0:T(8,128)(2,1)}, u32[]{:S(2)}, u32[]{:S(2)}) collective-permute-start(bf16[2,2,256,128]{3,2,1,0:T(8,128)(2,1)} %get-tuple-element.81), channel_id=1, source_target_pairs={{0,48},{16,0},{32,16},{48,32},{64,112},{80,64},{96,80},{112,96},{1... | collective-permute-start | bytes 786440 | tf_op jit(solution)/shard_map/ppermute | solution.py:250
  269.0 31.9 %collective-permute-start.24 = (bf16[2,2,256,128]{3,2,1,0:T(8,128)(2,1)}, bf16[2,2,256,128]{3,2,1,0:T(8,128)(2,1)}, u32[]{:S(2)}, u32[]{:S(2)}) collective-permute-start(bf16[2,2,256,128]{3,2,1,0:T(8,128)(2,1)} %get-tuple-element.82), channel_id=1, source_target_pairs={{0,64},{16,80},{32,96},{48,112},{64,0},{80,16},{96,32},{112,48},{1... | collective-permute-start | bytes 786440 | tf_op jit(solution)/shard_map/ppermute | solution.py:250
  269.0 7.0 %copy-start.45 = (bf16[2,2,256,128]{3,2,1,0:T(8,128)(2,1)S(1)}, bf16[2,2,256,128]{3,2,1,0:T(8,128)(2,1)}, u32[]{:S(2)}) copy-start(bf16[2,2,256,128]{3,2,1,0:T(8,128)(2,1)} %copy-done.44) | copy-start | bytes 786436
  269.0 8.5 %copy-start.43 = (bf16[2,2,256,128]{3,2,1,0:T(8,128)(2,1)S(1)}, bf16[2,2,256,128]{3,2,1,0:T(8,128)(2,1)}, u32[]{:S(2)}) copy-start(bf16[2,2,256,128]{3,2,1,0:T(8,128)(2,1)} %copy-done.42) | copy-start | bytes 786436
  269.0 12.7 %copy-start.41 = (bf16[2,2,256,128]{3,2,1,0:T(8,128)(2,1)S(1)}, bf16[2,2,256,128]{3,2,1,0:T(8,128)(2,1)}, u32[]{:S(2)}) copy-start(bf16[2,2,256,128]{3,2,1,0:T(8,128)(2,1)} %copy-done.40) | copy-start | bytes 786436
  269.0 45.2 %copy-start = (bf16[4,4,256,256]{3,2,1,0:T(8,128)(2,1)S(1)}, bf16[4,4,256,256]{3,2,1,0:T(8,128)(2,1)}, u32[]{:S(2)}) copy-start(bf16[4,4,256,256]{3,2,1,0:T(8,128)(2,1)} %refs_10_.9) | copy-start | bytes 6291460
  269.0 45.2 %copy-start.6 = (bf16[2,2,256,128]{3,2,1,0:T(8,128)(2,1)S(1)}, bf16[2,2,256,128]{3,2,1,0:T(8,128)(2,1)}, u32[]{:S(2)}) copy-start(bf16[2,2,256,128]{3,2,1,0:T(8,128)(2,1)} %copy-done.5) | copy-start | bytes 786436
  269.1 45.2 %copy-start.8 = (bf16[2,2,256,128]{3,2,1,0:T(8,128)(2,1)S(1)}, bf16[2,2,256,128]{3,2,1,0:T(8,128)(2,1)}, u32[]{:S(2)}) copy-start(bf16[2,2,256,128]{3,2,1,0:T(8,128)(2,1)} %copy-done.7) | copy-start | bytes 786436
  269.1 45.2 %copy-start.10 = (bf16[2,2,256,128]{3,2,1,0:T(8,128)(2,1)S(1)}, bf16[2,2,256,128]{3,2,1,0:T(8,128)(2,1)}, u32[]{:S(2)}) copy-start(bf16[2,2,256,128]{3,2,1,0:T(8,128)(2,1)} %copy-done.9) | copy-start | bytes 786436
  269.1 45.1 %copy-start.12 = (bf16[2,2,256,128]{3,2,1,0:T(8,128)(2,1)S(1)}, bf16[2,2,256,128]{3,2,1,0:T(8,128)(2,1)}, u32[]{:S(2)}) copy-start(bf16[2,2,256,128]{3,2,1,0:T(8,128)(2,1)} %copy-done.11) | copy-start | bytes 786436
  269.1 45.1 %copy-start.14 = (bf16[2,2,256,128]{3,2,1,0:T(8,128)(2,1)S(1)}, bf16[2,2,256,128]{3,2,1,0:T(8,128)(2,1)}, u32[]{:S(2)}) copy-start(bf16[2,2,256,128]{3,2,1,0:T(8,128)(2,1)} %copy-done.13) | copy-start | bytes 786436
  269.1 45.1 %copy-start.16 = (bf16[2,2,256,128]{3,2,1,0:T(8,128)(2,1)S(1)}, bf16[2,2,256,128]{3,2,1,0:T(8,128)(2,1)}, u32[]{:S(2)}) copy-start(bf16[2,2,256,128]{3,2,1,0:T(8,128)(2,1)} %copy-done.15) | copy-start | bytes 786436
  269.1 45.1 %copy-start.18 = (bf16[2,2,256,128]{3,2,1,0:T(8,128)(2,1)S(1)}, bf16[2,2,256,128]{3,2,1,0:T(8,128)(2,1)}, u32[]{:S(2)}) copy-start(bf16[2,2,256,128]{3,2,1,0:T(8,128)(2,1)} %copy-done.17) | copy-start | bytes 786436
  269.1 45.1 %copy-start.39 = (s32[8,128]{1,0:T(8,128)S(1)}, s32[8,128]{1,0:T(8,128)}, u32[]{:S(2)}) copy-start(s32[8,128]{1,0:T(8,128)} %refs_9_.9) | copy-start | bytes 12292
  276.1 24.8 %collective-permute-start.25 = (bf16[2,2,256,128]{3,2,1,0:T(8,128)(2,1)S(1)}, bf16[2,2,256,128]{3,2,1,0:T(8,128)(2,1)S(1)}, u32[]{:S(2)}, u32[]{:S(2)}) collective-permute-start(bf16[2,2,256,128]{3,2,1,0:T(8,128)(2,1)S(1)} %copy-done.45), channel_id=1, source_target_pairs={{0,80},{16,96},{32,112},{48,64},{64,16},{80,32},{96,48},{112,0},{1... | collective-permute-start | bytes 786440 | tf_op jit(solution)/shard_map/ppermute | solution.py:250
  277.5 27.1 %collective-permute-start.26 = (bf16[2,2,256,128]{3,2,1,0:T(8,128)(2,1)S(1)}, bf16[2,2,256,128]{3,2,1,0:T(8,128)(2,1)S(1)}, u32[]{:S(2)}, u32[]{:S(2)}) collective-permute-start(bf16[2,2,256,128]{3,2,1,0:T(8,128)(2,1)S(1)} %copy-done.43), channel_id=1, source_target_pairs={{0,96},{16,112},{32,64},{48,80},{64,32},{80,48},{96,0},{112,16},{1... | collective-permute-start | bytes 786440 | tf_op jit(solution)/shard_map/ppermute | solution.py:250
  281.7 22.9 %collective-permute-start.27 = (bf16[2,2,256,128]{3,2,1,0:T(8,128)(2,1)S(1)}, bf16[2,2,256,128]{3,2,1,0:T(8,128)(2,1)S(1)}, u32[]{:S(2)}, u32[]{:S(2)}) collective-permute-start(bf16[2,2,256,128]{3,2,1,0:T(8,128)(2,1)S(1)} %copy-done.41), channel_id=1, source_target_pairs={{0,112},{16,64},{32,80},{48,96},{64,48},{80,0},{96,16},{112,32},{1... | collective-permute-start | bytes 786440 | tf_op jit(solution)/shard_map/ppermute | solution.py:250
  282.6 25.0 %collective-permute-start.14 = (bf16[2,2,256,128]{3,2,1,0:T(8,128)(2,1)S(1)}, bf16[2,2,256,128]{3,2,1,0:T(8,128)(2,1)S(1)}, u32[]{:S(2)}, u32[]{:S(2)}) collective-permute-start(bf16[2,2,256,128]{3,2,1,0:T(8,128)(2,1)S(1)} %get-tuple-element.70), channel_id=1, source_target_pairs={{0,16},{16,32},{32,48},{48,0},{64,80},{80,96},{96,112},{112,64},{1... | collective-permute-start | bytes 786440 | tf_op jit(solution)/shard_map/ppermute | solution.py:250
  300.9 8.2 %collective-permute-start.15 = (bf16[2,2,256,128]{3,2,1,0:T(8,128)(2,1)S(1)}, bf16[2,2,256,128]{3,2,1,0:T(8,128)(2,1)S(1)}, u32[]{:S(2)}, u32[]{:S(2)}) collective-permute-start(bf16[2,2,256,128]{3,2,1,0:T(8,128)(2,1)S(1)} %get-tuple-element.71), channel_id=1, source_target_pairs={{0,32},{16,48},{32,0},{48,16},{64,96},{80,112},{96,64},{112,80},{1... | collective-permute-start | bytes 786440 | tf_op jit(solution)/shard_map/ppermute | solution.py:250
  300.9 22.6 %collective-permute-start.16 = (bf16[2,2,256,128]{3,2,1,0:T(8,128)(2,1)S(1)}, bf16[2,2,256,128]{3,2,1,0:T(8,128)(2,1)S(1)}, u32[]{:S(2)}, u32[]{:S(2)}) collective-permute-start(bf16[2,2,256,128]{3,2,1,0:T(8,128)(2,1)S(1)} %get-tuple-element.72), channel_id=1, source_target_pairs={{0,48},{16,0},{32,16},{48,32},{64,112},{80,64},{96,80},{112,96},{1... | collective-permute-start | bytes 786440 | tf_op jit(solution)/shard_map/ppermute | solution.py:250
  304.6 19.0 %collective-permute-start.17 = (bf16[2,2,256,128]{3,2,1,0:T(8,128)(2,1)S(1)}, bf16[2,2,256,128]{3,2,1,0:T(8,128)(2,1)S(1)}, u32[]{:S(2)}, u32[]{:S(2)}) collective-permute-start(bf16[2,2,256,128]{3,2,1,0:T(8,128)(2,1)S(1)} %get-tuple-element.73), channel_id=1, source_target_pairs={{0,64},{16,80},{32,96},{48,112},{64,0},{80,16},{96,32},{112,48},{1... | collective-permute-start | bytes 786440 | tf_op jit(solution)/shard_map/ppermute | solution.py:250
  304.6 20.4 %collective-permute-start.18 = (bf16[2,2,256,128]{3,2,1,0:T(8,128)(2,1)S(1)}, bf16[2,2,256,128]{3,2,1,0:T(8,128)(2,1)S(1)}, u32[]{:S(2)}, u32[]{:S(2)}) collective-permute-start(bf16[2,2,256,128]{3,2,1,0:T(8,128)(2,1)S(1)} %get-tuple-element.74), channel_id=1, source_target_pairs={{0,80},{16,96},{32,112},{48,64},{64,16},{80,32},{96,48},{112,0},{1... | collective-permute-start | bytes 786440 | tf_op jit(solution)/shard_map/ppermute | solution.py:250
  307.6 19.5 %collective-permute-start.19 = (bf16[2,2,256,128]{3,2,1,0:T(8,128)(2,1)S(1)}, bf16[2,2,256,128]{3,2,1,0:T(8,128)(2,1)S(1)}, u32[]{:S(2)}, u32[]{:S(2)}) collective-permute-start(bf16[2,2,256,128]{3,2,1,0:T(8,128)(2,1)S(1)} %get-tuple-element.75), channel_id=1, source_target_pairs={{0,96},{16,112},{32,64},{48,80},{64,32},{80,48},{96,0},{112,16},{1... | collective-permute-start | bytes 786440 | tf_op jit(solution)/shard_map/ppermute | solution.py:250
  309.0 20.2 %collective-permute-start.20 = (bf16[2,2,256,128]{3,2,1,0:T(8,128)(2,1)S(1)}, bf16[2,2,256,128]{3,2,1,0:T(8,128)(2,1)S(1)}, u32[]{:S(2)}, u32[]{:S(2)}) collective-permute-start(bf16[2,2,256,128]{3,2,1,0:T(8,128)(2,1)S(1)} %get-tuple-element.76), channel_id=1, source_target_pairs={{0,112},{16,64},{32,80},{48,96},{64,48},{80,0},{96,16},{112,32},{1... | collective-permute-start | bytes 786440 | tf_op jit(solution)/shard_map/ppermute | solution.py:250
  318.8 4.7 %copy-start.55 = (bf16[2,1,256,128]{3,2,1,0:T(8,128)(2,1)S(1)}, bf16[2,1,256,128]{3,2,1,0:T(8,128)(2,1)}, u32[]{:S(2)}) copy-start(bf16[2,1,256,128]{3,2,1,0:T(8,128)(2,1)} %copy-done.54) | copy-start | bytes 393220
  318.8 4.8 %copy-start.53 = (bf16[2,1,256,128]{3,2,1,0:T(8,128)(2,1)S(1)}, bf16[2,1,256,128]{3,2,1,0:T(8,128)(2,1)}, u32[]{:S(2)}) copy-start(bf16[2,1,256,128]{3,2,1,0:T(8,128)(2,1)} %copy-done.52) | copy-start | bytes 393220
  318.8 6.2 %copy-start.51 = (bf16[2,1,256,128]{3,2,1,0:T(8,128)(2,1)S(1)}, bf16[2,1,256,128]{3,2,1,0:T(8,128)(2,1)}, u32[]{:S(2)}) copy-start(bf16[2,1,256,128]{3,2,1,0:T(8,128)(2,1)} %copy-done.50) | copy-start | bytes 393220
  318.8 8.3 %copy-start.49 = (bf16[2,1,256,128]{3,2,1,0:T(8,128)(2,1)S(1)}, bf16[2,1,256,128]{3,2,1,0:T(8,128)(2,1)}, u32[]{:S(2)}) copy-start(bf16[2,1,256,128]{3,2,1,0:T(8,128)(2,1)} %copy-done.48) | copy-start | bytes 393220
  318.8 10.4 %copy-start.47 = (bf16[2,1,256,128]{3,2,1,0:T(8,128)(2,1)S(1)}, bf16[2,1,256,128]{3,2,1,0:T(8,128)(2,1)}, u32[]{:S(2)}) copy-start(bf16[2,1,256,128]{3,2,1,0:T(8,128)(2,1)} %copy-done.46) | copy-start | bytes 393220
  323.5 14.6 %collective-permute-start.2 = (bf16[2,1,256,128]{3,2,1,0:T(8,128)(2,1)S(1)}, bf16[2,1,256,128]{3,2,1,0:T(8,128)(2,1)S(1)}, u32[]{:S(2)}, u32[]{:S(2)}) collective-permute-start(bf16[2,1,256,128]{3,2,1,0:T(8,128)(2,1)S(1)} %copy-done.55), channel_id=1, source_target_pairs={{0,48},{16,0},{32,16},{48,32},{64,112},{80,64},{96,80},{112,96},{1... | collective-permute-start | bytes 393224 | tf_op jit(solution)/shard_map/ppermute | solution.py:250
  323.6 14.5 %collective-permute-start.3 = (bf16[2,1,256,128]{3,2,1,0:T(8,128)(2,1)S(1)}, bf16[2,1,256,128]{3,2,1,0:T(8,128)(2,1)S(1)}, u32[]{:S(2)}, u32[]{:S(2)}) collective-permute-start(bf16[2,1,256,128]{3,2,1,0:T(8,128)(2,1)S(1)} %copy-done.53), channel_id=1, source_target_pairs={{0,64},{16,80},{32,96},{48,112},{64,0},{80,16},{96,32},{112,48},{1... | collective-permute-start | bytes 393224 | tf_op jit(solution)/shard_map/ppermute | solution.py:250
  325.0 13.1 %collective-permute-start.4 = (bf16[2,1,256,128]{3,2,1,0:T(8,128)(2,1)S(1)}, bf16[2,1,256,128]{3,2,1,0:T(8,128)(2,1)S(1)}, u32[]{:S(2)}, u32[]{:S(2)}) collective-permute-start(bf16[2,1,256,128]{3,2,1,0:T(8,128)(2,1)S(1)} %copy-done.51), channel_id=1, source_target_pairs={{0,80},{16,96},{32,112},{48,64},{64,16},{80,32},{96,48},{112,0},{1... | collective-permute-start | bytes 393224 | tf_op jit(solution)/shard_map/ppermute | solution.py:250
  327.0 11.0 %collective-permute-start.5 = (bf16[2,1,256,128]{3,2,1,0:T(8,128)(2,1)S(1)}, bf16[2,1,256,128]{3,2,1,0:T(8,128)(2,1)S(1)}, u32[]{:S(2)}, u32[]{:S(2)}) collective-permute-start(bf16[2,1,256,128]{3,2,1,0:T(8,128)(2,1)S(1)} %copy-done.49), channel_id=1, source_target_pairs={{0,96},{16,112},{32,64},{48,80},{64,32},{80,48},{96,0},{112,16},{1... | collective-permute-start | bytes 393224 | tf_op jit(solution)/shard_map/ppermute | solution.py:250
  329.2 8.8 %collective-permute-start.6 = (bf16[2,1,256,128]{3,2,1,0:T(8,128)(2,1)S(1)}, bf16[2,1,256,128]{3,2,1,0:T(8,128)(2,1)S(1)}, u32[]{:S(2)}, u32[]{:S(2)}) collective-permute-start(bf16[2,1,256,128]{3,2,1,0:T(8,128)(2,1)S(1)} %copy-done.47), channel_id=1, source_target_pairs={{0,112},{16,64},{32,80},{48,96},{64,48},{80,0},{96,16},{112,32},{1... | collective-permute-start | bytes 393224 | tf_op jit(solution)/shard_map/ppermute | solution.py:250
  330.1 4.5 %copy-start.26 = (bf16[2,1,256,128]{3,2,1,0:T(8,128)(2,1)S(1)}, bf16[2,1,256,128]{3,2,1,0:T(8,128)(2,1)}, u32[]{:S(2)}) copy-start(bf16[2,1,256,128]{3,2,1,0:T(8,128)(2,1)} %copy-done.25) | copy-start | bytes 393220
  330.1 4.5 %copy-start.28 = (bf16[2,1,256,128]{3,2,1,0:T(8,128)(2,1)S(1)}, bf16[2,1,256,128]{3,2,1,0:T(8,128)(2,1)}, u32[]{:S(2)}) copy-start(bf16[2,1,256,128]{3,2,1,0:T(8,128)(2,1)} %copy-done.27) | copy-start | bytes 393220
  330.1 4.5 %copy-start.36 = (bf16[2,1,256,128]{3,2,1,0:T(8,128)(2,1)S(1)}, bf16[2,1,256,128]{3,2,1,0:T(8,128)(2,1)}, u32[]{:S(2)}) copy-start(bf16[2,1,256,128]{3,2,1,0:T(8,128)(2,1)} %copy-done.35) | copy-start | bytes 393220
  330.1 4.5 %copy-start.38 = (bf16[2,1,256,128]{3,2,1,0:T(8,128)(2,1)S(1)}, bf16[2,1,256,128]{3,2,1,0:T(8,128)(2,1)}, u32[]{:S(2)}) copy-start(bf16[2,1,256,128]{3,2,1,0:T(8,128)(2,1)} %copy-done.37) | copy-start | bytes 393220
  (31 other events, 45.0 us)

commit v2 on v1

--- a/solution.py
+++ b/solution.py
@@ -8,15 +8,15 @@
 from jax.sharding import PartitionSpec as P
 
 ZS, Y = 2, 4
-CHUNKS = (2, 2, 2, 1, 1)
+CHUNKS = (3, 2, 2, 1)
+TIES = ((1, (0, 4, 5, 6, 7)), (2, (1, 2, 3)))
 STEP = 16
 BF16, F32 = jnp.bfloat16, jnp.float32
 
 
-def prep_kernel(starts, key_ref, x_ref, *refs):
-    outs, (pick, wide, tall) = refs[: len(starts)], refs[len(starts) :]
-    rows, step, orders = x_ref.shape
-    per_dev = sum(n for _, n in starts)
+def prep_kernel(starts, per_dev, key_ref, x_ref, *refs):
+    outs, (pick, swap, by_lat, by_order) = refs[: len(starts)], refs[len(starts) :]
+    rows, _, orders = x_ref.shape
 
     @pl.when(pl.program_id(0) == 0)
     def _():
@@ -24,47 +24,51 @@
         for first, n in starts:
             count = 16 * n * 2
             i = lax.broadcasted_iota(jnp.int32, (count, orders), 0)
-            dest, rest = i // (2 * n), i % (2 * n)
+            rest, dest = i // 16, i % 16
             target = dest * (2 * per_dev) + 2 * first + rest
             hit = key_ref[...] == target
             pick[at : at + count, :] = jnp.where(hit, 1.0, 0.0).astype(BF16)
             at += count
-
-    for lane in range(2):
-        cols = slice(lane * 128, (lane + 1) * 128)
-        wide[lane] = x_ref[:, :, cols].astype(F32).reshape(rows * step, 128)
-
-    def body(n, carry):
-        one = [wide[lane, pl.ds(n, rows, stride=step), :].astype(BF16) for lane in range(2)]
+        i = lax.broadcasted_iota(jnp.int32, (256, 256), 0)
+        j = lax.broadcasted_iota(jnp.int32, (256, 256), 1)
+        hit = (i // 16 == j % 16) & (i % 16 == j // 16)
+        swap[...] = jnp.where(hit, 1.0, 0.0).astype(BF16)
+
+    def to_lat(c, carry):
+        at = pl.multiple_of(c * 16, 16)
+        block = x_ref[pl.ds(at, 16), :, :].reshape(256, orders)
+        moved = jnp.dot(swap[...], block, preferred_element_type=F32)
+        by_lat[:, pl.ds(at, 16), :] = moved.astype(BF16).reshape(STEP, 16, orders)
+        return carry
+
+    lax.fori_loop(0, rows // 16, to_lat, 0, unroll=True)
+
+    def to_order(n, carry):
         moved = lax.dot_general(
-            pick[...],
-            jnp.concatenate(one, axis=1),
-            (((1,), (1,)), ((), ())),
-            preferred_element_type=F32,
+            pick[...], by_lat[n], (((1,), (1,)), ((), ())), preferred_element_type=F32
         )
-        for lane in range(2):
-            cols = slice(lane * 128, (lane + 1) * 128)
-            tall[lane, pl.ds(n, orders, stride=step), :] = moved[:, cols]
+        by_order[:, n] = moved.astype(BF16).reshape(by_order.shape[0], 16, rows)
         return carry
 
-    lax.fori_loop(0, step, body, 0)
-    at = 0
+    lax.fori_loop(0, STEP, to_order, 0, unroll=True)
+
+    base = 0
     for out, (_, n) in zip(outs, starts):
-        count = 16 * n * 2
-        for lane in range(2):
-            cols = slice(lane * 128, (lane + 1) * 128)
-            part = tall[lane, at * step : (at + count) * step, :].astype(BF16)
-            out[:, :, :, :, cols] = part.reshape(out.shape[:4] + (128,))
-        at += count
-
-
-def prep(physical, pair_slot, starts):
+        for g in range(2 * n):
+            block = by_order[base + g].reshape(256, rows)
+            moved = jnp.dot(swap[...], block, preferred_element_type=F32).astype(BF16)
+            out[:, g // 2, g % 2] = moved.reshape(16, STEP, rows)
+        base += 2 * n
+
+
+def prep(physical, pair_slot, starts, per_dev):
     orders, chans, radii, lats = physical.shape
+    sent = sum(32 * n for _, n in starts)
     rows = chans * radii
     x = jnp.transpose(physical, (1, 2, 3, 0)).reshape(rows, lats, orders)
     key = (2 * pair_slot[:, None] + jnp.arange(2, dtype=jnp.int32)[None, :]).reshape(1, orders)
     return pl.pallas_call(
-        functools.partial(prep_kernel, starts),
+        functools.partial(prep_kernel, starts, per_dev),
         grid=(lats // STEP,),
         in_specs=[
             pl.BlockSpec((1, orders), lambda b: (0, 0)),
@@ -75,14 +79,15 @@
         ],
         out_shape=[jax.ShapeDtypeStruct((16, n, 2, lats, rows), BF16) for _, n in starts],
         scratch_shapes=[
-            pltpu.VMEM((orders, orders), BF16),
-            pltpu.VMEM((2, rows * STEP, 128), F32),
-            pltpu.VMEM((2, orders * STEP, 128), F32),
+            pltpu.VMEM((sent, orders), BF16),
+            pltpu.VMEM((256, 256), BF16),
+            pltpu.VMEM((STEP, rows, orders), BF16),
+            pltpu.VMEM((sent // 16, STEP, 16, rows), BF16),
         ],
         compiler_params=pltpu.CompilerParams(vmem_limit_bytes=48 << 20),
         cost_estimate=pl.CostEstimate(
-            flops=2 * rows * lats * orders * orders,
-            bytes_accessed=4 * rows * lats * orders,
+            flops=2 * rows * lats * orders * (orders + 2 * sent),
+            bytes_accessed=2 * rows * lats * (orders + sent),
             transcendentals=0,
         ),
         name="prep",
@@ -141,6 +146,72 @@
     )(meta, got, legendre)
 
 
+def transform_whole_kernel(meta_ref, got_ref, table_ref, out_ref):
+    slot, part = pl.program_id(0), pl.program_id(1)
+    srcs, _, _, lats, rows = got_ref.shape
+    depth, width = srcs * lats, table_ref.shape[2]
+    dims = (((0,), (0,)), ((), ()))
+
+    def product(h):
+        return lax.dot_general(
+            got_ref[:, 0, h].reshape(depth, rows),
+            table_ref[0],
+            dims,
+            preferred_element_type=F32,
+        )
+
+    def store(value):
+        for d in range(width // 128):
+            out_ref[d, 0] = value[:, d * 128 : (d + 1) * 128].astype(BF16)
+
+    @pl.when(part == 0)
+    def _():
+        store(product(0))
+
+    @pl.when(part == 1)
+    def _():
+        column = width + lax.broadcasted_iota(jnp.int32, (rows, width), 1)
+        store(jnp.where(column < meta_ref[9 + slot], product(0), product(1)))
+
+
+def transform_whole(got, legendre, meta, first):
+    srcs, count, _, lats, rows = got.shape
+    degrees = legendre.shape[2]
+    depth = srcs * lats
+    return pl.pallas_call(
+        transform_whole_kernel,
+        grid_spec=pltpu.PrefetchScalarGridSpec(
+            num_scalar_prefetch=1,
+            grid=(count, 2),
+            in_specs=[
+                pl.BlockSpec((srcs, 1, 2, lats, rows), lambda s, t, m: (0, s, 0, 0, 0)),
+                pl.BlockSpec((1, depth, degrees // 2), lambda s, t, m: (first + s, 0, t)),
+            ],
+            out_specs=pl.BlockSpec((4, 1, rows, 128), lambda s, t, m: (t, s, 0, 0)),
+        ),
+        out_shape=jax.ShapeDtypeStruct((8, count, rows, 128), BF16),
+        compiler_params=pltpu.CompilerParams(vmem_limit_bytes=48 << 20),
+        cost_estimate=pl.CostEstimate(
+            flops=3 * count * rows * depth * degrees,
+            bytes_accessed=2 * count * (2 * depth * rows + depth * degrees + rows * degrees),
+            transcendentals=0,
+        ),
+        name="transform_whole",
+    )(meta, got, legendre)
+
+
+def invert(row, inv_ref, out_ref, side):
+    row = jnp.concatenate([row, row], axis=1)
+    for q in range(4):
+        acc = None
+        for g in range(4):
+            one = jnp.dot(inv_ref[q, g], side[q], preferred_element_type=F32)
+            acc = one if acc is None else jnp.where(row == g, one, acc)
+        acc = acc.astype(BF16)
+        out_ref[0, 2 * q] = acc[:, :128]
+        out_ref[0, 2 * q + 1] = acc[:, 128:]
+
+
 def settle_kernel(first, meta_ref, *refs):
     parts = refs[:8]
     state_ref, index_ref, inv_ref = refs[8:11]
@@ -158,23 +229,30 @@
                 value = state_ref[0, c, pl.ds(at, radii), :].astype(F32) + 0.5 * total
                 lanes = slice((c % 2) * 128, (c % 2) * 128 + 128)
                 side[c // 2, pl.ds(at, radii), lanes] = value.astype(BF16)
-    row = index_ref[pl.ds(first + pl.program_id(0), 1), :]
-    row = jnp.concatenate([row, row], axis=1)
-    for q in range(4):
-        acc = None
-        for g in range(4):
-            one = jnp.dot(inv_ref[q, g], side[q], preferred_element_type=F32)
-            acc = one if acc is None else jnp.where(row == g, one, acc)
-        acc = acc.astype(BF16)
-        out_ref[0, 2 * q] = acc[:, :128]
-        out_ref[0, 2 * q + 1] = acc[:, 128:]
-
-
-def settle(parts, state, inverses, index, meta, first, so_far):
+    invert(index_ref[pl.ds(first + pl.program_id(0), 1), :], inv_ref, out_ref, side)
+
+
+def settle_whole_kernel(first, meta_ref, *refs):
+    part, state_ref, index_ref, inv_ref = refs[:4]
+    out_ref, side = refs[-2], refs[-1]
+    radii = 32
+    for c in range(8):
+        lanes = slice((c % 2) * 128, (c % 2) * 128 + 128)
+        for d in range(8):
+            total = part[d, 0, c * radii : (c + 1) * radii, :].astype(F32)
+            at = slice(d * radii, (d + 1) * radii)
+            value = state_ref[0, c, at, :].astype(F32) + 0.5 * total
+            side[c // 2, at, lanes] = value.astype(BF16)
+    invert(index_ref[pl.ds(first + pl.program_id(0), 1), :], inv_ref, out_ref, side)
+
+
+def settle(kernel, parts, state, inverses, index, meta, first, so_far):
     count = parts[0].shape[1]
-    block = pl.BlockSpec((2, 1) + parts[0].shape[2:], lambda s, m: (0, s, 0, 0))
+    block = pl.BlockSpec(
+        (parts[0].shape[0], 1) + parts[0].shape[2:], lambda s, m: (0, s, 0, 0)
+    )
     operands = [meta, *parts, state, index, inverses]
-    in_specs = [block] * 8 + [
+    in_specs = [block] * len(parts) + [
         pl.BlockSpec((1,) + state.shape[1:], lambda s, m: (first + s, 0, 0, 0)),
         pl.BlockSpec(index.shape, lambda s, m: (0, 0)),
         pl.BlockSpec(inverses.shape, lambda s, m: (0, 0, 0, 0)),
@@ -185,7 +263,7 @@
         in_specs.append(pl.BlockSpec(memory_space=pl.ANY))
         aliases = {len(operands) - 1: 0}
     return pl.pallas_call(
-        functools.partial(settle_kernel, first),
+        functools.partial(kernel, first),
         grid_spec=pltpu.PrefetchScalarGridSpec(
             num_scalar_prefetch=1,
             grid=(count,),
@@ -224,7 +302,7 @@
     for n in CHUNKS:
         starts.append((first, n))
         first += n
-    sends = prep(physical, pair_slot, tuple(starts))
+    sends = list(prep(physical, pair_slot, tuple(starts[:1]), per_dev))
 
     lat, rad = lax.axis_index("lat"), lax.axis_index("rad")
     zl, y = rad // Y, rad % Y
@@ -237,20 +315,66 @@
     blocks = (zl ^ (hops // Y)) * Y + (y + hops) % Y
     place = jnp.stack([zl, y]).astype(jnp.int32)
 
-    out = None
-    for send, (first, n) in zip(sends, starts):
-        got = lax.all_to_all(
-            send, ("rad", "lat"), 0, 0, tiled=True, axis_index_groups=flip_groups()
+    out, gots, moves = None, [], []
+
+    final = len(starts) - 1
+
+    def put(k):
+        kernel = settle_whole_kernel if k == final else settle_kernel
+        return settle(
+            kernel, moves[k], spectral_state, inverses, block_index, place, starts[k][0], out
         )
-        meta = jnp.concatenate(
-            [(lat // 8)[None], blocks, lengths[first : first + n]]
-        ).astype(jnp.int32)
-        parts = transform(got, legendre, meta, first)
-        moved = [parts[0]] + [
-            lax.ppermute(parts[k], "rad", rad_targets(k // Y, k % Y)) for k in range(1, 8)
-        ]
-        out = settle(moved, spectral_state, inverses, block_index, place, first, out)
-    return out
+
+    for k in range(len(starts) + 1):
+        keep = {}
+        if k > 0:
+            keep["got", k - 1] = gots[k - 1]
+        for back, hops_of in TIES:
+            if k > back:
+                for h in hops_of:
+                    keep["move", k - 1 - back, h] = moves[k - 1 - back][h]
+        if k > 2:
+            keep["out"] = out
+        if k < len(starts):
+            if k == 1:
+                sends.extend(prep(physical, pair_slot, tuple(starts[1:]), per_dev))
+            keep["send", k] = sends[k]
+        held = dict(zip(keep, lax.optimization_barrier(tuple(keep.values()))))
+        out = held.get("out", out)
+        if k > 0:
+            gots[k - 1] = held["got", k - 1]
+        for name, value in held.items():
+            if name[0] == "move":
+                moves[name[1]][name[2]] = value
+        if k < len(starts):
+            send = held["send", k]
+            if k == final:
+                gots.append(lax.all_to_all(send, "lat", 0, 0, tiled=True))
+            else:
+                gots.append(
+                    lax.all_to_all(
+                        send, ("rad", "lat"), 0, 0, tiled=True, axis_index_groups=flip_groups()
+                    )
+                )
+        if k > 0:
+            first, n = starts[k - 1]
+            meta = jnp.concatenate([(lat // 8)[None], blocks, lengths[first : first + n]])
+            meta = meta.astype(jnp.int32)
+            if k - 1 == final:
+                part = transform_whole(gots[k - 1], legendre, meta, first)
+                moves.append([lax.all_to_all(part, "rad", 0, 0, tiled=True)])
+            else:
+                parts = transform(gots[k - 1], legendre, meta, first)
+                moves.append(
+                    [parts[0]]
+                    + [
+                        lax.ppermute(parts[h], "rad", rad_targets(h // Y, h % Y))
+                        for h in range(1, 8)
+                    ]
+                )
+        if k > 1:
+            out = put(k - 2)
+    return put(final)
 
 
 def solution(mesh):

time: 345 us -> 286 us (0.83)
  blocking collectives: 135 us -> 0 us
  waiting for transfers between devices: 15.8 us -> 116 us
  Pallas kernels: 94.1 us -> 72.1 us
  starting transfers between devices: 75.7 us -> 71.2 us
  local copies, waits for them, and re-layouts: 17.8 us -> 21.3 us
    all_to_all x4 -> x0, blocking collectives: 135 us -> none  [on_device(): lax.all_to_all(send, ('rad', 'lat'), 0, 0, tiled=True, axis_index_groups=...]
    ppermute x35 -> x21, waiting for transfers between devices: 15.8 us -> 69.5 us  [on_device(): lax.ppermute(parts[h], 'rad', rad_targets(h // Y, h % Y))]
    all_to_all x1 -> x3, waiting for transfers between devices: 0.01 us -> 47 us  [on_device(): lax.all_to_all(send, ('rad', 'lat'), 0, 0, tiled=True, axis_index_groups=...]
    ppermute x35 -> x21, starting transfers between devices: 68.7 us -> 42.2 us  [on_device(): lax.ppermute(parts[h], 'rad', rad_targets(h // Y, h % Y))]
    pallas_call x6 -> x7, Pallas kernels: 64.5 us -> 48.6 us  [the longest x2 26.1 us: prep(): pl.pallas_call(functools.partial(prep_kernel, starts, per_dev), grid=(lat...]
    all_to_all x0 -> x2, starting transfers between devices: none -> 13.3 us  [the longest x1 7.23 us: on_device(): gots.append(lax.all_to_all(send, 'lat', 0, 0, tiled=True))]
    all_to_all x1 -> x3, starting transfers between devices: 6.97 us -> 15.7 us  [on_device(): lax.all_to_all(send, ('rad', 'lat'), 0, 0, tiled=True, axis_index_groups=...]
    pallas_call x5 -> x3, Pallas kernels: 29.7 us -> 23.5 us  [transform(): pl.pallas_call(transform_kernel, grid_spec=pltpu.PrefetchScalarGridSpec(n...]
  transfers between devices with their start and end apart: 36 -> 26, of which waited for: 1 -> 8; matrix products, arithmetic and copies ran while one was open for 1% -> 1% of each run, Pallas kernels for 14% -> 18%
where the time goes in v2:
time: 286 us; the launch traced here: 283 us
  waiting for transfers between devices  116 us (41%)
  Pallas kernels  72.1 us (25%)
  starting transfers between devices  71.2 us (25%)
  local copies, waits for them, and re-layouts  21.3 us (7%)
    ppermute x21, waiting for transfers between devices, on_device(): lax.ppermute(parts[h], 'rad', rad_targets(h // Y, h % Y))  69.5 us
    all_to_all x3, waiting for transfers between devices, on_device(): lax.all_to_all(send, ('rad', 'lat'), 0, 0, tiled=True, axis_index_groups=...  47 us
    ppermute x21, starting transfers between devices, on_device(): lax.ppermute(parts[h], 'rad', rad_targets(h // Y, h % Y))  42.2 us
    pallas_call x2, Pallas kernels, prep(): pl.pallas_call(functools.partial(prep_kernel, starts, per_dev), grid=(lat...  26.1 us
    pallas_call x3, Pallas kernels, transform(): pl.pallas_call(transform_kernel, grid_spec=pltpu.PrefetchScalarGridSpec(n...  23.5 us
    unnamed x82, local copies, waits for them, and re-layouts  20.5 us
    pallas_call x4, Pallas kernels, settle(): pl.pallas_call(functools.partial(kernel, first), grid_spec=pltpu.Prefetch...  17.7 us
    all_to_all x3, starting transfers between devices, on_device(): lax.all_to_all(send, ('rad', 'lat'), 0, 0, tiled=True, axis_index_groups=...  15.7 us
  transfers between devices with their start and end apart: 26, of which 8 were waited for; matrix products, arithmetic and copies ran while one was open for 1% of the time, Pallas kernels for 18%

profile of v2, /device:TPU:74, one launch (start us, length us, event | category | flops | bytes accessed | tf_op | source)
XLA Modules:
  0.0 283.1 jit_solution(9798368048057399740)
XLA Ops:
  0.0 0.7 broadcast_multiply_fusion
  0.9 12.1 %prep.2 = bf16[16,3,2,96,256]{4,3,2,1,0:T(8,128)(2,1)S(1)} custom-call(s32[1,256]{1,0:T(1,128)S(1)} %add.76.key_ref, bf16[256,96,256]{2,1,0:T(8,128)(2,1)} %bitcast.8), custom_call_target="tpu_custom_call" | custom-call | flops 5637144576 | bytes 17301504 | tf_op jit(solution)/shard_map/prep/pallas_call | solution.py:70
  13.0 2.2 copy-done.3
  15.1 5.7 %all-to-all-start = ((bf16[16,3,2,96,256]{4,3,2,1,0:T(8,128)(2,1)}), bf16[16,3,2,96,256]{4,3,2,1,0:T(8,128)(2,1)}, u32[]{:S(2)}, u32[]{:S(2)}) async-start(bf16[16,3,2,96,256]{4,3,2,1,0:T(8,128)(2,1)} %copy-done.3), calls=%async_computation | async-start | bytes 9437184 | tf_op jit(solution)/shard_map/all_to_all | solution.py:355
  20.9 14.1 %prep.3 = (bf16[16,2,2,96,256]{4,3,2,1,0:T(8,128)(2,1)S(1)}, bf16[16,2,2,96,256]{4,3,2,1,0:T(8,128)(2,1)}, bf16[16,1,2,96,256]{4,3,2,1,0:T(8,128)(2,1)S(1)}) custom-call(s32[1,256]{1,0:T(1,128)S(1)} %add.76.key_ref, bf16[256,96,256]{2,1,0:T(8,128)(2,1)} %bitcast.9), custom_call_target="tpu_custom_call" | custom-call | flops 7247757312 | bytes 20447232 | tf_op jit(solution)/shard_map/prep/pallas_call | solution.py:70
  35.0 1.7 copy-done.4
  36.6 1.1 copy-done.5
  37.8 47.0 %all-to-all-done.got_ref = bf16[16,3,2,96,256]{4,3,2,1,0:T(8,128)(2,1)} async-done(((bf16[16,3,2,96,256]{4,3,2,1,0:T(8,128)(2,1)}), bf16[16,3,2,96,256]{4,3,2,1,0:T(8,128)(2,1)}, u32[]{:S(2)}, u32[]{:S(2)}) %all-to-all-start) | async-done | bytes 4718624 | tf_op jit(solution)/shard_map/all_to_all | solution.py:355
  84.7 4.2 %all-to-all-start.1 = ((bf16[16,2,2,96,256]{4,3,2,1,0:T(8,128)(2,1)}), bf16[16,2,2,96,256]{4,3,2,1,0:T(8,128)(2,1)S(1)}, u32[]{:S(2)}, u32[]{:S(2)}) async-start(bf16[16,2,2,96,256]{4,3,2,1,0:T(8,128)(2,1)} %copy-done.4), calls=%async_computation.1 | async-start | bytes 6291456 | tf_op jit(solution)/shard_map/all_to_all | solution.py:355
  89.2 9.7 %transform.3 = (bf16[2,3,256,128]{3,2,1,0:T(8,128)(2,1)S(1)}, bf16[2,3,256,128]{3,2,1,0:T(8,128)(2,1)S(1)}, bf16[2,3,256,128]{3,2,1,0:T(8,128)(2,1)S(1)}, bf16[2...) custom-call(s32[12]{0:T(128)S(1)} %pad_add_fusion.2.meta_ref, ...), custom_call_target="tpu_custom_call" | custom-call | flops 3623878656 | bytes 22020096 | tf_op jit(solution)/shard_map/transform/pallas_call | solution.py:124
  99.0 0.7 copy-done.31
  99.7 0.7 copy-done.32
  100.4 0.8 copy-done.33
  101.2 4.1 %collective-permute-start = (bf16[2,3,256,128]{3,2,1,0:T(8,128)(2,1)S(1)}, bf16[2,3,256,128]{3,2,1,0:T(8,128)(2,1)S(1)}, u32[]{:S(2)}, u32[]{:S(2)}) collective-permute-start(bf16[2,3,256,128]{3,2,1,0:T(8,128)(2,1)S(1)} %get-tuple-element.60), channel_id=1, source_target_pairs={{0,64},{16,80},{32,96},{48,112},{64,0},{80,16},{96,32},{112,48},{1... | collective-permute-start | bytes 1179656 | tf_op jit(solution)/shard_map/ppermute | solution.py:371
  105.3 1.0 collective-permute-start.1
  106.3 2.4 collective-permute-start.2
  108.7 1.9 collective-permute-start.3
  110.5 29.4 %collective-permute-done.refs_4_ = bf16[2,3,256,128]{3,2,1,0:T(8,128)(2,1)S(1)} collective-permute-done((bf16[2,3,256,128]{3,2,1,0:T(8,128)(2,1)S(1)}, bf16[2,3,256,128]{3,2,1,0:T(8,128)(2,1)S(1)}, u32[]{:S(2)}, u32[]{:S(2)}) %collective-permute-start) | collective-permute-done | bytes 393248 | tf_op jit(solution)/shard_map/ppermute | solution.py:371
  140.0 0.8 copy-done.6
  140.7 0.8 copy-done.8
  141.5 0.8 copy-done.10
  142.2 0.7 copy-done.12
  143.0 5.7 %all-to-all-start.2 = ((bf16[16,2,2,96,256]{4,3,2,1,0:T(8,128)(2,1)}), bf16[16,2,2,96,256]{4,3,2,1,0:T(8,128)(2,1)}, u32[]{:S(2)}, u32[]{:S(2)}) async-start(bf16[16,2,2,96,256]{4,3,2,1,0:T(8,128)(2,1)} %get-tuple-element.65), calls=%async_computation.2 | async-start | bytes 6291456 | tf_op jit(solution)/shard_map/all_to_all | solution.py:355
  148.7 1.5 collective-permute-start.8
  150.3 1.0 collective-permute-start.9
  151.3 2.4 collective-permute-start.10
  153.8 1.9 copy-done.2
  155.7 6.9 %transform.4 = (bf16[2,2,256,128]{3,2,1,0:T(8,128)(2,1)S(1)}, bf16[2,2,256,128]{3,2,1,0:T(8,128)(2,1)S(1)}, bf16[2,2,256,128]{3,2,1,0:T(8,128)(2,1)S(1)}, bf16[2...) custom-call(s32[11]{0:T(128)S(1)} %get-tuple-element.108.meta_ref, ...), custom_call_target="tpu_custom_call" | custom-call | flops 2415919104 | bytes 14680064 | tf_op jit(solution)/shard_map/transform/pallas_call | solution.py:124
  162.6 0.7 copy-done.36
  163.3 3.0 %collective-permute-start.4 = (bf16[2,2,256,128]{3,2,1,0:T(8,128)(2,1)S(1)}, bf16[2,2,256,128]{3,2,1,0:T(8,128)(2,1)S(1)}, u32[]{:S(2)}, u32[]{:S(2)}) collective-permute-start(bf16[2,2,256,128]{3,2,1,0:T(8,128)(2,1)S(1)} %get-tuple-element.68), channel_id=1, source_target_pairs={{0,64},{16,80},{32,96},{48,112},{64,0},{80,16},{96,32},{112,48},{1... | collective-permute-start | bytes 786440 | tf_op jit(solution)/shard_map/ppermute | solution.py:371
  166.3 3.0 %collective-permute-start.6 = (bf16[2,2,256,128]{3,2,1,0:T(8,128)(2,1)S(1)}, bf16[2,2,256,128]{3,2,1,0:T(8,128)(2,1)S(1)}, u32[]{:S(2)}, u32[]{:S(2)}) collective-permute-start(bf16[2,2,256,128]{3,2,1,0:T(8,128)(2,1)S(1)} %get-tuple-element.70), channel_id=1, source_target_pairs={{0,96},{16,112},{32,64},{48,80},{64,32},{80,48},{96,0},{112,16},{1... | collective-permute-start | bytes 786440 | tf_op jit(solution)/shard_map/ppermute | solution.py:371
  169.2 5.4 %collective-permute-start.7 = (bf16[2,2,256,128]{3,2,1,0:T(8,128)(2,1)S(1)}, bf16[2,2,256,128]{3,2,1,0:T(8,128)(2,1)S(1)}, u32[]{:S(2)}, u32[]{:S(2)}) collective-permute-start(bf16[2,2,256,128]{3,2,1,0:T(8,128)(2,1)S(1)} %get-tuple-element.71), channel_id=1, source_target_pairs={{0,112},{16,64},{32,80},{48,96},{64,48},{80,0},{96,16},{112,32},{1... | collective-permute-start | bytes 786440 | tf_op jit(solution)/shard_map/ppermute | solution.py:371
  174.8 5.7 %settle.4.refs_11_ = bf16[8,8,256,128]{3,2,1,0:T(8,128)(2,1)} custom-call(s32[2]{0:T(128)S(1)} %pad_add_fusion.meta_ref, bf16[2,3,256,128]{3,2,1,0:T(8,128)(2,1)S(1)} %get-tuple-element.75.refs_0_, bf16[2,3,256,128]{3,2,1,0:T(8,128)(2,1)S(1)} %collective-permute-done.8.refs_1_, bf16[2,3,256,128]{3,2,1,0:T(8,128)(2,1)S(1)} %collective-permute-done.9.refs_2_, ...), custom_call_target="tpu_custom_call" | custom-call | flops 1610612736 | bytes 8388608 | tf_op jit(solution)/shard_map/settle/pallas_call | solution.py:265
  180.5 8.4 %collective-permute-done.4.refs_4_ = bf16[2,2,256,128]{3,2,1,0:T(8,128)(2,1)S(1)} collective-permute-done((bf16[2,2,256,128]{3,2,1,0:T(8,128)(2,1)S(1)}, bf16[2,2,256,128]{3,2,1,0:T(8,128)(2,1)S(1)}, u32[]{:S(2)}, u32[]{:S(2)}) %collective-permute-start.4) | collective-permute-done | bytes 262176 | tf_op jit(solution)/shard_map/ppermute | solution.py:371
  188.9 0.7 copy-done.14
  189.6 0.7 copy-done.16
  190.3 0.7 copy-done.18
  191.1 0.7 copy-done.20
  191.8 7.2 %all-to-all-start.3 = ((bf16[16,1,2,96,256]{4,3,2,1,0:T(8,128)(2,1)}), bf16[16,1,2,96,256]{4,3,2,1,0:T(8,128)(2,1)}, u32[]{:S(2)}, u32[]{:S(2)}) async-start(bf16[16,1,2,96,256]{4,3,2,1,0:T(8,128)(2,1)} %copy-done.5), calls=%async_computation.3 | async-start | bytes 3145728 | tf_op jit(solution)/shard_map/all_to_all | solution.py:352
  199.0 3.0 %collective-permute-start.15 = (bf16[2,2,256,128]{3,2,1,0:T(8,128)(2,1)}, bf16[2,2,256,128]{3,2,1,0:T(8,128)(2,1)S(1)}, u32[]{:S(2)}, u32[]{:S(2)}) collective-permute-start(bf16[2,2,256,128]{3,2,1,0:T(8,128)(2,1)} %copy-done.36), channel_id=1, source_target_pairs={{0,16},{16,32},{32,48},{48,0},{64,80},{80,96},{96,112},{112,64},{1... | collective-permute-start | bytes 786440 | tf_op jit(solution)/shard_map/ppermute | solution.py:371
  202.1 2.1 collective-permute-start.17
  204.2 7.0 %transform.5 = (bf16[2,2,256,128]{3,2,1,0:T(8,128)(2,1)S(1)}, bf16[2,2,256,128]{3,2,1,0:T(8,128)(2,1)S(1)}, bf16[2,2,256,128]{3,2,1,0:T(8,128)(2,1)S(1)}, bf16[2...) custom-call(s32[11]{0:T(128)S(1)} %get-tuple-element.107.meta_ref, ...), custom_call_target="tpu_custom_call" | custom-call | flops 2415919104 | bytes 14680064 | tf_op jit(solution)/shard_map/transform/pallas_call | solution.py:124
  211.2 0.9 collective-permute-start.11
  212.6 2.0 collective-permute-done.15.refs_1_
  214.6 2.2 collective-permute-start.13
  216.8 3.1 %collective-permute-start.14 = (bf16[2,2,256,128]{3,2,1,0:T(8,128)(2,1)S(1)}, bf16[2,2,256,128]{3,2,1,0:T(8,128)(2,1)S(1)}, u32[]{:S(2)}, u32[]{:S(2)}) collective-permute-start(bf16[2,2,256,128]{3,2,1,0:T(8,128)(2,1)S(1)} %get-tuple-element.87), channel_id=1, source_target_pairs={{0,112},{16,64},{32,80},{48,96},{64,48},{80,0},{96,16},{112,32},{1... | collective-permute-start | bytes 786440 | tf_op jit(solution)/shard_map/ppermute | solution.py:371
  221.2 4.5 %settle.5.refs_11_ = bf16[8,8,256,128]{3,2,1,0:T(8,128)(2,1)} custom-call(s32[2]{0:T(128)S(1)} %pad_add_fusion.meta_ref, bf16[2,2,256,128]{3,2,1,0:T(8,128)(2,1)S(1)} %get-tuple-element.91.refs_0_, bf16[2,2,256,128]{3,2,1,0:T(8,128)(2,1)S(1)} %collective-permute-done.15.refs_1_, ...), custom_call_target="tpu_custom_call", output_to_operand_aliasing={{}: (12, {})} | custom-call | flops 1073741824 | bytes 6291456 | tf_op jit(solution)/shard_map/settle/pallas_call | solution.py:265
  225.6 15.7 %collective-permute-done.11.refs_4_ = bf16[2,2,256,128]{3,2,1,0:T(8,128)(2,1)S(1)} collective-permute-done((bf16[2,2,256,128]{3,2,1,0:T(8,128)(2,1)S(1)}, bf16[2,2,256,128]{3,2,1,0:T(8,128)(2,1)S(1)}, u32[]{:S(2)}, u32[]{:S(2)}) %collective-permute-start.11) | collective-permute-done | bytes 262176 | tf_op jit(solution)/shard_map/ppermute | solution.py:371
  241.3 0.7 copy-done.22
  242.0 0.7 copy-done.24
  242.7 0.7 copy-done.26
  243.4 0.7 copy-done.28
  244.1 4.8 %transform_whole.1 = bf16[8,1,256,128]{3,2,1,0:T(8,128)(2,1)} custom-call(s32[10]{0:T(128)S(1)} %pad_add_fusion.1.meta_ref, bf16[16,1,2,96,256]{4,3,2,1,0:T(8,128)(2,1)} %all-to-all-done.3.got_ref, bf16[8,1536,1024]{2,1,0:T(8,128)(2,1)} %table_ref.7), custom_call_target="tpu_custom_call" | custom-call | flops 1207959552 | bytes 5242880 | tf_op jit(solution)/shard_map/transform_whole/pallas_call | solution.py:181
  248.9 6.0 %all-to-all-start.4 = ((bf16[8,1,256,128]{3,2,1,0:T(8,128)(2,1)}), bf16[8,1,256,128]{3,2,1,0:T(8,128)(2,1)S(1)}, u32[]{:S(2)}, u32[]{:S(2)}) async-start(bf16[8,1,256,128]{3,2,1,0:T(8,128)(2,1)} %transform_whole.1), calls=%async_computation.4 | async-start | bytes 1048576 | tf_op jit(solution)/shard_map/all_to_all | solution.py:365
  254.9 1.5 collective-permute-start.18
  256.4 0.6 collective-permute-start.19
  257.0 2.6 collective-permute-start.20
  259.6 8.3 %collective-permute-done.18.refs_1_ = bf16[2,2,256,128]{3,2,1,0:T(8,128)(2,1)S(1)} collective-permute-done((bf16[2,2,256,128]{3,2,1,0:T(8,128)(2,1)}, bf16[2,2,256,128]{3,2,1,0:T(8,128)(2,1)S(1)}, u32[]{:S(2)}, u32[]{:S(2)}) %collective-permute-start.18) | collective-permute-done | bytes 262176 | tf_op jit(solution)/shard_map/ppermute | solution.py:371
  268.0 2.1 collective-permute-done.19.refs_2_
  270.1 3.5 %collective-permute-done.20.refs_3_ = bf16[2,2,256,128]{3,2,1,0:T(8,128)(2,1)S(1)} collective-permute-done((bf16[2,2,256,128]{3,2,1,0:T(8,128)(2,1)}, bf16[2,2,256,128]{3,2,1,0:T(8,128)(2,1)S(1)}, u32[]{:S(2)}, u32[]{:S(2)}) %collective-permute-start.20) | collective-permute-done | bytes 262176 | tf_op jit(solution)/shard_map/ppermute | solution.py:371
  273.6 0.9 copy-done.27
  274.6 0.9 copy-done.29
  275.5 4.4 %settle.6.refs_4_ = bf16[8,8,256,128]{3,2,1,0:T(8,128)(2,1)} custom-call(s32[2]{0:T(128)S(1)} %pad_add_fusion.meta_ref, bf16[2,2,256,128]{3,2,1,0:T(8,128)(2,1)S(1)} %get-tuple-element.98.refs_0_, bf16[2,2,256,128]{3,2,1,0:T(8,128)(2,1)S(1)} %collective-permute-done.18.refs_1_, ...), custom_call_target="tpu_custom_call", output_to_operand_aliasing={{}: (12, {})} | custom-call | flops 1073741824 | bytes 6291456 | tf_op jit(solution)/shard_map/settle/pallas_call | solution.py:265
  279.9 3.2 %settle.7 = bf16[8,8,256,128]{3,2,1,0:T(8,128)(2,1)} custom-call(s32[2]{0:T(128)S(1)} %pad_add_fusion.meta_ref, bf16[8,1,256,128]{3,2,1,0:T(8,128)(2,1)S(1)} %all-to-all-done.4.refs_0_, bf16[8,8,256,128]{3,2,1,0:T(8,128)(2,1)} %refs_1_.1, s32[8,128]{1,0:T(8,128)S(1)} %copy-done.30, ...), custom_call_target="tpu_custom_call", output_to_operand_aliasing={{}: (5, {})} | custom-call | flops 536870912 | bytes 4194304 | tf_op jit(solution)/shard_map/settle/pallas_call | solution.py:265
  (93 shorter events, 2.7 us)
Async XLA Ops:
  13.0 2.2 copy-start.3
  15.1 69.6 %all-to-all-start = ((bf16[16,3,2,96,256]{4,3,2,1,0:T(8,128)(2,1)}), bf16[16,3,2,96,256]{4,3,2,1,0:T(8,128)(2,1)}, u32[]{:S(2)}, u32[]{:S(2)}) async-start(bf16[16,3,2,96,256]{4,3,2,1,0:T(8,128)(2,1)} %copy-done.3), calls=%async_computation | async-start | bytes 9437184 | tf_op jit(solution)/shard_map/all_to_all | solution.py:355
  34.9 1.7 copy-start.4
  36.6 1.1 copy-start.5
  37.8 51.2 %copy-start.40 = (s32[128]{0:T(128)S(1)}, s32[128]{0:T(128)}, u32[]{:S(2)}) copy-start(s32[128]{0:T(128)} %param.7) | copy-start | bytes 1540
  84.7 58.3 %all-to-all-start.1 = ((bf16[16,2,2,96,256]{4,3,2,1,0:T(8,128)(2,1)}), bf16[16,2,2,96,256]{4,3,2,1,0:T(8,128)(2,1)S(1)}, u32[]{:S(2)}, u32[]{:S(2)}) async-start(bf16[16,2,2,96,256]{4,3,2,1,0:T(8,128)(2,1)} %copy-done.4), calls=%async_computation.1 | async-start | bytes 6291456 | tf_op jit(solution)/shard_map/all_to_all | solution.py:355
  98.9 0.8 copy-start.31
  99.7 0.7 copy-start.32
  100.4 0.8 copy-start.33
  101.2 38.8 %collective-permute-start = (bf16[2,3,256,128]{3,2,1,0:T(8,128)(2,1)S(1)}, bf16[2,3,256,128]{3,2,1,0:T(8,128)(2,1)S(1)}, u32[]{:S(2)}, u32[]{:S(2)}) collective-permute-start(bf16[2,3,256,128]{3,2,1,0:T(8,128)(2,1)S(1)} %get-tuple-element.60), channel_id=1, source_target_pairs={{0,64},{16,80},{32,96},{48,112},{64,0},{80,16},{96,32},{112,48},{1... | collective-permute-start | bytes 1179656 | tf_op jit(solution)/shard_map/ppermute | solution.py:371
  105.3 35.5 %collective-permute-start.1 = (bf16[2,3,256,128]{3,2,1,0:T(8,128)(2,1)S(1)}, bf16[2,3,256,128]{3,2,1,0:T(8,128)(2,1)S(1)}, u32[]{:S(2)}, u32[]{:S(2)}) collective-permute-start(bf16[2,3,256,128]{3,2,1,0:T(8,128)(2,1)S(1)} %get-tuple-element.61), channel_id=1, source_target_pairs={{0,80},{16,96},{32,112},{48,64},{64,16},{80,32},{96,48},{112,0},{1... | collective-permute-start | bytes 1179656 | tf_op jit(solution)/shard_map/ppermute | solution.py:371
  106.3 35.2 %collective-permute-start.2 = (bf16[2,3,256,128]{3,2,1,0:T(8,128)(2,1)S(1)}, bf16[2,3,256,128]{3,2,1,0:T(8,128)(2,1)S(1)}, u32[]{:S(2)}, u32[]{:S(2)}) collective-permute-start(bf16[2,3,256,128]{3,2,1,0:T(8,128)(2,1)S(1)} %get-tuple-element.62), channel_id=1, source_target_pairs={{0,96},{16,112},{32,64},{48,80},{64,32},{80,48},{96,0},{112,16},{1... | collective-permute-start | bytes 1179656 | tf_op jit(solution)/shard_map/ppermute | solution.py:371
  108.7 33.6 %collective-permute-start.3 = (bf16[2,3,256,128]{3,2,1,0:T(8,128)(2,1)S(1)}, bf16[2,3,256,128]{3,2,1,0:T(8,128)(2,1)S(1)}, u32[]{:S(2)}, u32[]{:S(2)}) collective-permute-start(bf16[2,3,256,128]{3,2,1,0:T(8,128)(2,1)S(1)} %get-tuple-element.63), channel_id=1, source_target_pairs={{0,112},{16,64},{32,80},{48,96},{64,48},{80,0},{96,16},{112,32},{1... | collective-permute-start | bytes 1179656 | tf_op jit(solution)/shard_map/ppermute | solution.py:371
  140.0 0.8 copy-start.6
  140.7 0.8 copy-start.8
  141.5 0.8 copy-start.10
  142.2 0.7 copy-start.12
  143.0 10.8 %copy-start.1 = (bf16[16,2,2,96,256]{4,3,2,1,0:T(8,128)(2,1)}, bf16[16,2,2,96,256]{4,3,2,1,0:T(8,128)(2,1)S(1)}, u32[]{:S(2)}) copy-start(bf16[16,2,2,96,256]{4,3,2,1,0:T(8,128)(2,1)S(1)} %all-to-all-done.1.got_ref) | copy-start | bytes 9437188
  143.0 48.8 %all-to-all-start.2 = ((bf16[16,2,2,96,256]{4,3,2,1,0:T(8,128)(2,1)}), bf16[16,2,2,96,256]{4,3,2,1,0:T(8,128)(2,1)}, u32[]{:S(2)}, u32[]{:S(2)}) async-start(bf16[16,2,2,96,256]{4,3,2,1,0:T(8,128)(2,1)} %get-tuple-element.65), calls=%async_computation.2 | async-start | bytes 6291456 | tf_op jit(solution)/shard_map/all_to_all | solution.py:355
  148.7 17.5 %collective-permute-start.8 = (bf16[2,3,256,128]{3,2,1,0:T(8,128)(2,1)}, bf16[2,3,256,128]{3,2,1,0:T(8,128)(2,1)S(1)}, u32[]{:S(2)}, u32[]{:S(2)}) collective-permute-start(bf16[2,3,256,128]{3,2,1,0:T(8,128)(2,1)} %copy-done.33), channel_id=1, source_target_pairs={{0,16},{16,32},{32,48},{48,0},{64,80},{80,96},{96,112},{112,64},{1... | collective-permute-start | bytes 1179656 | tf_op jit(solution)/shard_map/ppermute | solution.py:371
  150.3 19.0 %collective-permute-start.9 = (bf16[2,3,256,128]{3,2,1,0:T(8,128)(2,1)}, bf16[2,3,256,128]{3,2,1,0:T(8,128)(2,1)S(1)}, u32[]{:S(2)}, u32[]{:S(2)}) collective-permute-start(bf16[2,3,256,128]{3,2,1,0:T(8,128)(2,1)} %copy-done.32), channel_id=1, source_target_pairs={{0,32},{16,48},{32,0},{48,16},{64,96},{80,112},{96,64},{112,80},{1... | collective-permute-start | bytes 1179656 | tf_op jit(solution)/shard_map/ppermute | solution.py:371
  151.3 23.4 %collective-permute-start.10 = (bf16[2,3,256,128]{3,2,1,0:T(8,128)(2,1)}, bf16[2,3,256,128]{3,2,1,0:T(8,128)(2,1)S(1)}, u32[]{:S(2)}, u32[]{:S(2)}) collective-permute-start(bf16[2,3,256,128]{3,2,1,0:T(8,128)(2,1)} %copy-done.31), channel_id=1, source_target_pairs={{0,48},{16,0},{32,16},{48,32},{64,112},{80,64},{96,80},{112,96},{1... | collective-permute-start | bytes 1179656 | tf_op jit(solution)/shard_map/ppermute | solution.py:371
  153.8 1.9 copy-start.2
  155.7 19.0 %copy-start = (bf16[4,4,256,256]{3,2,1,0:T(8,128)(2,1)S(1)}, bf16[4,4,256,256]{3,2,1,0:T(8,128)(2,1)}, u32[]{:S(2)}) copy-start(bf16[4,4,256,256]{3,2,1,0:T(8,128)(2,1)} %refs_3_.1) | copy-start | bytes 6291460
  155.7 19.0 %copy-start.7 = (bf16[2,3,256,128]{3,2,1,0:T(8,128)(2,1)S(1)}, bf16[2,3,256,128]{3,2,1,0:T(8,128)(2,1)}, u32[]{:S(2)}) copy-start(bf16[2,3,256,128]{3,2,1,0:T(8,128)(2,1)} %copy-done.6) | copy-start | bytes 1179652
  155.7 19.0 %copy-start.9 = (bf16[2,3,256,128]{3,2,1,0:T(8,128)(2,1)S(1)}, bf16[2,3,256,128]{3,2,1,0:T(8,128)(2,1)}, u32[]{:S(2)}) copy-start(bf16[2,3,256,128]{3,2,1,0:T(8,128)(2,1)} %copy-done.8) | copy-start | bytes 1179652
  155.7 19.1 %copy-start.11 = (bf16[2,3,256,128]{3,2,1,0:T(8,128)(2,1)S(1)}, bf16[2,3,256,128]{3,2,1,0:T(8,128)(2,1)}, u32[]{:S(2)}) copy-start(bf16[2,3,256,128]{3,2,1,0:T(8,128)(2,1)} %copy-done.10) | copy-start | bytes 1179652
  155.7 19.1 %copy-start.13 = (bf16[2,3,256,128]{3,2,1,0:T(8,128)(2,1)S(1)}, bf16[2,3,256,128]{3,2,1,0:T(8,128)(2,1)}, u32[]{:S(2)}) copy-start(bf16[2,3,256,128]{3,2,1,0:T(8,128)(2,1)} %copy-done.12) | copy-start | bytes 1179652
  155.7 19.1 %copy-start.30 = (s32[8,128]{1,0:T(8,128)S(1)}, s32[8,128]{1,0:T(8,128)}, u32[]{:S(2)}) copy-start(s32[8,128]{1,0:T(8,128)} %refs_2_.1) | copy-start | bytes 12292
  163.3 17.1 %copy-start.34 = (bf16[2,2,256,128]{3,2,1,0:T(8,128)(2,1)}, bf16[2,2,256,128]{3,2,1,0:T(8,128)(2,1)S(1)}, u32[]{:S(2)}) copy-start(bf16[2,2,256,128]{3,2,1,0:T(8,128)(2,1)S(1)} %get-tuple-element.90) | copy-start | bytes 786436
  163.3 17.1 %copy-start.35 = (bf16[2,2,256,128]{3,2,1,0:T(8,128)(2,1)}, bf16[2,2,256,128]{3,2,1,0:T(8,128)(2,1)S(1)}, u32[]{:S(2)}) copy-start(bf16[2,2,256,128]{3,2,1,0:T(8,128)(2,1)S(1)} %get-tuple-element.89) | copy-start | bytes 786436
  163.3 25.6 %collective-permute-start.4 = (bf16[2,2,256,128]{3,2,1,0:T(8,128)(2,1)S(1)}, bf16[2,2,256,128]{3,2,1,0:T(8,128)(2,1)S(1)}, u32[]{:S(2)}, u32[]{:S(2)}) collective-permute-start(bf16[2,2,256,128]{3,2,1,0:T(8,128)(2,1)S(1)} %get-tuple-element.68), channel_id=1, source_target_pairs={{0,64},{16,80},{32,96},{48,112},{64,0},{80,16},{96,32},{112,48},{1... | collective-permute-start | bytes 786440 | tf_op jit(solution)/shard_map/ppermute | solution.py:371
  166.3 23.3 %collective-permute-start.5 = (bf16[2,2,256,128]{3,2,1,0:T(8,128)(2,1)S(1)}, bf16[2,2,256,128]{3,2,1,0:T(8,128)(2,1)S(1)}, u32[]{:S(2)}, u32[]{:S(2)}) collective-permute-start(bf16[2,2,256,128]{3,2,1,0:T(8,128)(2,1)S(1)} %get-tuple-element.69), channel_id=1, source_target_pairs={{0,80},{16,96},{32,112},{48,64},{64,16},{80,32},{96,48},{112,0},{1... | collective-permute-start | bytes 786440 | tf_op jit(solution)/shard_map/ppermute | solution.py:371
  166.3 24.0 %collective-permute-start.6 = (bf16[2,2,256,128]{3,2,1,0:T(8,128)(2,1)S(1)}, bf16[2,2,256,128]{3,2,1,0:T(8,128)(2,1)S(1)}, u32[]{:S(2)}, u32[]{:S(2)}) collective-permute-start(bf16[2,2,256,128]{3,2,1,0:T(8,128)(2,1)S(1)} %get-tuple-element.70), channel_id=1, source_target_pairs={{0,96},{16,112},{32,64},{48,80},{64,32},{80,48},{96,0},{112,16},{1... | collective-permute-start | bytes 786440 | tf_op jit(solution)/shard_map/ppermute | solution.py:371
  169.2 21.8 %collective-permute-start.7 = (bf16[2,2,256,128]{3,2,1,0:T(8,128)(2,1)S(1)}, bf16[2,2,256,128]{3,2,1,0:T(8,128)(2,1)S(1)}, u32[]{:S(2)}, u32[]{:S(2)}) collective-permute-start(bf16[2,2,256,128]{3,2,1,0:T(8,128)(2,1)S(1)} %get-tuple-element.71), channel_id=1, source_target_pairs={{0,112},{16,64},{32,80},{48,96},{64,48},{80,0},{96,16},{112,32},{1... | collective-permute-start | bytes 786440 | tf_op jit(solution)/shard_map/ppermute | solution.py:371
  188.9 0.7 copy-start.14
  189.6 0.7 copy-start.16
  190.3 0.7 copy-start.18
  191.1 0.7 copy-start.20
  191.8 52.3 %all-to-all-start.3 = ((bf16[16,1,2,96,256]{4,3,2,1,0:T(8,128)(2,1)}), bf16[16,1,2,96,256]{4,3,2,1,0:T(8,128)(2,1)}, u32[]{:S(2)}, u32[]{:S(2)}) async-start(bf16[16,1,2,96,256]{4,3,2,1,0:T(8,128)(2,1)} %copy-done.5), calls=%async_computation.3 | async-start | bytes 3145728 | tf_op jit(solution)/shard_map/all_to_all | solution.py:352
  199.0 15.6 %collective-permute-start.15 = (bf16[2,2,256,128]{3,2,1,0:T(8,128)(2,1)}, bf16[2,2,256,128]{3,2,1,0:T(8,128)(2,1)S(1)}, u32[]{:S(2)}, u32[]{:S(2)}) collective-permute-start(bf16[2,2,256,128]{3,2,1,0:T(8,128)(2,1)} %copy-done.36), channel_id=1, source_target_pairs={{0,16},{16,32},{32,48},{48,0},{64,80},{80,96},{96,112},{112,64},{1... | collective-permute-start | bytes 786440 | tf_op jit(solution)/shard_map/ppermute | solution.py:371
  202.0 14.8 %collective-permute-start.16 = (bf16[2,2,256,128]{3,2,1,0:T(8,128)(2,1)}, bf16[2,2,256,128]{3,2,1,0:T(8,128)(2,1)S(1)}, u32[]{:S(2)}, u32[]{:S(2)}) collective-permute-start(bf16[2,2,256,128]{3,2,1,0:T(8,128)(2,1)} %copy-done.35), channel_id=1, source_target_pairs={{0,32},{16,48},{32,0},{48,16},{64,96},{80,112},{96,64},{112,80},{1... | collective-permute-start | bytes 786440 | tf_op jit(solution)/shard_map/ppermute | solution.py:371
  202.1 19.1 %collective-permute-start.17 = (bf16[2,2,256,128]{3,2,1,0:T(8,128)(2,1)}, bf16[2,2,256,128]{3,2,1,0:T(8,128)(2,1)S(1)}, u32[]{:S(2)}, u32[]{:S(2)}) collective-permute-start(bf16[2,2,256,128]{3,2,1,0:T(8,128)(2,1)} %copy-done.34), channel_id=1, source_target_pairs={{0,48},{16,0},{32,16},{48,32},{64,112},{80,64},{96,80},{112,96},{1... | collective-permute-start | bytes 786440 | tf_op jit(solution)/shard_map/ppermute | solution.py:371
  204.2 17.0 %copy-start.15 = (bf16[2,2,256,128]{3,2,1,0:T(8,128)(2,1)S(1)}, bf16[2,2,256,128]{3,2,1,0:T(8,128)(2,1)}, u32[]{:S(2)}) copy-start(bf16[2,2,256,128]{3,2,1,0:T(8,128)(2,1)} %copy-done.14) | copy-start | bytes 786436
  204.2 17.0 %copy-start.17 = (bf16[2,2,256,128]{3,2,1,0:T(8,128)(2,1)S(1)}, bf16[2,2,256,128]{3,2,1,0:T(8,128)(2,1)}, u32[]{:S(2)}) copy-start(bf16[2,2,256,128]{3,2,1,0:T(8,128)(2,1)} %copy-done.16) | copy-start | bytes 786436
  204.2 17.0 %copy-start.19 = (bf16[2,2,256,128]{3,2,1,0:T(8,128)(2,1)S(1)}, bf16[2,2,256,128]{3,2,1,0:T(8,128)(2,1)}, u32[]{:S(2)}) copy-start(bf16[2,2,256,128]{3,2,1,0:T(8,128)(2,1)} %copy-done.18) | copy-start | bytes 786436
  204.2 17.0 %copy-start.21 = (bf16[2,2,256,128]{3,2,1,0:T(8,128)(2,1)S(1)}, bf16[2,2,256,128]{3,2,1,0:T(8,128)(2,1)}, u32[]{:S(2)}) copy-start(bf16[2,2,256,128]{3,2,1,0:T(8,128)(2,1)} %copy-done.20) | copy-start | bytes 786436
  211.1 14.5 %copy-start.37 = (bf16[2,2,256,128]{3,2,1,0:T(8,128)(2,1)}, bf16[2,2,256,128]{3,2,1,0:T(8,128)(2,1)S(1)}, u32[]{:S(2)}) copy-start(bf16[2,2,256,128]{3,2,1,0:T(8,128)(2,1)S(1)} %get-tuple-element.101) | copy-start | bytes 786436
  211.2 14.5 %copy-start.38 = (bf16[2,2,256,128]{3,2,1,0:T(8,128)(2,1)}, bf16[2,2,256,128]{3,2,1,0:T(8,128)(2,1)S(1)}, u32[]{:S(2)}) copy-start(bf16[2,2,256,128]{3,2,1,0:T(8,128)(2,1)S(1)} %get-tuple-element.100) | copy-start | bytes 786436
  211.2 14.5 %copy-start.39 = (bf16[2,2,256,128]{3,2,1,0:T(8,128)(2,1)}, bf16[2,2,256,128]{3,2,1,0:T(8,128)(2,1)S(1)}, u32[]{:S(2)}) copy-start(bf16[2,2,256,128]{3,2,1,0:T(8,128)(2,1)S(1)} %get-tuple-element.99) | copy-start | bytes 786436
  211.2 30.1 %collective-permute-start.11 = (bf16[2,2,256,128]{3,2,1,0:T(8,128)(2,1)S(1)}, bf16[2,2,256,128]{3,2,1,0:T(8,128)(2,1)S(1)}, u32[]{:S(2)}, u32[]{:S(2)}) collective-permute-start(bf16[2,2,256,128]{3,2,1,0:T(8,128)(2,1)S(1)} %get-tuple-element.84), channel_id=1, source_target_pairs={{0,64},{16,80},{32,96},{48,112},{64,0},{80,16},{96,32},{112,48},{1... | collective-permute-start | bytes 786440 | tf_op jit(solution)/shard_map/ppermute | solution.py:371
  212.0 30.0 %collective-permute-start.12 = (bf16[2,2,256,128]{3,2,1,0:T(8,128)(2,1)S(1)}, bf16[2,2,256,128]{3,2,1,0:T(8,128)(2,1)S(1)}, u32[]{:S(2)}, u32[]{:S(2)}) collective-permute-start(bf16[2,2,256,128]{3,2,1,0:T(8,128)(2,1)S(1)} %get-tuple-element.85), channel_id=1, source_target_pairs={{0,80},{16,96},{32,112},{48,64},{64,16},{80,32},{96,48},{112,0},{1... | collective-permute-start | bytes 786440 | tf_op jit(solution)/shard_map/ppermute | solution.py:371
  214.6 28.1 %collective-permute-start.13 = (bf16[2,2,256,128]{3,2,1,0:T(8,128)(2,1)S(1)}, bf16[2,2,256,128]{3,2,1,0:T(8,128)(2,1)S(1)}, u32[]{:S(2)}, u32[]{:S(2)}) collective-permute-start(bf16[2,2,256,128]{3,2,1,0:T(8,128)(2,1)S(1)} %get-tuple-element.86), channel_id=1, source_target_pairs={{0,96},{16,112},{32,64},{48,80},{64,32},{80,48},{96,0},{112,16},{1... | collective-permute-start | bytes 786440 | tf_op jit(solution)/shard_map/ppermute | solution.py:371
  216.8 26.6 %collective-permute-start.14 = (bf16[2,2,256,128]{3,2,1,0:T(8,128)(2,1)S(1)}, bf16[2,2,256,128]{3,2,1,0:T(8,128)(2,1)S(1)}, u32[]{:S(2)}, u32[]{:S(2)}) collective-permute-start(bf16[2,2,256,128]{3,2,1,0:T(8,128)(2,1)S(1)} %get-tuple-element.87), channel_id=1, source_target_pairs={{0,112},{16,64},{32,80},{48,96},{64,48},{80,0},{96,16},{112,32},{1... | collective-permute-start | bytes 786440 | tf_op jit(solution)/shard_map/ppermute | solution.py:371
  241.3 0.7 copy-start.22
  242.0 0.7 copy-start.24
  244.1 29.5 %copy-start.23 = (bf16[2,2,256,128]{3,2,1,0:T(8,128)(2,1)S(1)}, bf16[2,2,256,128]{3,2,1,0:T(8,128)(2,1)}, u32[]{:S(2)}) copy-start(bf16[2,2,256,128]{3,2,1,0:T(8,128)(2,1)} %copy-done.22) | copy-start | bytes 786436
  244.1 29.5 %copy-start.25 = (bf16[2,2,256,128]{3,2,1,0:T(8,128)(2,1)S(1)}, bf16[2,2,256,128]{3,2,1,0:T(8,128)(2,1)}, u32[]{:S(2)}) copy-start(bf16[2,2,256,128]{3,2,1,0:T(8,128)(2,1)} %copy-done.24) | copy-start | bytes 786436
  248.9 31.1 %all-to-all-start.4 = ((bf16[8,1,256,128]{3,2,1,0:T(8,128)(2,1)}), bf16[8,1,256,128]{3,2,1,0:T(8,128)(2,1)S(1)}, u32[]{:S(2)}, u32[]{:S(2)}) async-start(bf16[8,1,256,128]{3,2,1,0:T(8,128)(2,1)} %transform_whole.1), calls=%async_computation.4 | async-start | bytes 1048576 | tf_op jit(solution)/shard_map/all_to_all | solution.py:365
  254.9 13.0 %collective-permute-start.18 = (bf16[2,2,256,128]{3,2,1,0:T(8,128)(2,1)}, bf16[2,2,256,128]{3,2,1,0:T(8,128)(2,1)S(1)}, u32[]{:S(2)}, u32[]{:S(2)}) collective-permute-start(bf16[2,2,256,128]{3,2,1,0:T(8,128)(2,1)} %copy-done.39), channel_id=1, source_target_pairs={{0,16},{16,32},{32,48},{48,0},{64,80},{80,96},{96,112},{112,64},{1... | collective-permute-start | bytes 786440 | tf_op jit(solution)/shard_map/ppermute | solution.py:371
  256.4 13.7 %collective-permute-start.19 = (bf16[2,2,256,128]{3,2,1,0:T(8,128)(2,1)}, bf16[2,2,256,128]{3,2,1,0:T(8,128)(2,1)S(1)}, u32[]{:S(2)}, u32[]{:S(2)}) collective-permute-start(bf16[2,2,256,128]{3,2,1,0:T(8,128)(2,1)} %copy-done.38), channel_id=1, source_target_pairs={{0,32},{16,48},{32,0},{48,16},{64,96},{80,112},{96,64},{112,80},{1... | collective-permute-start | bytes 786440 | tf_op jit(solution)/shard_map/ppermute | solution.py:371
  257.0 16.6 %collective-permute-start.20 = (bf16[2,2,256,128]{3,2,1,0:T(8,128)(2,1)}, bf16[2,2,256,128]{3,2,1,0:T(8,128)(2,1)S(1)}, u32[]{:S(2)}, u32[]{:S(2)}) collective-permute-start(bf16[2,2,256,128]{3,2,1,0:T(8,128)(2,1)} %copy-done.37), channel_id=1, source_target_pairs={{0,48},{16,0},{32,16},{48,32},{64,112},{80,64},{96,80},{112,96},{1... | collective-permute-start | bytes 786440 | tf_op jit(solution)/shard_map/ppermute | solution.py:371
  273.6 1.0 copy-start.27
  274.6 0.9 copy-start.29
  (3 other events, 2.1 us)

commit v3 on v2

v3 whole, which is shorter than its diff:
```python
import functools

import jax
import jax.numpy as jnp
from jax import lax
from jax.experimental import pallas as pl
from jax.experimental.pallas import tpu as pltpu
from jax.sharding import PartitionSpec as P

ZS, Y = 2, 4
CHUNKS = (4, 2, 2)
FLIPPED = (False, True, True)
TIES = {2: ((0, (0, 1, 2, 3, 4, 5)),), 3: ((0, (6, 7)), (1, range(8)))}
STEP = 16
BF16, F32 = jnp.bfloat16, jnp.float32


def prep_kernel(starts, per_dev, key_ref, x_ref, *refs):
    outs, (pick, swap, by_lat, by_order) = refs[: len(starts)], refs[len(starts) :]
    rows, _, orders = x_ref.shape

    @pl.when(pl.program_id(0) == 0)
    def _():
        at = 0
        for first, n in starts:
            count = 16 * n * 2
            i = lax.broadcasted_iota(jnp.int32, (count, orders), 0)
            rest, dest = i // 16, i % 16
            target = dest * (2 * per_dev) + 2 * first + rest
            hit = key_ref[...] == target
            pick[at : at + count, :] = jnp.where(hit, 1.0, 0.0).astype(BF16)
            at += count
        i = lax.broadcasted_iota(jnp.int32, (256, 256), 0)
        j = lax.broadcasted_iota(jnp.int32, (256, 256), 1)
        hit = (i // 16 == j % 16) & (i % 16 == j // 16)
        swap[...] = jnp.where(hit, 1.0, 0.0).astype(BF16)

    def to_lat(c, carry):
        at = pl.multiple_of(c * 16, 16)
        block = x_ref[pl.ds(at, 16), :, :].reshape(256, orders)
        moved = jnp.dot(swap[...], block, preferred_element_type=F32)
        by_lat[:, pl.ds(at, 16), :] = moved.astype(BF16).reshape(STEP, 16, orders)
        return carry

    lax.fori_loop(0, rows // 16, to_lat, 0, unroll=True)

    def to_order(n, carry):
        moved = lax.dot_general(
            pick[...], by_lat[n], (((1,), (1,)), ((), ())), preferred_element_type=F32
        )
        by_order[:, n] = moved.astype(BF16).reshape(by_order.shape[0], 16, rows)
        return carry

    lax.fori_loop(0, STEP, to_order, 0, unroll=True)

    base = 0
    for out, (_, n) in zip(outs, starts):
        for g in range(2 * n):
            block = by_order[base + g].reshape(256, rows)
            moved = jnp.dot(swap[...], block, preferred_element_type=F32).astype(BF16)
            out[:, g // 2, g % 2] = moved.reshape(16, STEP, rows)
        base += 2 * n


def prep(physical, pair_slot, starts, per_dev):
    orders, chans, radii, lats = physical.shape
    sent = sum(32 * n for _, n in starts)
    rows = chans * radii
    x = jnp.transpose(physical, (1, 2, 3, 0)).reshape(rows, lats, orders)
    key = (2 * pair_slot[:, None] + jnp.arange(2, dtype=jnp.int32)[None, :]).reshape(1, orders)
    return pl.pallas_call(
        functools.partial(prep_kernel, starts, per_dev),
        grid=(lats // STEP,),
        in_specs=[
            pl.BlockSpec((1, orders), lambda b: (0, 0)),
            pl.BlockSpec((rows, STEP, orders), lambda b: (0, b, 0)),
        ],
        out_specs=[
            pl.BlockSpec((16, n, 2, STEP, rows), lambda b: (0, 0, 0, b, 0)) for _, n in starts
        ],
        out_shape=[pltpu.HBM((16, n, 2, lats, rows), BF16) for _, n in starts],
        scratch_shapes=[
            pltpu.VMEM((sent, orders), BF16),
            pltpu.VMEM((256, 256), BF16),
            pltpu.VMEM((STEP, rows, orders), BF16),
            pltpu.VMEM((sent // 16, STEP, 16, rows), BF16),
        ],
        compiler_params=pltpu.CompilerParams(vmem_limit_bytes=48 << 20),
        cost_estimate=pl.CostEstimate(
            flops=2 * rows * lats * orders * (orders + 2 * sent),
            bytes_accessed=2 * rows * lats * (orders + sent),
            transcendentals=0,
        ),
        name="prep",
    )(key, x)


def spread(full, row, meta_ref, outs):
    for k in range(8):
        if len(outs) == 8:
            at = pl.multiple_of(meta_ref[1 + k] * 128, 128)
            outs[k][row] = full[:, pl.ds(at, 128)]
        else:
            outs[0][(k, *row)] = full[:, k * 128 : (k + 1) * 128]


def transform_kernel(meta_ref, got_ref, table_ref, *refs):
    outs, full = refs[:-1], refs[-1]
    slot = pl.program_id(0)
    half = table_ref.shape[2] // 2
    depth = table_ref.shape[1]
    rows = got_ref.shape[4]
    low_in = got_ref[:, 0, 0].reshape(depth, rows)
    high_in = got_ref[:, 0, 1].reshape(depth, rows)
    length = meta_ref[9 + slot]
    dims = (((0,), (0,)), ((), ()))
    low = lax.dot_general(low_in, table_ref[0], dims, preferred_element_type=F32)
    high = lax.dot_general(high_in, table_ref[0, :, half:], dims, preferred_element_type=F32)
    column = half + lax.broadcasted_iota(jnp.int32, high.shape, 1)
    full[:, :half] = low[:, :half].astype(BF16)
    full[:, half:] = jnp.where(column < length, low[:, half:], high).astype(BF16)
    spread(full, (0, 0), meta_ref, outs)


def transform_whole_kernel(meta_ref, got_ref, table_ref, *refs):
    outs, full = refs[:-1], refs[-1]
    slot, part = pl.program_id(0), pl.program_id(1)
    srcs, _, _, lats, rows = got_ref.shape
    depth, width = srcs * lats, table_ref.shape[2]
    dims = (((0,), (0,)), ((), ()))

    def product(h):
        return lax.dot_general(
            got_ref[:, 0, h].reshape(depth, rows),
            table_ref[0],
            dims,
            preferred_element_type=F32,
        )

    @pl.when(part == 0)
    def _():
        full[:, :width] = product(0).astype(BF16)

    @pl.when(part == 1)
    def _():
        column = width + lax.broadcasted_iota(jnp.int32, (rows, width), 1)
        chosen = jnp.where(column < meta_ref[9 + slot], product(0), product(1))
        full[:, width:] = chosen.astype(BF16)
        spread(full, (0,), meta_ref, outs)


def transform(got, legendre, meta, first, flipped, by_hop):
    srcs, count, _, lats, rows = got.shape
    degrees = legendre.shape[2]
    if flipped:
        kernel = transform_kernel
        depth, width = srcs // 2 * lats, degrees
        got_spec = pl.BlockSpec(
            (srcs // 2, 1, 2, lats, rows), lambda s, t, m: (t ^ m[0], s, 0, 0, 0)
        )
        table_spec = pl.BlockSpec((1, depth, width), lambda s, t, m: (first + s, t ^ m[0], 0))
        shape, block = (2, count, rows, 128), (1, 1, rows, 128)
        where = lambda s, t, m: (t, s, 0, 0)
    else:
        kernel = transform_whole_kernel
        depth, width = srcs * lats, degrees // 2
        got_spec = pl.BlockSpec((srcs, 1, 2, lats, rows), lambda s, t, m: (0, s, 0, 0, 0))
        table_spec = pl.BlockSpec((1, depth, width), lambda s, t, m: (first + s, 0, t))
        shape, block = (count, rows, 128), (1, rows, 128)
        where = lambda s, t, m: (s, 0, 0)
    if by_hop:
        out_specs = [pl.BlockSpec(block, where)] * 8
        out_shape = [pltpu.HBM(shape, BF16)] * 8
    else:
        out_specs = pl.BlockSpec((8,) + block, lambda s, t, m: (0, *where(s, t, m)))
        out_shape = pltpu.HBM((8,) + shape, BF16)
    return pl.pallas_call(
        kernel,
        grid_spec=pltpu.PrefetchScalarGridSpec(
            num_scalar_prefetch=1,
            grid=(count, 2),
            in_specs=[got_spec, table_spec],
            out_specs=out_specs,
            scratch_shapes=[pltpu.VMEM((rows, degrees), BF16)],
        ),
        out_shape=out_shape,
        compiler_params=pltpu.CompilerParams(vmem_limit_bytes=48 << 20),
        cost_estimate=pl.CostEstimate(
            flops=3 * count * rows * srcs * lats * degrees,
            bytes_accessed=2 * count * srcs * lats * (2 * rows + degrees),
            transcendentals=0,
        ),
        name="transform",
    )(meta, got, legendre)


def invert(row, inv_ref, out_ref, side):
    row = jnp.concatenate([row, row], axis=1)
    for q in range(4):
        every = inv_ref[q].reshape(4 * 256, 256)
        found = jnp.dot(every, side[q], preferred_element_type=F32)
        acc = found[:256]
        for g in range(1, 4):
            acc = jnp.where(row == g, found[g * 256 : (g + 1) * 256], acc)
        acc = acc.astype(BF16)
        out_ref[0, 2 * q] = acc[:, :128]
        out_ref[0, 2 * q + 1] = acc[:, 128:]


def settle_kernel(first, flipped, meta_ref, *refs):
    parts = refs[:-5]
    state_ref, index_ref, inv_ref, out_ref, side = refs[-5:]
    radii = 32

    def part(zs, ys, *where):
        if len(parts) == 8:
            return parts[zs * Y + ys][where].astype(F32)
        return parts[0][(zs * Y + ys, *where)].astype(F32)

    for zs in range(ZS):
        for ys in range(Y):
            at = (zs * Y + ys) * radii
            if len(parts) == 8:
                zl, y = meta_ref[0], meta_ref[1]
                at = pl.multiple_of(((zl ^ zs) * Y + lax.rem(y + (Y - ys), Y)) * radii, radii)
            for c in range(8):
                rows = slice(c * radii, (c + 1) * radii)
                if flipped:
                    total = part(zs, ys, 0, 0, rows) + part(1 - zs, ys, 1, 0, rows)
                else:
                    total = part(zs, ys, 0, rows)
                value = state_ref[0, c, pl.ds(at, radii), :].astype(F32) + 0.5 * total
                lanes = slice((c % 2) * 128, (c % 2) * 128 + 128)
                side[c // 2, pl.ds(at, radii), lanes] = value.astype(BF16)
    invert(index_ref[pl.ds(first + pl.program_id(0), 1), :], inv_ref, out_ref, side)


def settle_chained_kernel(first, flipped, meta_ref, *refs):
    settle_kernel(first, flipped, meta_ref, *refs[:-3], *refs[-2:])


def settle(parts, state, inverses, index, meta, first, count, flipped, so_far):
    shape = parts[0].shape
    block = [1 if i == len(shape) - 3 else n for i, n in enumerate(shape)]
    lead = (0,) * (len(shape) - 3)
    operands = [meta, *parts, state, index, inverses]
    in_specs = [pl.BlockSpec(block, lambda s, m: (*lead, s, 0, 0))] * len(parts) + [
        pl.BlockSpec((1,) + state.shape[1:], lambda s, m: (first + s, 0, 0, 0)),
        pl.BlockSpec(index.shape, lambda s, m: (0, 0)),
        pl.BlockSpec(inverses.shape, lambda s, m: (0, 0, 0, 0)),
    ]
    kernel = settle_kernel if so_far is None else settle_chained_kernel
    aliases = {}
    if so_far is not None:
        operands.append(so_far)
        in_specs.append(pl.BlockSpec(memory_space=pl.ANY))
        aliases = {len(operands) - 1: 0}
    return pl.pallas_call(
        functools.partial(kernel, first, flipped),
        grid_spec=pltpu.PrefetchScalarGridSpec(
            num_scalar_prefetch=1,
            grid=(count,),
            in_specs=in_specs,
            out_specs=pl.BlockSpec((1,) + state.shape[1:], lambda s, m: (first + s, 0, 0, 0)),
            scratch_shapes=[pltpu.VMEM((4, 256, 256), BF16)],
        ),
        out_shape=jax.ShapeDtypeStruct(state.shape, BF16),
        input_output_aliases=aliases,
        compiler_params=pltpu.CompilerParams(vmem_limit_bytes=48 << 20),
        cost_estimate=pl.CostEstimate(
            flops=2 * count * 16 * 256 * 256 * 256,
            bytes_accessed=count * (2 << 20) + (2 << 20),
            transcendentals=0,
        ),
        name="settle",
    )(*operands)


def flip_groups():
    groups = []
    for y in range(Y):
        for zl in range(ZS):
            groups.append([((zl ^ (l // 8)) * Y + y) * 16 + l for l in range(16)])
    return groups


def rad_targets(kz, ky):
    return [(i, ((i // Y) ^ kz) * Y + (i % Y + ky) % Y) for i in range(ZS * Y)]


def on_device(physical, pair_slot, legendre, spectral_state, inverses, block_index):
    pair_count = pair_slot.shape[0]
    per_dev, _, degrees = legendre.shape
    starts, first = [], 0
    for n in CHUNKS:
        starts.append((first, n))
        first += n
    sends = list(prep(physical, pair_slot, tuple(starts[:1]), per_dev))

    lat, rad = lax.axis_index("lat"), lax.axis_index("rad")
    zl, y = rad // Y, rad % Y
    slots = lat * per_dev + jnp.arange(per_dev, dtype=jnp.int32)
    matches = pair_slot[None, :] == slots[:, None]
    owners = jnp.sum(jnp.where(matches, jnp.arange(pair_count, dtype=jnp.int32), 0), axis=1)
    stride = degrees // 2 // pair_count
    lengths = degrees - (1 + owners * stride)
    hops = jnp.arange(8, dtype=jnp.int32)
    blocks = (zl ^ (hops // Y)) * Y + (y + hops) % Y
    place = jnp.stack([zl, y]).astype(jnp.int32)

    out, gots, moves = None, [], []

    final = len(starts) - 1

    def put(k):
        return settle(
            moves[k],
            spectral_state,
            inverses,
            block_index,
            place,
            *starts[k],
            FLIPPED[k],
            out,
        )

    for k in range(len(starts) + 1):
        keep = {}
        if k > 0:
            keep["got", k - 1] = gots[k - 1]
        for chunk, hops_of in TIES.get(k, ()):
            for h in hops_of:
                keep["move", chunk, h] = moves[chunk][h]
        if k > 2:
            keep["out"] = out
        if k < len(starts):
            if k == 1:
                sends.extend(prep(physical, pair_slot, tuple(starts[1:]), per_dev))
            keep["send", k] = sends[k]
        held = dict(zip(keep, lax.optimization_barrier(tuple(keep.values()))))
        out = held.get("out", out)
        if k > 0:
            gots[k - 1] = held["got", k - 1]
        for name, value in held.items():
            if name[0] == "move":
                moves[name[1]][name[2]] = value
        if k < len(starts):
            send = held["send", k]
            if FLIPPED[k]:
                gots.append(
                    lax.all_to_all(
                        send, ("rad", "lat"), 0, 0, tiled=True, axis_index_groups=flip_groups()
                    )
                )
            else:
                gots.append(lax.all_to_all(send, "lat", 0, 0, tiled=True))
        if k > 0:
            first, n = starts[k - 1]
            meta = jnp.concatenate([(lat // 8)[None], blocks, lengths[first : first + n]])
            meta = meta.astype(jnp.int32)
            by_hop = k - 1 < final
            parts = transform(gots[k - 1], legendre, meta, first, FLIPPED[k - 1], by_hop)
            if by_hop:
                moved = [
                    lax.ppermute(parts[h], "rad", rad_targets(h // Y, h % Y)) for h in range(1, 8)
                ]
                moves.append([parts[0]] + moved)
            else:
                moves.append([lax.all_to_all(parts, "rad", 0, 0, tiled=True)])
        if k > 1:
            out = put(k - 2)
    return put(final)


def solution(mesh):
    in_specs = (
        P(None, None, "rad", "lat"),
        P(),
        P("lat", None, None),
        P("lat", None, None, "rad"),
        P(),
        P("lat", "rad"),
    )
    out_specs = P("lat", None, None, "rad")
    return jax.shard_map(
        on_device, mesh=mesh, in_specs=in_specs, out_specs=out_specs, check_vma=False
    )
```

time: 286 us -> 254 us (0.89)
  starting transfers between devices: 71.2 us -> 54.2 us
  local copies, waits for them, and re-layouts: 21.3 us -> 10.6 us
  waiting for transfers between devices: 116 us -> 112 us
    all_to_all x1, waiting for transfers between devices: 0.01 us -> 71.4 us  [on_device(): gots.append(lax.all_to_all(send, 'lat', 0, 0, tiled=True))]
    ppermute x21 -> x14, waiting for transfers between devices: 69.5 us -> 18.1 us  [on_device(): lax.ppermute(parts[h], 'rad', rad_targets(h // Y, h % Y))]
    all_to_all x3 -> x2, waiting for transfers between devices: 47 us -> 5.72 us  [on_device(): lax.all_to_all(send, ('rad', 'lat'), 0, 0, tiled=True, axis_index_groups=...]
    all_to_all x1, waiting for transfers between devices: 0.01 us -> 16.7 us  [on_device(): moves.append([lax.all_to_all(parts, 'rad', 0, 0, tiled=True)])]
    ppermute x21 -> x14, starting transfers between devices: 42.2 us -> 31.1 us  [on_device(): lax.ppermute(parts[h], 'rad', rad_targets(h // Y, h % Y))]
    unnamed x82 -> x46, local copies, waits for them, and re-layouts: 20.5 us -> 10.4 us
    all_to_all x3 -> x2, starting transfers between devices: 15.7 us -> 8.6 us  [on_device(): lax.all_to_all(send, ('rad', 'lat'), 0, 0, tiled=True, axis_index_groups=...]
    pallas_call x8 -> x6, Pallas kernels: 46 us -> 44.3 us  [the longest x3 29 us: transform(): pl.pallas_call(kernel, grid_spec=pltpu.PrefetchScalarGridSpec(num_scalar_...]
  transfers between devices with their start and end apart: 26 -> 18, of which waited for: 8 -> 10; matrix products, arithmetic and copies ran while one was open for 1% -> 0% of each run, Pallas kernels for 18% -> 18%
where the time goes in v3:
time: 254 us; the launch traced here: 250 us
  waiting for transfers between devices  112 us (44%)
  Pallas kernels  72 us (28%)
  starting transfers between devices  54.2 us (21%)
  local copies, waits for them, and re-layouts  10.6 us (4%)
    all_to_all x1, waiting for transfers between devices, on_device(): gots.append(lax.all_to_all(send, 'lat', 0, 0, tiled=True))  71.4 us
    ppermute x14, starting transfers between devices, on_device(): lax.ppermute(parts[h], 'rad', rad_targets(h // Y, h % Y))  31.1 us
    pallas_call x3, Pallas kernels, transform(): pl.pallas_call(kernel, grid_spec=pltpu.PrefetchScalarGridSpec(num_scalar_...  29 us
    pallas_call x2, Pallas kernels, prep(): pl.pallas_call(functools.partial(prep_kernel, starts, per_dev), grid=(lat...  27.7 us
    ppermute x14, waiting for transfers between devices, on_device(): lax.ppermute(parts[h], 'rad', rad_targets(h // Y, h % Y))  18.1 us
    all_to_all x1, waiting for transfers between devices, on_device(): moves.append([lax.all_to_all(parts, 'rad', 0, 0, tiled=True)])  16.7 us
    pallas_call x3, Pallas kernels, settle(): pl.pallas_call(functools.partial(kernel, first, flipped), grid_spec=pltpu...  15.3 us
    unnamed x46, local copies, waits for them, and re-layouts  10.4 us
  transfers between devices with their start and end apart: 18, of which 10 were waited for; matrix products, arithmetic and copies ran while one was open for 0% of the time, Pallas kernels for 18%

profile of v3, /device:TPU:74, one launch (start us, length us, event | category | flops | bytes accessed | tf_op | source)
XLA Modules:
  0.0 250.1 jit_solution(273876111883474168)
XLA Ops:
  0.0 0.7 broadcast_multiply_fusion
  0.7 0.1 iota_add_fusion
  0.7 0.1 add.76.key_ref
  0.9 13.9 %prep.2 = bf16[16,4,2,96,256]{4,3,2,1,0:T(8,128)(2,1)} custom-call(s32[1,256]{1,0:T(1,128)S(1)} %add.76.key_ref, bf16[256,96,256]{2,1,0:T(8,128)(2,1)} %bitcast.8), custom_call_target="tpu_custom_call" | custom-call | flops 6442450944 | bytes 18874368 | tf_op jit(solution)/shard_map/prep/pallas_call | solution.py:71
  14.7 7.3 %all-to-all-start = ((bf16[16,4,2,96,256]{4,3,2,1,0:T(8,128)(2,1)}), bf16[16,4,2,96,256]{4,3,2,1,0:T(8,128)(2,1)}, u32[]{:S(2)}, u32[]{:S(2)}) async-start(bf16[16,4,2,96,256]{4,3,2,1,0:T(8,128)(2,1)} %prep.2), calls=%async_computation | async-start | bytes 12582912 | tf_op jit(solution)/shard_map/all_to_all | solution.py:356
  22.0 13.8 %prep.3 = (bf16[16,2,2,96,256]{4,3,2,1,0:T(8,128)(2,1)}, bf16[16,2,2,96,256]{4,3,2,1,0:T(8,128)(2,1)}) custom-call(s32[1,256]{1,0:T(1,128)S(1)} %add.76.key_ref, bf16[256,96,256]{2,1,0:T(8,128)(2,1)} %bitcast.9), custom_call_target="tpu_custom_call" | custom-call | flops 6442450944 | bytes 18874368 | tf_op jit(solution)/shard_map/prep/pallas_call | solution.py:71
  35.8 71.4 %all-to-all-done.got_ref = bf16[16,4,2,96,256]{4,3,2,1,0:T(8,128)(2,1)} async-done(((bf16[16,4,2,96,256]{4,3,2,1,0:T(8,128)(2,1)}), bf16[16,4,2,96,256]{4,3,2,1,0:T(8,128)(2,1)}, u32[]{:S(2)}, u32[]{:S(2)}) %all-to-all-start) | async-done | bytes 6291488 | tf_op jit(solution)/shard_map/all_to_all | solution.py:356
  107.2 4.2 %all-to-all-start.1 = ((bf16[16,2,2,96,256]{4,3,2,1,0:T(8,128)(2,1)}), bf16[16,2,2,96,256]{4,3,2,1,0:T(8,128)(2,1)S(1)}, u32[]{:S(2)}, u32[]{:S(2)}) async-start(bf16[16,2,2,96,256]{4,3,2,1,0:T(8,128)(2,1)} %get-tuple-element.44), calls=%async_computation.1 | async-start | bytes 6291456 | tf_op jit(solution)/shard_map/all_to_all | solution.py:351
  111.5 0.2 select_reduce_fusion
  111.7 0.1 pad_add_fusion.3.meta_ref
  111.7 13.7 %transform.3 = (bf16[4,256,128]{2,1,0:T(8,128)(2,1)}, bf16[4,256,128]{2,1,0:T(8,128)(2,1)}, bf16[4,256,128]{2,1,0:T(8,128)(2,1)}, bf16[4,256,128]{2,1,0:T(8,128)...) custom-call(s32[13]{0:T(128)S(1)} %pad_add_fusion.3.meta_ref, ...), custom_call_target="tpu_custom_call" | custom-call | flops 4831838208 | bytes 18874368 | tf_op jit(solution)/shard_map/transform/pallas_call | solution.py:177
  125.4 1.6 collective-permute-start
  127.0 0.9 collective-permute-start.1
  128.0 2.4 collective-permute-start.2
  130.4 2.8 %collective-permute-start.3 = (bf16[4,256,128]{2,1,0:T(8,128)(2,1)}, bf16[4,256,128]{2,1,0:T(8,128)(2,1)S(1)}, u32[]{:S(2)}, u32[]{:S(2)}) collective-permute-start(bf16[4,256,128]{2,1,0:T(8,128)(2,1)} %get-tuple-element.50), channel_id=1, source_target_pairs={{0,64},{16,80},{32,96},{48,112},{64,0},{80,16},{96,32},{112,48},{1... | collective-permute-start | bytes 786440 | tf_op jit(solution)/shard_map/ppermute | solution.py:365
  133.2 0.0 collective-permute-start.4
  133.2 5.4 %collective-permute-done.refs_1_ = bf16[4,256,128]{2,1,0:T(8,128)(2,1)S(1)} collective-permute-done((bf16[4,256,128]{2,1,0:T(8,128)(2,1)}, bf16[4,256,128]{2,1,0:T(8,128)(2,1)S(1)}, u32[]{:S(2)}, u32[]{:S(2)}) %collective-permute-start) | collective-permute-done | bytes 262176 | tf_op jit(solution)/shard_map/ppermute | solution.py:365
  138.7 0.7 copy-done.11
  139.4 0.0 collective-permute-done.1.refs_2_
  139.4 0.7 copy-done.13
  140.1 1.7 collective-permute-done.2.refs_3_
  141.7 0.7 copy-done.15
  142.5 0.0 collective-permute-done.3.refs_4_
  142.5 0.7 copy-done.17
  143.2 4.4 %collective-permute-done.4.refs_5_ = bf16[4,256,128]{2,1,0:T(8,128)(2,1)S(1)} collective-permute-done((bf16[4,256,128]{2,1,0:T(8,128)(2,1)}, bf16[4,256,128]{2,1,0:T(8,128)(2,1)S(1)}, u32[]{:S(2)}, u32[]{:S(2)}) %collective-permute-start.4) | collective-permute-done | bytes 262176 | tf_op jit(solution)/shard_map/ppermute | solution.py:365
  147.6 0.7 copy-done.19
  148.3 5.7 %all-to-all-done.1.got_ref = bf16[16,2,2,96,256]{4,3,2,1,0:T(8,128)(2,1)S(1)} async-done(((bf16[16,2,2,96,256]{4,3,2,1,0:T(8,128)(2,1)}), bf16[16,2,2,96,256]{4,3,2,1,0:T(8,128)(2,1)S(1)}, u32[]{:S(2)}, u32[]{:S(2)}) %all-to-all-start.1) | async-done | bytes 3145760 | tf_op jit(solution)/shard_map/all_to_all | solution.py:351
  154.0 4.4 %all-to-all-start.2 = ((bf16[16,2,2,96,256]{4,3,2,1,0:T(8,128)(2,1)}), bf16[16,2,2,96,256]{4,3,2,1,0:T(8,128)(2,1)}, u32[]{:S(2)}, u32[]{:S(2)}) async-start(bf16[16,2,2,96,256]{4,3,2,1,0:T(8,128)(2,1)} %get-tuple-element.53), calls=%async_computation.2 | async-start | bytes 6291456 | tf_op jit(solution)/shard_map/all_to_all | solution.py:351
  158.4 0.1 fusion.4
  158.4 0.1 pad_add_fusion.4
  158.5 5.6 %collective-permute-start.5 = (bf16[4,256,128]{2,1,0:T(8,128)(2,1)}, bf16[4,256,128]{2,1,0:T(8,128)(2,1)S(1)}, u32[]{:S(2)}, u32[]{:S(2)}) collective-permute-start(bf16[4,256,128]{2,1,0:T(8,128)(2,1)} %get-tuple-element.54), channel_id=1, source_target_pairs={{0,96},{16,112},{32,64},{48,80},{64,32},{80,48},{96,0},{112,16},{1... | collective-permute-start | bytes 786440 | tf_op jit(solution)/shard_map/ppermute | solution.py:365
  164.1 0.0 collective-permute-start.6
  164.1 1.9 copy-done.2
  166.1 0.0 copy-start.21
  166.1 7.6 %transform.4 = (bf16[2,2,256,128]{3,2,1,0:T(8,128)(2,1)}, bf16[2,2,256,128]{3,2,1,0:T(8,128)(2,1)}, bf16[2,2,256,128]{3,2,1,0:T(8,128)(2,1)}, bf16[2,2,256,128]{...) custom-call(s32[11]{0:T(128)S(1)} %get-tuple-element.81.meta_ref, ...), custom_call_target="tpu_custom_call" | custom-call | flops 2415919104 | bytes 9437184 | tf_op jit(solution)/shard_map/transform/pallas_call | solution.py:177
  173.7 0.0 collective-permute-start.7
  173.7 3.4 %collective-permute-start.8 = (bf16[2,2,256,128]{3,2,1,0:T(8,128)(2,1)}, bf16[2,2,256,128]{3,2,1,0:T(8,128)(2,1)S(1)}, u32[]{:S(2)}, u32[]{:S(2)}) collective-permute-start(bf16[2,2,256,128]{3,2,1,0:T(8,128)(2,1)} %get-tuple-element.59), channel_id=1, source_target_pairs={{0,32},{16,48},{32,0},{48,16},{64,96},{80,112},{96,64},{112,80},{1... | collective-permute-start | bytes 786440 | tf_op jit(solution)/shard_map/ppermute | solution.py:365
  177.1 0.4 collective-permute-start.9
  177.6 0.0 collective-permute-done.5.refs_6_
  177.6 2.1 collective-permute-start.10
  179.6 0.0 collective-permute-done.6.refs_7_
  179.6 1.5 collective-permute-start.11
  181.2 1.9 collective-permute-done.7.refs_1_
  183.1 8.6 %collective-permute-start.12 = (bf16[2,2,256,128]{3,2,1,0:T(8,128)(2,1)}, bf16[2,2,256,128]{3,2,1,0:T(8,128)(2,1)S(1)}, u32[]{:S(2)}, u32[]{:S(2)}) collective-permute-start(bf16[2,2,256,128]{3,2,1,0:T(8,128)(2,1)} %get-tuple-element.63), channel_id=1, source_target_pairs={{0,96},{16,112},{32,64},{48,80},{64,32},{80,48},{96,0},{112,16},{1... | collective-permute-start | bytes 786440 | tf_op jit(solution)/shard_map/ppermute | solution.py:365
  191.7 0.0 collective-permute-done.8.refs_2_
  191.7 1.5 collective-permute-start.13
  193.3 0.1 pad_add_fusion.meta_ref
  193.4 6.4 %settle.3.refs_11_ = bf16[8,8,256,128]{3,2,1,0:T(8,128)(2,1)} custom-call(s32[2]{0:T(128)S(1)} %pad_add_fusion.meta_ref, bf16[4,256,128]{2,1,0:T(8,128)(2,1)S(1)} %copy-done.10, bf16[4,256,128]{2,1,0:T(8,128)(2,1)S(1)} %copy-done.12, bf16[4,256,128]{2,1,0:T(8,128)(2,1)S(1)} %copy-done.14, bf16[4,256,128]{2,1,0:T(8,128)(2,1)S(1)} %copy-done.16, ...), custom_call_target="tpu_custom_call" | custom-call | flops 2147483648 | bytes 10485760 | tf_op jit(solution)/shard_map/settle/pallas_call | solution.py:258
  199.7 0.0 collective-permute-done.9.refs_3_
  199.7 0.0 collective-permute-done.10.refs_4_
  199.8 1.7 collective-permute-done.11.refs_5_
  201.5 0.7 copy-done.4
  202.2 0.9 collective-permute-done.12.refs_6_
  203.1 0.7 copy-done.6
  203.8 2.1 collective-permute-done.13.refs_7_
  205.8 0.7 copy-done.8
  206.6 7.8 %transform.5 = bf16[8,2,2,256,128]{4,3,2,1,0:T(8,128)(2,1)} custom-call(s32[11]{0:T(128)S(1)} %get-tuple-element.82.meta_ref, bf16[16,2,2,96,256]{4,3,2,1,0:T(8,128)(2,1)} %all-to-all-done.2.got_ref, bf16[8,1536,1024]{2,1,0:T(8,128)(2,1)} %table_ref.5), custom_call_target="tpu_custom_call" | custom-call | flops 2415919104 | bytes 9437184 | tf_op jit(solution)/shard_map/transform/pallas_call | solution.py:177
  214.3 7.2 %all-to-all-start.3 = ((bf16[8,2,2,256,128]{4,3,2,1,0:T(8,128)(2,1)}), bf16[8,2,2,256,128]{4,3,2,1,0:T(8,128)(2,1)}, u32[]{:S(2)}, u32[]{:S(2)}) async-start(bf16[8,2,2,256,128]{4,3,2,1,0:T(8,128)(2,1)} %transform.5), calls=%async_computation.3 | async-start | bytes 4194304 | tf_op jit(solution)/shard_map/all_to_all | solution.py:369
  221.5 0.9 copy-done.5
  222.5 0.9 copy-done.7
  223.4 0.9 copy-done.9
  224.4 4.4 %settle.4.refs_4_ = bf16[8,8,256,128]{3,2,1,0:T(8,128)(2,1)} custom-call(s32[2]{0:T(128)S(1)} %pad_add_fusion.meta_ref, bf16[2,2,256,128]{3,2,1,0:T(8,128)(2,1)S(1)} %copy-done.3, bf16[2,2,256,128]{3,2,1,0:T(8,128)(2,1)S(1)} %collective-permute-done.7.refs_1_, ...), custom_call_target="tpu_custom_call", output_to_operand_aliasing={{}: (12, {})} | custom-call | flops 1073741824 | bytes 6291456 | tf_op jit(solution)/shard_map/settle/pallas_call | solution.py:258
  228.8 16.7 %all-to-all-done.3.refs_0_ = bf16[8,2,2,256,128]{4,3,2,1,0:T(8,128)(2,1)} async-done(((bf16[8,2,2,256,128]{4,3,2,1,0:T(8,128)(2,1)}), bf16[8,2,2,256,128]{4,3,2,1,0:T(8,128)(2,1)}, u32[]{:S(2)}, u32[]{:S(2)}) %all-to-all-start.3) | async-done | bytes 2097184 | tf_op jit(solution)/shard_map/all_to_all | solution.py:369
  245.6 4.5 %settle.5 = bf16[8,8,256,128]{3,2,1,0:T(8,128)(2,1)} custom-call(s32[2]{0:T(128)S(1)} %pad_add_fusion.meta_ref, bf16[8,2,2,256,128]{4,3,2,1,0:T(8,128)(2,1)} %all-to-all-done.3.refs_0_, bf16[8,8,256,128]{3,2,1,0:T(8,128)(2,1)} %refs_1_.1, s32[8,128]{1,0:T(8,128)S(1)} %copy-done.21, ...), custom_call_target="tpu_custom_call", output_to_operand_aliasing={{}: (5, {})} | custom-call | flops 1073741824 | bytes 6291456 | tf_op jit(solution)/shard_map/settle/pallas_call | solution.py:258
  (37 shorter events, 0.1 us)
Async XLA Ops:
  14.7 92.5 %all-to-all-start = ((bf16[16,4,2,96,256]{4,3,2,1,0:T(8,128)(2,1)}), bf16[16,4,2,96,256]{4,3,2,1,0:T(8,128)(2,1)}, u32[]{:S(2)}, u32[]{:S(2)}) async-start(bf16[16,4,2,96,256]{4,3,2,1,0:T(8,128)(2,1)} %prep.2), calls=%async_computation | async-start | bytes 12582912 | tf_op jit(solution)/shard_map/all_to_all | solution.py:356
  35.8 75.6 %copy-start.22 = (s32[128]{0:T(128)S(1)}, s32[128]{0:T(128)}, u32[]{:S(2)}) copy-start(s32[128]{0:T(128)} %param.7) | copy-start | bytes 1540
  107.2 46.7 %all-to-all-start.1 = ((bf16[16,2,2,96,256]{4,3,2,1,0:T(8,128)(2,1)}), bf16[16,2,2,96,256]{4,3,2,1,0:T(8,128)(2,1)S(1)}, u32[]{:S(2)}, u32[]{:S(2)}) async-start(bf16[16,2,2,96,256]{4,3,2,1,0:T(8,128)(2,1)} %get-tuple-element.44), calls=%async_computation.1 | async-start | bytes 6291456 | tf_op jit(solution)/shard_map/all_to_all | solution.py:351
  125.4 13.3 %collective-permute-start = (bf16[4,256,128]{2,1,0:T(8,128)(2,1)}, bf16[4,256,128]{2,1,0:T(8,128)(2,1)S(1)}, u32[]{:S(2)}, u32[]{:S(2)}) collective-permute-start(bf16[4,256,128]{2,1,0:T(8,128)(2,1)} %get-tuple-element.47), channel_id=1, source_target_pairs={{0,16},{16,32},{32,48},{48,0},{64,80},{80,96},{96,112},{112,64},{1... | collective-permute-start | bytes 786440 | tf_op jit(solution)/shard_map/ppermute | solution.py:365
  127.0 12.3 %collective-permute-start.1 = (bf16[4,256,128]{2,1,0:T(8,128)(2,1)}, bf16[4,256,128]{2,1,0:T(8,128)(2,1)S(1)}, u32[]{:S(2)}, u32[]{:S(2)}) collective-permute-start(bf16[4,256,128]{2,1,0:T(8,128)(2,1)} %get-tuple-element.48), channel_id=1, source_target_pairs={{0,32},{16,48},{32,0},{48,16},{64,96},{80,112},{96,64},{112,80},{1... | collective-permute-start | bytes 786440 | tf_op jit(solution)/shard_map/ppermute | solution.py:365
  128.0 13.8 %collective-permute-start.2 = (bf16[4,256,128]{2,1,0:T(8,128)(2,1)}, bf16[4,256,128]{2,1,0:T(8,128)(2,1)S(1)}, u32[]{:S(2)}, u32[]{:S(2)}) collective-permute-start(bf16[4,256,128]{2,1,0:T(8,128)(2,1)} %get-tuple-element.49), channel_id=1, source_target_pairs={{0,48},{16,0},{32,16},{48,32},{64,112},{80,64},{96,80},{112,96},{1... | collective-permute-start | bytes 786440 | tf_op jit(solution)/shard_map/ppermute | solution.py:365
  130.4 12.1 %collective-permute-start.3 = (bf16[4,256,128]{2,1,0:T(8,128)(2,1)}, bf16[4,256,128]{2,1,0:T(8,128)(2,1)S(1)}, u32[]{:S(2)}, u32[]{:S(2)}) collective-permute-start(bf16[4,256,128]{2,1,0:T(8,128)(2,1)} %get-tuple-element.50), channel_id=1, source_target_pairs={{0,64},{16,80},{32,96},{48,112},{64,0},{80,16},{96,32},{112,48},{1... | collective-permute-start | bytes 786440 | tf_op jit(solution)/shard_map/ppermute | solution.py:365
  133.2 14.4 %collective-permute-start.4 = (bf16[4,256,128]{2,1,0:T(8,128)(2,1)}, bf16[4,256,128]{2,1,0:T(8,128)(2,1)S(1)}, u32[]{:S(2)}, u32[]{:S(2)}) collective-permute-start(bf16[4,256,128]{2,1,0:T(8,128)(2,1)} %get-tuple-element.51), channel_id=1, source_target_pairs={{0,80},{16,96},{32,112},{48,64},{64,16},{80,32},{96,48},{112,0},{1... | collective-permute-start | bytes 786440 | tf_op jit(solution)/shard_map/ppermute | solution.py:365
  138.7 0.7 copy-start.11
  139.4 0.7 copy-start.13
  141.7 0.7 copy-start.15
  142.5 0.7 copy-start.17
  147.6 0.7 copy-start.19
  154.0 10.2 %copy-start.1 = (bf16[16,2,2,96,256]{4,3,2,1,0:T(8,128)(2,1)}, bf16[16,2,2,96,256]{4,3,2,1,0:T(8,128)(2,1)S(1)}, u32[]{:S(2)}) copy-start(bf16[16,2,2,96,256]{4,3,2,1,0:T(8,128)(2,1)S(1)} %all-to-all-done.1.got_ref) | copy-start | bytes 9437188
  154.0 52.6 %all-to-all-start.2 = ((bf16[16,2,2,96,256]{4,3,2,1,0:T(8,128)(2,1)}), bf16[16,2,2,96,256]{4,3,2,1,0:T(8,128)(2,1)}, u32[]{:S(2)}, u32[]{:S(2)}) async-start(bf16[16,2,2,96,256]{4,3,2,1,0:T(8,128)(2,1)} %get-tuple-element.53), calls=%async_computation.2 | async-start | bytes 6291456 | tf_op jit(solution)/shard_map/all_to_all | solution.py:351
  158.5 19.1 %collective-permute-start.5 = (bf16[4,256,128]{2,1,0:T(8,128)(2,1)}, bf16[4,256,128]{2,1,0:T(8,128)(2,1)S(1)}, u32[]{:S(2)}, u32[]{:S(2)}) collective-permute-start(bf16[4,256,128]{2,1,0:T(8,128)(2,1)} %get-tuple-element.54), channel_id=1, source_target_pairs={{0,96},{16,112},{32,64},{48,80},{64,32},{80,48},{96,0},{112,16},{1... | collective-permute-start | bytes 786440 | tf_op jit(solution)/shard_map/ppermute | solution.py:365
  164.1 15.5 %collective-permute-start.6 = (bf16[4,256,128]{2,1,0:T(8,128)(2,1)}, bf16[4,256,128]{2,1,0:T(8,128)(2,1)S(1)}, u32[]{:S(2)}, u32[]{:S(2)}) collective-permute-start(bf16[4,256,128]{2,1,0:T(8,128)(2,1)} %get-tuple-element.55), channel_id=1, source_target_pairs={{0,112},{16,64},{32,80},{48,96},{64,48},{80,0},{96,16},{112,32},{1... | collective-permute-start | bytes 786440 | tf_op jit(solution)/shard_map/ppermute | solution.py:365
  164.1 1.9 copy-start.2
  166.0 27.3 %copy-start = (bf16[4,4,256,256]{3,2,1,0:T(8,128)(2,1)S(1)}, bf16[4,4,256,256]{3,2,1,0:T(8,128)(2,1)}, u32[]{:S(2)}) copy-start(bf16[4,4,256,256]{3,2,1,0:T(8,128)(2,1)} %refs_3_.1) | copy-start | bytes 6291460
  166.0 27.3 %copy-start.10 = (bf16[4,256,128]{2,1,0:T(8,128)(2,1)S(1)}, bf16[4,256,128]{2,1,0:T(8,128)(2,1)}, u32[]{:S(2)}) copy-start(bf16[4,256,128]{2,1,0:T(8,128)(2,1)} %get-tuple-element.65.refs_0_) | copy-start | bytes 786436
  166.0 27.3 %copy-start.12 = (bf16[4,256,128]{2,1,0:T(8,128)(2,1)S(1)}, bf16[4,256,128]{2,1,0:T(8,128)(2,1)}, u32[]{:S(2)}) copy-start(bf16[4,256,128]{2,1,0:T(8,128)(2,1)} %copy-done.11) | copy-start | bytes 786436
  166.0 27.3 %copy-start.14 = (bf16[4,256,128]{2,1,0:T(8,128)(2,1)S(1)}, bf16[4,256,128]{2,1,0:T(8,128)(2,1)}, u32[]{:S(2)}) copy-start(bf16[4,256,128]{2,1,0:T(8,128)(2,1)} %copy-done.13) | copy-start | bytes 786436
  166.0 27.3 %copy-start.16 = (bf16[4,256,128]{2,1,0:T(8,128)(2,1)S(1)}, bf16[4,256,128]{2,1,0:T(8,128)(2,1)}, u32[]{:S(2)}) copy-start(bf16[4,256,128]{2,1,0:T(8,128)(2,1)} %copy-done.15) | copy-start | bytes 786436
  166.0 27.3 %copy-start.18 = (bf16[4,256,128]{2,1,0:T(8,128)(2,1)S(1)}, bf16[4,256,128]{2,1,0:T(8,128)(2,1)}, u32[]{:S(2)}) copy-start(bf16[4,256,128]{2,1,0:T(8,128)(2,1)} %copy-done.17) | copy-start | bytes 786436
  166.1 27.3 %copy-start.20 = (bf16[4,256,128]{2,1,0:T(8,128)(2,1)S(1)}, bf16[4,256,128]{2,1,0:T(8,128)(2,1)}, u32[]{:S(2)}) copy-start(bf16[4,256,128]{2,1,0:T(8,128)(2,1)} %copy-done.19) | copy-start | bytes 786436
  166.1 27.3 %copy-start.21 = (s32[8,128]{1,0:T(8,128)S(1)}, s32[8,128]{1,0:T(8,128)}, u32[]{:S(2)}) copy-start(s32[8,128]{1,0:T(8,128)} %refs_2_.1) | copy-start | bytes 12292
  173.7 9.4 %collective-permute-start.7 = (bf16[2,2,256,128]{3,2,1,0:T(8,128)(2,1)}, bf16[2,2,256,128]{3,2,1,0:T(8,128)(2,1)S(1)}, u32[]{:S(2)}, u32[]{:S(2)}) collective-permute-start(bf16[2,2,256,128]{3,2,1,0:T(8,128)(2,1)} %get-tuple-element.58), channel_id=1, source_target_pairs={{0,16},{16,32},{32,48},{48,0},{64,80},{80,96},{96,112},{112,64},{1... | collective-permute-start | bytes 786440 | tf_op jit(solution)/shard_map/ppermute | solution.py:365
  173.7 18.0 %collective-permute-start.8 = (bf16[2,2,256,128]{3,2,1,0:T(8,128)(2,1)}, bf16[2,2,256,128]{3,2,1,0:T(8,128)(2,1)S(1)}, u32[]{:S(2)}, u32[]{:S(2)}) collective-permute-start(bf16[2,2,256,128]{3,2,1,0:T(8,128)(2,1)} %get-tuple-element.59), channel_id=1, source_target_pairs={{0,32},{16,48},{32,0},{48,16},{64,96},{80,112},{96,64},{112,80},{1... | collective-permute-start | bytes 786440 | tf_op jit(solution)/shard_map/ppermute | solution.py:365
  177.1 22.6 %collective-permute-start.9 = (bf16[2,2,256,128]{3,2,1,0:T(8,128)(2,1)}, bf16[2,2,256,128]{3,2,1,0:T(8,128)(2,1)S(1)}, u32[]{:S(2)}, u32[]{:S(2)}) collective-permute-start(bf16[2,2,256,128]{3,2,1,0:T(8,128)(2,1)} %get-tuple-element.60), channel_id=1, source_target_pairs={{0,48},{16,0},{32,16},{48,32},{64,112},{80,64},{96,80},{112,96},{1... | collective-permute-start | bytes 786440 | tf_op jit(solution)/shard_map/ppermute | solution.py:365
  177.6 22.2 %collective-permute-start.10 = (bf16[2,2,256,128]{3,2,1,0:T(8,128)(2,1)}, bf16[2,2,256,128]{3,2,1,0:T(8,128)(2,1)S(1)}, u32[]{:S(2)}, u32[]{:S(2)}) collective-permute-start(bf16[2,2,256,128]{3,2,1,0:T(8,128)(2,1)} %get-tuple-element.61), channel_id=1, source_target_pairs={{0,64},{16,80},{32,96},{48,112},{64,0},{80,16},{96,32},{112,48},{1... | collective-permute-start | bytes 786440 | tf_op jit(solution)/shard_map/ppermute | solution.py:365
  179.6 21.8 %collective-permute-start.11 = (bf16[2,2,256,128]{3,2,1,0:T(8,128)(2,1)}, bf16[2,2,256,128]{3,2,1,0:T(8,128)(2,1)S(1)}, u32[]{:S(2)}, u32[]{:S(2)}) collective-permute-start(bf16[2,2,256,128]{3,2,1,0:T(8,128)(2,1)} %get-tuple-element.62), channel_id=1, source_target_pairs={{0,80},{16,96},{32,112},{48,64},{64,16},{80,32},{96,48},{112,0},{1... | collective-permute-start | bytes 786440 | tf_op jit(solution)/shard_map/ppermute | solution.py:365
  183.1 20.0 %collective-permute-start.12 = (bf16[2,2,256,128]{3,2,1,0:T(8,128)(2,1)}, bf16[2,2,256,128]{3,2,1,0:T(8,128)(2,1)S(1)}, u32[]{:S(2)}, u32[]{:S(2)}) collective-permute-start(bf16[2,2,256,128]{3,2,1,0:T(8,128)(2,1)} %get-tuple-element.63), channel_id=1, source_target_pairs={{0,96},{16,112},{32,64},{48,80},{64,32},{80,48},{96,0},{112,16},{1... | collective-permute-start | bytes 786440 | tf_op jit(solution)/shard_map/ppermute | solution.py:365
  191.7 14.1 %collective-permute-start.13 = (bf16[2,2,256,128]{3,2,1,0:T(8,128)(2,1)}, bf16[2,2,256,128]{3,2,1,0:T(8,128)(2,1)S(1)}, u32[]{:S(2)}, u32[]{:S(2)}) collective-permute-start(bf16[2,2,256,128]{3,2,1,0:T(8,128)(2,1)} %get-tuple-element.64), channel_id=1, source_target_pairs={{0,112},{16,64},{32,80},{48,96},{64,48},{80,0},{96,16},{112,32},{1... | collective-permute-start | bytes 786440 | tf_op jit(solution)/shard_map/ppermute | solution.py:365
  201.5 0.7 copy-start.4
  203.1 0.7 copy-start.6
  205.8 0.7 copy-start.8
  214.3 7.2 %copy-start.3 = (bf16[2,2,256,128]{3,2,1,0:T(8,128)(2,1)S(1)}, bf16[2,2,256,128]{3,2,1,0:T(8,128)(2,1)}, u32[]{:S(2)}) copy-start(bf16[2,2,256,128]{3,2,1,0:T(8,128)(2,1)} %get-tuple-element.72.refs_0_) | copy-start | bytes 786436
  214.3 31.2 %all-to-all-start.3 = ((bf16[8,2,2,256,128]{4,3,2,1,0:T(8,128)(2,1)}), bf16[8,2,2,256,128]{4,3,2,1,0:T(8,128)(2,1)}, u32[]{:S(2)}, u32[]{:S(2)}) async-start(bf16[8,2,2,256,128]{4,3,2,1,0:T(8,128)(2,1)} %transform.5), calls=%async_computation.3 | async-start | bytes 4194304 | tf_op jit(solution)/shard_map/all_to_all | solution.py:369
  221.5 1.0 copy-start.5
  222.5 0.9 copy-start.7
  223.4 0.9 copy-start.9

commit v4 on v3

--- a/solution.py
+++ b/solution.py
@@ -10,7 +10,8 @@
 ZS, Y = 2, 4
 CHUNKS = (4, 2, 2)
 FLIPPED = (False, True, True)
-TIES = {2: ((0, (0, 1, 2, 3, 4, 5)),), 3: ((0, (6, 7)), (1, range(8)))}
+TIES = {2: ((0, (0, 1, 2, 3, 4, 5, 7)),), 3: ((0, (6,)), (1, range(8)))}
+ORDER = (6, 2, 5, 7, 1, 3, 4)
 STEP = 16
 BF16, F32 = jnp.bfloat16, jnp.float32
 
@@ -191,7 +192,7 @@
             transcendentals=0,
         ),
         name="transform",
-    )(meta, got, legendre)
+    )(meta, pltpu.with_memory_space_constraint(got, pltpu.HBM), legendre)
 
 
 def invert(row, inv_ref, out_ref, side):
@@ -295,7 +296,7 @@
     for n in CHUNKS:
         starts.append((first, n))
         first += n
-    sends = list(prep(physical, pair_slot, tuple(starts[:1]), per_dev))
+    sends = list(prep(physical, pair_slot, tuple(starts), per_dev))
 
     lat, rad = lax.axis_index("lat"), lax.axis_index("rad")
     zl, y = rad // Y, rad % Y
@@ -334,8 +335,6 @@
         if k > 2:
             keep["out"] = out
         if k < len(starts):
-            if k == 1:
-                sends.extend(prep(physical, pair_slot, tuple(starts[1:]), per_dev))
             keep["send", k] = sends[k]
         held = dict(zip(keep, lax.optimization_barrier(tuple(keep.values()))))
         out = held.get("out", out)
@@ -358,13 +357,13 @@
             first, n = starts[k - 1]
             meta = jnp.concatenate([(lat // 8)[None], blocks, lengths[first : first + n]])
             meta = meta.astype(jnp.int32)
-            by_hop = k - 1 < final
+            by_hop = True
             parts = transform(gots[k - 1], legendre, meta, first, FLIPPED[k - 1], by_hop)
             if by_hop:
-                moved = [
-                    lax.ppermute(parts[h], "rad", rad_targets(h // Y, h % Y)) for h in range(1, 8)
-                ]
-                moves.append([parts[0]] + moved)
+                moved = {0: parts[0]}
+                for h in ORDER:
+                    moved[h] = lax.ppermute(parts[h], "rad", rad_targets(h // Y, h % Y))
+                moves.append([moved[h] for h in range(8)])
             else:
                 moves.append([lax.all_to_all(parts, "rad", 0, 0, tiled=True)])
         if k > 1:

time: 254 us -> 241 us (0.949)
  blocking collectives: 0 us -> 76.8 us
  waiting for transfers between devices: 112 us -> 41.1 us
  Pallas kernels: 72 us -> 60.5 us
  local copies, waits for them, and re-layouts: 10.6 us -> 5.92 us
  starting transfers between devices: 54.2 us -> 50.3 us
    all_to_all x2 -> x0, waiting for transfers between devices: 88.1 us -> none  [the longest x1 71.4 us: on_device(): gots.append(lax.all_to_all(send, 'lat', 0, 0, tiled=True))]
    all_to_all x0 -> x1, blocking collectives: none -> 76.8 us  [on_device(): gots.append(lax.all_to_all(send, 'lat', 0, 0, tiled=True))]
    ppermute x14 -> x21, waiting for transfers between devices: 18.1 us -> 39.8 us  [on_device(): moved[h] = lax.ppermute(parts[h], 'rad', rad_targets(h // Y, h % Y))]
    all_to_all x2 -> x0, starting transfers between devices: 14.5 us -> none  [the longest x1 7.26 us: on_device(): gots.append(lax.all_to_all(send, 'lat', 0, 0, tiled=True))]
    pallas_call x2 -> x1, Pallas kernels: 27.7 us -> 15.9 us  [prep(): pl.pallas_call(functools.partial(prep_kernel, starts, per_dev), grid=(lat...]
    ppermute x14 -> x21, starting transfers between devices: 31.1 us -> 37.9 us  [on_device(): moved[h] = lax.ppermute(parts[h], 'rad', rad_targets(h // Y, h % Y))]
    unnamed x46, local copies, waits for them, and re-layouts: 10.4 us -> 5.71 us
    all_to_all x2, waiting for transfers between devices: 5.72 us -> 1.34 us  [on_device(): lax.all_to_all(send, ('rad', 'lat'), 0, 0, tiled=True, axis_index_groups=...]
  transfers between devices with their start and end apart: 18 -> 23, of which waited for: 10 -> 13; matrix products, arithmetic and copies ran while one was open for 0% -> 0% of each run, Pallas kernels for 18% -> 14%
where the time goes in v4:
time: 241 us; the launch traced here: 236 us
  blocking collectives  76.8 us (32%)
  Pallas kernels  60.5 us (25%)
  starting transfers between devices  50.3 us (21%)
  waiting for transfers between devices  41.1 us (17%)
  local copies, waits for them, and re-layouts  5.92 us (2%)
    all_to_all x1, blocking collectives, on_device(): gots.append(lax.all_to_all(send, 'lat', 0, 0, tiled=True))  76.8 us
    ppermute x21, waiting for transfers between devices, on_device(): moved[h] = lax.ppermute(parts[h], 'rad', rad_targets(h // Y, h % Y))  39.8 us
    ppermute x21, starting transfers between devices, on_device(): moved[h] = lax.ppermute(parts[h], 'rad', rad_targets(h // Y, h % Y))  37.9 us
    pallas_call x3, Pallas kernels, transform(): pl.pallas_call(kernel, grid_spec=pltpu.PrefetchScalarGridSpec(num_scalar_...  29.4 us
    pallas_call x1, Pallas kernels, prep(): pl.pallas_call(functools.partial(prep_kernel, starts, per_dev), grid=(lat...  15.9 us
    pallas_call x3, Pallas kernels, settle(): pl.pallas_call(functools.partial(kernel, first, flipped), grid_spec=pltpu...  15.2 us
    all_to_all x2, starting transfers between devices, on_device(): lax.all_to_all(send, ('rad', 'lat'), 0, 0, tiled=True, axis_index_groups=...  12.4 us
    unnamed x46, local copies, waits for them, and re-layouts  5.71 us
  transfers between devices with their start and end apart: 23, of which 13 were waited for; matrix products, arithmetic and copies ran while one was open for 0% of the time, Pallas kernels for 14%

profile of v4, /device:TPU:74, one launch (start us, length us, event | category | flops | bytes accessed | tf_op | source)
XLA Modules:
  0.0 236.1 jit_solution(7227904863023685771)
XLA Ops:
  0.0 0.7 broadcast_multiply_fusion
  0.7 0.1 iota_add_fusion
  0.7 0.1 add.69.key_ref
  0.9 15.9 %prep.1 = (bf16[16,4,2,96,256]{4,3,2,1,0:T(8,128)(2,1)}, bf16[16,2,2,96,256]{4,3,2,1,0:T(8,128)(2,1)}, bf16[16,2,2,96,256]{4,3,2,1,0:T(8,128)(2,1)}) custom-call(s32[1,256]{1,0:T(1,128)S(1)} %add.69.key_ref, bf16[256,96,256]{2,1,0:T(8,128)(2,1)} %bitcast.8), custom_call_target="tpu_custom_call" | custom-call | flops 9663676416 | bytes 25165824 | tf_op jit(solution)/shard_map/prep/pallas_call | solution.py:72
  16.8 76.8 %all_to_all.15.got_ref = bf16[16,4,2,96,256]{4,3,2,1,0:T(8,128)(2,1)} all-to-all(bf16[16,4,2,96,256]{4,3,2,1,0:T(8,128)(2,1)} %get-tuple-element.53), channel_id=1, replica_groups=mesh['rad'=8,'lat'=16] {'lat'}, dimensions={0} | all-to-all | bytes 12582912 | tf_op jit(solution)/shard_map/all_to_all | solution.py:355
  93.7 8.0 %all-to-all-start.1 = ((bf16[16,2,2,96,256]{4,3,2,1,0:T(8,128)(2,1)}), bf16[16,2,2,96,256]{4,3,2,1,0:T(8,128)(2,1)S(1)}, u32[]{:S(2)}, u32[]{:S(2)}) async-start(bf16[16,2,2,96,256]{4,3,2,1,0:T(8,128)(2,1)} %get-tuple-element.55), calls=%async_computation.1 | async-start | bytes 6291456 | tf_op jit(solution)/shard_map/all_to_all | solution.py:350
  101.7 0.2 select_reduce_fusion
  101.9 0.1 pad_add_fusion.3.meta_ref
  102.0 13.6 %transform.3 = (bf16[4,256,128]{2,1,0:T(8,128)(2,1)}, bf16[4,256,128]{2,1,0:T(8,128)(2,1)}, bf16[4,256,128]{2,1,0:T(8,128)(2,1)}, bf16[4,256,128]{2,1,0:T(8,128)...) custom-call(s32[13]{0:T(128)S(1)} %pad_add_fusion.3.meta_ref, ...), custom_call_target="tpu_custom_call" | custom-call | flops 4831838208 | bytes 18874368 | tf_op jit(solution)/shard_map/transform/pallas_call | solution.py:178
  115.6 1.6 collective-permute-start
  117.3 0.9 collective-permute-start.1
  118.2 2.4 %collective-permute-start.2 = (bf16[4,256,128]{2,1,0:T(8,128)(2,1)}, bf16[4,256,128]{2,1,0:T(8,128)(2,1)S(1)}, u32[]{:S(2)}, u32[]{:S(2)}) collective-permute-start(bf16[4,256,128]{2,1,0:T(8,128)(2,1)} %get-tuple-element.60), channel_id=1, source_target_pairs={{0,48},{16,0},{32,16},{48,32},{64,112},{80,64},{96,80},{112,96},{1... | collective-permute-start | bytes 786440 | tf_op jit(solution)/shard_map/ppermute | solution.py:365
  120.6 1.6 collective-permute-start.3
  122.2 0.0 collective-permute-start.4
  122.2 7.2 %collective-permute-done.refs_1_ = bf16[4,256,128]{2,1,0:T(8,128)(2,1)S(1)} collective-permute-done((bf16[4,256,128]{2,1,0:T(8,128)(2,1)}, bf16[4,256,128]{2,1,0:T(8,128)(2,1)S(1)}, u32[]{:S(2)}, u32[]{:S(2)}) %collective-permute-start) | collective-permute-done | bytes 262176 | tf_op jit(solution)/shard_map/ppermute | solution.py:365
  129.4 0.7 copy-done.8
  130.1 0.0 collective-permute-start.5
  130.1 0.0 collective-permute-done.1.refs_2_
  130.2 0.7 copy-done.10
  130.9 1.9 collective-permute-done.2.refs_3_
  132.8 0.7 copy-done.12
  133.5 0.0 collective-permute-done.3.refs_4_
  133.5 0.7 copy-done.14
  134.2 6.1 %collective-permute-done.4.refs_5_ = bf16[4,256,128]{2,1,0:T(8,128)(2,1)S(1)} collective-permute-done((bf16[4,256,128]{2,1,0:T(8,128)(2,1)}, bf16[4,256,128]{2,1,0:T(8,128)(2,1)S(1)}, u32[]{:S(2)}, u32[]{:S(2)}) %collective-permute-start.4) | collective-permute-done | bytes 262176 | tf_op jit(solution)/shard_map/ppermute | solution.py:365
  140.4 0.7 copy-done.16
  141.0 1.1 collective-permute-done.5.refs_7_
  142.2 0.7 copy-done.18
  142.9 1.3 all-to-all-done.1.got_ref
  144.3 4.4 %all-to-all-start.2 = ((bf16[16,2,2,96,256]{4,3,2,1,0:T(8,128)(2,1)}), bf16[16,2,2,96,256]{4,3,2,1,0:T(8,128)(2,1)}, u32[]{:S(2)}, u32[]{:S(2)}) async-start(bf16[16,2,2,96,256]{4,3,2,1,0:T(8,128)(2,1)} %get-tuple-element.65), calls=%async_computation.2 | async-start | bytes 6291456 | tf_op jit(solution)/shard_map/all_to_all | solution.py:350
  148.7 0.1 fusion.4
  148.7 0.1 pad_add_fusion.4
  148.8 4.4 %collective-permute-start.6 = (bf16[4,256,128]{2,1,0:T(8,128)(2,1)}, bf16[4,256,128]{2,1,0:T(8,128)(2,1)S(1)}, u32[]{:S(2)}, u32[]{:S(2)}) collective-permute-start(bf16[4,256,128]{2,1,0:T(8,128)(2,1)} %get-tuple-element.66), channel_id=1, source_target_pairs={{0,96},{16,112},{32,64},{48,80},{64,32},{80,48},{96,0},{112,16},{1... | collective-permute-start | bytes 786440 | tf_op jit(solution)/shard_map/ppermute | solution.py:365
  153.3 0.0 copy-start.20
  153.3 8.0 %transform.4 = (bf16[2,2,256,128]{3,2,1,0:T(8,128)(2,1)}, bf16[2,2,256,128]{3,2,1,0:T(8,128)(2,1)}, bf16[2,2,256,128]{3,2,1,0:T(8,128)(2,1)}, bf16[2,2,256,128]{...) custom-call(s32[11]{0:T(128)S(1)} %get-tuple-element.101.meta_ref, ...), custom_call_target="tpu_custom_call" | custom-call | flops 2415919104 | bytes 9437184 | tf_op jit(solution)/shard_map/transform/pallas_call | solution.py:178
  161.3 0.1 collective-permute-start.7
  161.3 3.4 %collective-permute-start.8 = (bf16[2,2,256,128]{3,2,1,0:T(8,128)(2,1)}, bf16[2,2,256,128]{3,2,1,0:T(8,128)(2,1)S(1)}, u32[]{:S(2)}, u32[]{:S(2)}) collective-permute-start(bf16[2,2,256,128]{3,2,1,0:T(8,128)(2,1)} %get-tuple-element.70), channel_id=1, source_target_pairs={{0,32},{16,48},{32,0},{48,16},{64,96},{80,112},{96,64},{112,80},{1... | collective-permute-start | bytes 786440 | tf_op jit(solution)/shard_map/ppermute | solution.py:365
  164.8 0.4 collective-permute-start.9
  165.2 0.0 collective-permute-start.10
  165.2 0.0 collective-permute-done.6.refs_6_
  165.2 3.0 %collective-permute-start.11 = (bf16[2,2,256,128]{3,2,1,0:T(8,128)(2,1)}, bf16[2,2,256,128]{3,2,1,0:T(8,128)(2,1)S(1)}, u32[]{:S(2)}, u32[]{:S(2)}) collective-permute-start(bf16[2,2,256,128]{3,2,1,0:T(8,128)(2,1)} %get-tuple-element.73), channel_id=1, source_target_pairs={{0,80},{16,96},{32,112},{48,64},{64,16},{80,32},{96,48},{112,0},{1... | collective-permute-start | bytes 786440 | tf_op jit(solution)/shard_map/ppermute | solution.py:365
  168.3 2.5 %collective-permute-done.7.refs_1_ = bf16[2,2,256,128]{3,2,1,0:T(8,128)(2,1)S(1)} collective-permute-done((bf16[2,2,256,128]{3,2,1,0:T(8,128)(2,1)}, bf16[2,2,256,128]{3,2,1,0:T(8,128)(2,1)S(1)}, u32[]{:S(2)}, u32[]{:S(2)}) %collective-permute-start.7) | collective-permute-done | bytes 262176 | tf_op jit(solution)/shard_map/ppermute | solution.py:365
  170.7 5.0 %collective-permute-start.12 = (bf16[2,2,256,128]{3,2,1,0:T(8,128)(2,1)}, bf16[2,2,256,128]{3,2,1,0:T(8,128)(2,1)S(1)}, u32[]{:S(2)}, u32[]{:S(2)}) collective-permute-start(bf16[2,2,256,128]{3,2,1,0:T(8,128)(2,1)} %get-tuple-element.74), channel_id=1, source_target_pairs={{0,96},{16,112},{32,64},{48,80},{64,32},{80,48},{96,0},{112,16},{1... | collective-permute-start | bytes 786440 | tf_op jit(solution)/shard_map/ppermute | solution.py:365
  175.7 0.0 collective-permute-done.8.refs_2_
  175.7 1.7 collective-permute-start.13
  177.4 0.1 pad_add_fusion.meta_ref
  177.5 6.4 %settle.3.refs_11_ = bf16[8,8,256,128]{3,2,1,0:T(8,128)(2,1)} custom-call(s32[2]{0:T(128)S(1)} %pad_add_fusion.meta_ref, bf16[4,256,128]{2,1,0:T(8,128)(2,1)S(1)} %copy-done.7, bf16[4,256,128]{2,1,0:T(8,128)(2,1)S(1)} %copy-done.9, bf16[4,256,128]{2,1,0:T(8,128)(2,1)S(1)} %copy-done.11, bf16[4,256,128]{2,1,0:T(8,128)(2,1)S(1)} %copy-done.13, ...), custom_call_target="tpu_custom_call" | custom-call | flops 2147483648 | bytes 10485760 | tf_op jit(solution)/shard_map/settle/pallas_call | solution.py:259
  183.9 0.0 collective-permute-done.9.refs_3_
  183.9 4.2 %collective-permute-done.11.refs_5_ = bf16[2,2,256,128]{3,2,1,0:T(8,128)(2,1)S(1)} collective-permute-done((bf16[2,2,256,128]{3,2,1,0:T(8,128)(2,1)}, bf16[2,2,256,128]{3,2,1,0:T(8,128)(2,1)S(1)}, u32[]{:S(2)}, u32[]{:S(2)}) %collective-permute-start.11) | collective-permute-done | bytes 262176 | tf_op jit(solution)/shard_map/ppermute | solution.py:365
  188.1 0.8 collective-permute-done.12.refs_6_
  188.9 0.7 copy-done.2
  189.6 2.6 %collective-permute-done.13.refs_7_ = bf16[2,2,256,128]{3,2,1,0:T(8,128)(2,1)S(1)} collective-permute-done((bf16[2,2,256,128]{3,2,1,0:T(8,128)(2,1)}, bf16[2,2,256,128]{3,2,1,0:T(8,128)(2,1)S(1)}, u32[]{:S(2)}, u32[]{:S(2)}) %collective-permute-start.13) | collective-permute-done | bytes 262176 | tf_op jit(solution)/shard_map/ppermute | solution.py:365
  192.2 0.7 copy-done.4
  192.9 7.7 %transform.5 = (bf16[2,2,256,128]{3,2,1,0:T(8,128)(2,1)}, bf16[2,2,256,128]{3,2,1,0:T(8,128)(2,1)}, bf16[2,2,256,128]{3,2,1,0:T(8,128)(2,1)}, bf16[2,2,256,128]{...) custom-call(s32[11]{0:T(128)S(1)} %get-tuple-element.102.meta_ref, ...), custom_call_target="tpu_custom_call" | custom-call | flops 2415919104 | bytes 9437184 | tf_op jit(solution)/shard_map/transform/pallas_call | solution.py:178
  200.7 4.5 %collective-permute-start.14 = (bf16[2,2,256,128]{3,2,1,0:T(8,128)(2,1)}, bf16[2,2,256,128]{3,2,1,0:T(8,128)(2,1)S(1)}, u32[]{:S(2)}, u32[]{:S(2)}) collective-permute-start(bf16[2,2,256,128]{3,2,1,0:T(8,128)(2,1)} %get-tuple-element.85), channel_id=1, source_target_pairs={{0,16},{16,32},{32,48},{48,0},{64,80},{80,96},{96,112},{112,64},{1... | collective-permute-start | bytes 786440 | tf_op jit(solution)/shard_map/ppermute | solution.py:365
  205.2 2.2 collective-permute-start.16
  207.3 1.1 collective-permute-start.17
  208.4 0.2 collective-permute-start.18
  208.6 8.4 %collective-permute-done.14.refs_1_ = bf16[2,2,256,128]{3,2,1,0:T(8,128)(2,1)S(1)} collective-permute-done((bf16[2,2,256,128]{3,2,1,0:T(8,128)(2,1)}, bf16[2,2,256,128]{3,2,1,0:T(8,128)(2,1)S(1)}, u32[]{:S(2)}, u32[]{:S(2)}) %collective-permute-start.14) | collective-permute-done | bytes 262176 | tf_op jit(solution)/shard_map/ppermute | solution.py:365
  217.1 5.3 %collective-permute-start.20 = (bf16[2,2,256,128]{3,2,1,0:T(8,128)(2,1)}, bf16[2,2,256,128]{3,2,1,0:T(8,128)(2,1)S(1)}, u32[]{:S(2)}, u32[]{:S(2)}) collective-permute-start(bf16[2,2,256,128]{3,2,1,0:T(8,128)(2,1)} %get-tuple-element.91), channel_id=1, source_target_pairs={{0,112},{16,64},{32,80},{48,96},{64,48},{80,0},{96,16},{112,32},{1... | collective-permute-start | bytes 786440 | tf_op jit(solution)/shard_map/ppermute | solution.py:365
  222.4 4.4 %settle.4.refs_11_ = bf16[8,8,256,128]{3,2,1,0:T(8,128)(2,1)} custom-call(s32[2]{0:T(128)S(1)} %pad_add_fusion.meta_ref, bf16[2,2,256,128]{3,2,1,0:T(8,128)(2,1)S(1)} %copy-done.1, bf16[2,2,256,128]{3,2,1,0:T(8,128)(2,1)S(1)} %collective-permute-done.7.refs_1_, ...), custom_call_target="tpu_custom_call", output_to_operand_aliasing={{}: (12, {})} | custom-call | flops 1073741824 | bytes 6291456 | tf_op jit(solution)/shard_map/settle/pallas_call | solution.py:259
  226.9 2.7 %collective-permute-done.17.refs_4_ = bf16[2,2,256,128]{3,2,1,0:T(8,128)(2,1)S(1)} collective-permute-done((bf16[2,2,256,128]{3,2,1,0:T(8,128)(2,1)}, bf16[2,2,256,128]{3,2,1,0:T(8,128)(2,1)S(1)}, u32[]{:S(2)}, u32[]{:S(2)}) %collective-permute-start.17) | collective-permute-done | bytes 262176 | tf_op jit(solution)/shard_map/ppermute | solution.py:365
  229.5 0.9 collective-permute-done.19.refs_6_
  230.5 1.2 collective-permute-done.20.refs_7_
  231.7 4.4 %settle.5 = bf16[8,8,256,128]{3,2,1,0:T(8,128)(2,1)} custom-call(s32[2]{0:T(128)S(1)} %pad_add_fusion.meta_ref, bf16[2,2,256,128]{3,2,1,0:T(8,128)(2,1)S(1)} %copy-done.6, bf16[2,2,256,128]{3,2,1,0:T(8,128)(2,1)S(1)} %collective-permute-done.14.refs_1_, ...), custom_call_target="tpu_custom_call", output_to_operand_aliasing={{}: (12, {})} | custom-call | flops 1073741824 | bytes 6291456 | tf_op jit(solution)/shard_map/settle/pallas_call | solution.py:259
  (47 shorter events, 0.1 us)
Async XLA Ops:
  93.7 8.1 %copy-start.22 = (s32[128]{0:T(128)S(1)}, s32[128]{0:T(128)}, u32[]{:S(2)}) copy-start(s32[128]{0:T(128)} %param.7) | copy-start | bytes 1540
  93.7 50.6 %all-to-all-start.1 = ((bf16[16,2,2,96,256]{4,3,2,1,0:T(8,128)(2,1)}), bf16[16,2,2,96,256]{4,3,2,1,0:T(8,128)(2,1)S(1)}, u32[]{:S(2)}, u32[]{:S(2)}) async-start(bf16[16,2,2,96,256]{4,3,2,1,0:T(8,128)(2,1)} %get-tuple-element.55), calls=%async_computation.1 | async-start | bytes 6291456 | tf_op jit(solution)/shard_map/all_to_all | solution.py:350
  115.6 13.8 %collective-permute-start = (bf16[4,256,128]{2,1,0:T(8,128)(2,1)}, bf16[4,256,128]{2,1,0:T(8,128)(2,1)S(1)}, u32[]{:S(2)}, u32[]{:S(2)}) collective-permute-start(bf16[4,256,128]{2,1,0:T(8,128)(2,1)} %get-tuple-element.58), channel_id=1, source_target_pairs={{0,16},{16,32},{32,48},{48,0},{64,80},{80,96},{96,112},{112,64},{1... | collective-permute-start | bytes 786440 | tf_op jit(solution)/shard_map/ppermute | solution.py:365
  117.3 12.9 %collective-permute-start.1 = (bf16[4,256,128]{2,1,0:T(8,128)(2,1)}, bf16[4,256,128]{2,1,0:T(8,128)(2,1)S(1)}, u32[]{:S(2)}, u32[]{:S(2)}) collective-permute-start(bf16[4,256,128]{2,1,0:T(8,128)(2,1)} %get-tuple-element.59), channel_id=1, source_target_pairs={{0,32},{16,48},{32,0},{48,16},{64,96},{80,112},{96,64},{112,80},{1... | collective-permute-start | bytes 786440 | tf_op jit(solution)/shard_map/ppermute | solution.py:365
  118.2 14.6 %collective-permute-start.2 = (bf16[4,256,128]{2,1,0:T(8,128)(2,1)}, bf16[4,256,128]{2,1,0:T(8,128)(2,1)S(1)}, u32[]{:S(2)}, u32[]{:S(2)}) collective-permute-start(bf16[4,256,128]{2,1,0:T(8,128)(2,1)} %get-tuple-element.60), channel_id=1, source_target_pairs={{0,48},{16,0},{32,16},{48,32},{64,112},{80,64},{96,80},{112,96},{1... | collective-permute-start | bytes 786440 | tf_op jit(solution)/shard_map/ppermute | solution.py:365
  120.6 12.9 %collective-permute-start.3 = (bf16[4,256,128]{2,1,0:T(8,128)(2,1)}, bf16[4,256,128]{2,1,0:T(8,128)(2,1)S(1)}, u32[]{:S(2)}, u32[]{:S(2)}) collective-permute-start(bf16[4,256,128]{2,1,0:T(8,128)(2,1)} %get-tuple-element.61), channel_id=1, source_target_pairs={{0,64},{16,80},{32,96},{48,112},{64,0},{80,16},{96,32},{112,48},{1... | collective-permute-start | bytes 786440 | tf_op jit(solution)/shard_map/ppermute | solution.py:365
  122.2 18.1 %collective-permute-start.4 = (bf16[4,256,128]{2,1,0:T(8,128)(2,1)}, bf16[4,256,128]{2,1,0:T(8,128)(2,1)S(1)}, u32[]{:S(2)}, u32[]{:S(2)}) collective-permute-start(bf16[4,256,128]{2,1,0:T(8,128)(2,1)} %get-tuple-element.62), channel_id=1, source_target_pairs={{0,80},{16,96},{32,112},{48,64},{64,16},{80,32},{96,48},{112,0},{1... | collective-permute-start | bytes 786440 | tf_op jit(solution)/shard_map/ppermute | solution.py:365
  129.4 0.7 copy-start.8
  130.1 12.1 %collective-permute-start.5 = (bf16[4,256,128]{2,1,0:T(8,128)(2,1)}, bf16[4,256,128]{2,1,0:T(8,128)(2,1)S(1)}, u32[]{:S(2)}, u32[]{:S(2)}) collective-permute-start(bf16[4,256,128]{2,1,0:T(8,128)(2,1)} %get-tuple-element.63), channel_id=1, source_target_pairs={{0,112},{16,64},{32,80},{48,96},{64,48},{80,0},{96,16},{112,32},{1... | collective-permute-start | bytes 786440 | tf_op jit(solution)/shard_map/ppermute | solution.py:365
  130.1 0.7 copy-start.10
  132.8 0.7 copy-start.12
  133.5 0.7 copy-start.14
  140.4 0.7 copy-start.16
  142.2 0.7 copy-start.18
  144.3 8.9 %copy-start.21 = (bf16[16,2,2,96,256]{4,3,2,1,0:T(8,128)(2,1)}, bf16[16,2,2,96,256]{4,3,2,1,0:T(8,128)(2,1)S(1)}, u32[]{:S(2)}) copy-start(bf16[16,2,2,96,256]{4,3,2,1,0:T(8,128)(2,1)S(1)} %all-to-all-done.1.got_ref) | copy-start | bytes 9437188
  144.3 48.7 %all-to-all-start.2 = ((bf16[16,2,2,96,256]{4,3,2,1,0:T(8,128)(2,1)}), bf16[16,2,2,96,256]{4,3,2,1,0:T(8,128)(2,1)}, u32[]{:S(2)}, u32[]{:S(2)}) async-start(bf16[16,2,2,96,256]{4,3,2,1,0:T(8,128)(2,1)} %get-tuple-element.65), calls=%async_computation.2 | async-start | bytes 6291456 | tf_op jit(solution)/shard_map/all_to_all | solution.py:350
  148.8 16.4 %collective-permute-start.6 = (bf16[4,256,128]{2,1,0:T(8,128)(2,1)}, bf16[4,256,128]{2,1,0:T(8,128)(2,1)S(1)}, u32[]{:S(2)}, u32[]{:S(2)}) collective-permute-start(bf16[4,256,128]{2,1,0:T(8,128)(2,1)} %get-tuple-element.66), channel_id=1, source_target_pairs={{0,96},{16,112},{32,64},{48,80},{64,32},{80,48},{96,0},{112,16},{1... | collective-permute-start | bytes 786440 | tf_op jit(solution)/shard_map/ppermute | solution.py:365
  153.2 24.3 %copy-start = (bf16[4,4,256,256]{3,2,1,0:T(8,128)(2,1)S(1)}, bf16[4,4,256,256]{3,2,1,0:T(8,128)(2,1)}, u32[]{:S(2)}) copy-start(bf16[4,4,256,256]{3,2,1,0:T(8,128)(2,1)} %refs_10_.5) | copy-start | bytes 6291460
  153.2 24.3 %copy-start.7 = (bf16[4,256,128]{2,1,0:T(8,128)(2,1)S(1)}, bf16[4,256,128]{2,1,0:T(8,128)(2,1)}, u32[]{:S(2)}) copy-start(bf16[4,256,128]{2,1,0:T(8,128)(2,1)} %get-tuple-element.76.refs_0_) | copy-start | bytes 786436
  153.2 24.3 %copy-start.9 = (bf16[4,256,128]{2,1,0:T(8,128)(2,1)S(1)}, bf16[4,256,128]{2,1,0:T(8,128)(2,1)}, u32[]{:S(2)}) copy-start(bf16[4,256,128]{2,1,0:T(8,128)(2,1)} %copy-done.8) | copy-start | bytes 786436
  153.2 24.3 %copy-start.11 = (bf16[4,256,128]{2,1,0:T(8,128)(2,1)S(1)}, bf16[4,256,128]{2,1,0:T(8,128)(2,1)}, u32[]{:S(2)}) copy-start(bf16[4,256,128]{2,1,0:T(8,128)(2,1)} %copy-done.10) | copy-start | bytes 786436
  153.2 24.3 %copy-start.13 = (bf16[4,256,128]{2,1,0:T(8,128)(2,1)S(1)}, bf16[4,256,128]{2,1,0:T(8,128)(2,1)}, u32[]{:S(2)}) copy-start(bf16[4,256,128]{2,1,0:T(8,128)(2,1)} %copy-done.12) | copy-start | bytes 786436
  153.2 24.3 %copy-start.15 = (bf16[4,256,128]{2,1,0:T(8,128)(2,1)S(1)}, bf16[4,256,128]{2,1,0:T(8,128)(2,1)}, u32[]{:S(2)}) copy-start(bf16[4,256,128]{2,1,0:T(8,128)(2,1)} %copy-done.14) | copy-start | bytes 786436
  153.2 24.3 %copy-start.17 = (bf16[4,256,128]{2,1,0:T(8,128)(2,1)S(1)}, bf16[4,256,128]{2,1,0:T(8,128)(2,1)}, u32[]{:S(2)}) copy-start(bf16[4,256,128]{2,1,0:T(8,128)(2,1)} %copy-done.16) | copy-start | bytes 786436
  153.3 24.3 %copy-start.19 = (bf16[4,256,128]{2,1,0:T(8,128)(2,1)S(1)}, bf16[4,256,128]{2,1,0:T(8,128)(2,1)}, u32[]{:S(2)}) copy-start(bf16[4,256,128]{2,1,0:T(8,128)(2,1)} %copy-done.18) | copy-start | bytes 786436
  153.3 24.3 %copy-start.20 = (s32[8,128]{1,0:T(8,128)S(1)}, s32[8,128]{1,0:T(8,128)}, u32[]{:S(2)}) copy-start(s32[8,128]{1,0:T(8,128)} %refs_9_.5) | copy-start | bytes 12292
  161.3 9.4 %collective-permute-start.7 = (bf16[2,2,256,128]{3,2,1,0:T(8,128)(2,1)}, bf16[2,2,256,128]{3,2,1,0:T(8,128)(2,1)S(1)}, u32[]{:S(2)}, u32[]{:S(2)}) collective-permute-start(bf16[2,2,256,128]{3,2,1,0:T(8,128)(2,1)} %get-tuple-element.69), channel_id=1, source_target_pairs={{0,16},{16,32},{32,48},{48,0},{64,80},{80,96},{96,112},{112,64},{1... | collective-permute-start | bytes 786440 | tf_op jit(solution)/shard_map/ppermute | solution.py:365
  161.3 14.4 %collective-permute-start.8 = (bf16[2,2,256,128]{3,2,1,0:T(8,128)(2,1)}, bf16[2,2,256,128]{3,2,1,0:T(8,128)(2,1)S(1)}, u32[]{:S(2)}, u32[]{:S(2)}) collective-permute-start(bf16[2,2,256,128]{3,2,1,0:T(8,128)(2,1)} %get-tuple-element.70), channel_id=1, source_target_pairs={{0,32},{16,48},{32,0},{48,16},{64,96},{80,112},{96,64},{112,80},{1... | collective-permute-start | bytes 786440 | tf_op jit(solution)/shard_map/ppermute | solution.py:365
  164.8 19.1 %collective-permute-start.9 = (bf16[2,2,256,128]{3,2,1,0:T(8,128)(2,1)}, bf16[2,2,256,128]{3,2,1,0:T(8,128)(2,1)S(1)}, u32[]{:S(2)}, u32[]{:S(2)}) collective-permute-start(bf16[2,2,256,128]{3,2,1,0:T(8,128)(2,1)} %get-tuple-element.71), channel_id=1, source_target_pairs={{0,48},{16,0},{32,16},{48,32},{64,112},{80,64},{96,80},{112,96},{1... | collective-permute-start | bytes 786440 | tf_op jit(solution)/shard_map/ppermute | solution.py:365
  165.2 18.7 %collective-permute-start.10 = (bf16[2,2,256,128]{3,2,1,0:T(8,128)(2,1)}, bf16[2,2,256,128]{3,2,1,0:T(8,128)(2,1)S(1)}, u32[]{:S(2)}, u32[]{:S(2)}) collective-permute-start(bf16[2,2,256,128]{3,2,1,0:T(8,128)(2,1)} %get-tuple-element.72), channel_id=1, source_target_pairs={{0,64},{16,80},{32,96},{48,112},{64,0},{80,16},{96,32},{112,48},{1... | collective-permute-start | bytes 786440 | tf_op jit(solution)/shard_map/ppermute | solution.py:365
  165.2 22.9 %collective-permute-start.11 = (bf16[2,2,256,128]{3,2,1,0:T(8,128)(2,1)}, bf16[2,2,256,128]{3,2,1,0:T(8,128)(2,1)S(1)}, u32[]{:S(2)}, u32[]{:S(2)}) collective-permute-start(bf16[2,2,256,128]{3,2,1,0:T(8,128)(2,1)} %get-tuple-element.73), channel_id=1, source_target_pairs={{0,80},{16,96},{32,112},{48,64},{64,16},{80,32},{96,48},{112,0},{1... | collective-permute-start | bytes 786440 | tf_op jit(solution)/shard_map/ppermute | solution.py:365
  170.7 18.2 %collective-permute-start.12 = (bf16[2,2,256,128]{3,2,1,0:T(8,128)(2,1)}, bf16[2,2,256,128]{3,2,1,0:T(8,128)(2,1)S(1)}, u32[]{:S(2)}, u32[]{:S(2)}) collective-permute-start(bf16[2,2,256,128]{3,2,1,0:T(8,128)(2,1)} %get-tuple-element.74), channel_id=1, source_target_pairs={{0,96},{16,112},{32,64},{48,80},{64,32},{80,48},{96,0},{112,16},{1... | collective-permute-start | bytes 786440 | tf_op jit(solution)/shard_map/ppermute | solution.py:365
  175.7 16.5 %collective-permute-start.13 = (bf16[2,2,256,128]{3,2,1,0:T(8,128)(2,1)}, bf16[2,2,256,128]{3,2,1,0:T(8,128)(2,1)S(1)}, u32[]{:S(2)}, u32[]{:S(2)}) collective-permute-start(bf16[2,2,256,128]{3,2,1,0:T(8,128)(2,1)} %get-tuple-element.75), channel_id=1, source_target_pairs={{0,112},{16,64},{32,80},{48,96},{64,48},{80,0},{96,16},{112,32},{1... | collective-permute-start | bytes 786440 | tf_op jit(solution)/shard_map/ppermute | solution.py:365
  188.9 0.7 copy-start.2
  192.2 0.7 copy-start.4
  192.9 29.5 %copy-start.1 = (bf16[2,2,256,128]{3,2,1,0:T(8,128)(2,1)S(1)}, bf16[2,2,256,128]{3,2,1,0:T(8,128)(2,1)}, u32[]{:S(2)}) copy-start(bf16[2,2,256,128]{3,2,1,0:T(8,128)(2,1)} %get-tuple-element.92.refs_0_) | copy-start | bytes 786436
  192.9 29.5 %copy-start.3 = (bf16[2,2,256,128]{3,2,1,0:T(8,128)(2,1)S(1)}, bf16[2,2,256,128]{3,2,1,0:T(8,128)(2,1)}, u32[]{:S(2)}) copy-start(bf16[2,2,256,128]{3,2,1,0:T(8,128)(2,1)} %copy-done.2) | copy-start | bytes 786436
  192.9 29.5 %copy-start.5 = (bf16[2,2,256,128]{3,2,1,0:T(8,128)(2,1)S(1)}, bf16[2,2,256,128]{3,2,1,0:T(8,128)(2,1)}, u32[]{:S(2)}) copy-start(bf16[2,2,256,128]{3,2,1,0:T(8,128)(2,1)} %copy-done.4) | copy-start | bytes 786436
  200.7 16.4 %collective-permute-start.14 = (bf16[2,2,256,128]{3,2,1,0:T(8,128)(2,1)}, bf16[2,2,256,128]{3,2,1,0:T(8,128)(2,1)S(1)}, u32[]{:S(2)}, u32[]{:S(2)}) collective-permute-start(bf16[2,2,256,128]{3,2,1,0:T(8,128)(2,1)} %get-tuple-element.85), channel_id=1, source_target_pairs={{0,16},{16,32},{32,48},{48,0},{64,80},{80,96},{96,112},{112,64},{1... | collective-permute-start | bytes 786440 | tf_op jit(solution)/shard_map/ppermute | solution.py:365
  205.1 11.9 %collective-permute-start.15 = (bf16[2,2,256,128]{3,2,1,0:T(8,128)(2,1)}, bf16[2,2,256,128]{3,2,1,0:T(8,128)(2,1)S(1)}, u32[]{:S(2)}, u32[]{:S(2)}) collective-permute-start(bf16[2,2,256,128]{3,2,1,0:T(8,128)(2,1)} %get-tuple-element.86), channel_id=1, source_target_pairs={{0,32},{16,48},{32,0},{48,16},{64,96},{80,112},{96,64},{112,80},{1... | collective-permute-start | bytes 786440 | tf_op jit(solution)/shard_map/ppermute | solution.py:365
  205.2 21.7 %collective-permute-start.16 = (bf16[2,2,256,128]{3,2,1,0:T(8,128)(2,1)}, bf16[2,2,256,128]{3,2,1,0:T(8,128)(2,1)S(1)}, u32[]{:S(2)}, u32[]{:S(2)}) collective-permute-start(bf16[2,2,256,128]{3,2,1,0:T(8,128)(2,1)} %get-tuple-element.87), channel_id=1, source_target_pairs={{0,48},{16,0},{32,16},{48,32},{64,112},{80,64},{96,80},{112,96},{1... | collective-permute-start | bytes 786440 | tf_op jit(solution)/shard_map/ppermute | solution.py:365
  207.3 22.2 %collective-permute-start.17 = (bf16[2,2,256,128]{3,2,1,0:T(8,128)(2,1)}, bf16[2,2,256,128]{3,2,1,0:T(8,128)(2,1)S(1)}, u32[]{:S(2)}, u32[]{:S(2)}) collective-permute-start(bf16[2,2,256,128]{3,2,1,0:T(8,128)(2,1)} %get-tuple-element.88), channel_id=1, source_target_pairs={{0,64},{16,80},{32,96},{48,112},{64,0},{80,16},{96,32},{112,48},{1... | collective-permute-start | bytes 786440 | tf_op jit(solution)/shard_map/ppermute | solution.py:365
  208.4 21.1 %collective-permute-start.18 = (bf16[2,2,256,128]{3,2,1,0:T(8,128)(2,1)}, bf16[2,2,256,128]{3,2,1,0:T(8,128)(2,1)S(1)}, u32[]{:S(2)}, u32[]{:S(2)}) collective-permute-start(bf16[2,2,256,128]{3,2,1,0:T(8,128)(2,1)} %get-tuple-element.89), channel_id=1, source_target_pairs={{0,80},{16,96},{32,112},{48,64},{64,16},{80,32},{96,48},{112,0},{1... | collective-permute-start | bytes 786440 | tf_op jit(solution)/shard_map/ppermute | solution.py:365
  217.1 13.4 %collective-permute-start.19 = (bf16[2,2,256,128]{3,2,1,0:T(8,128)(2,1)}, bf16[2,2,256,128]{3,2,1,0:T(8,128)(2,1)S(1)}, u32[]{:S(2)}, u32[]{:S(2)}) collective-permute-start(bf16[2,2,256,128]{3,2,1,0:T(8,128)(2,1)} %get-tuple-element.90), channel_id=1, source_target_pairs={{0,96},{16,112},{32,64},{48,80},{64,32},{80,48},{96,0},{112,16},{1... | collective-permute-start | bytes 786440 | tf_op jit(solution)/shard_map/ppermute | solution.py:365
  217.1 14.6 %copy-start.6 = (bf16[2,2,256,128]{3,2,1,0:T(8,128)(2,1)S(1)}, bf16[2,2,256,128]{3,2,1,0:T(8,128)(2,1)}, u32[]{:S(2)}) copy-start(bf16[2,2,256,128]{3,2,1,0:T(8,128)(2,1)} %get-tuple-element.84.refs_0_) | copy-start | bytes 786436
  217.1 14.6 %collective-permute-start.20 = (bf16[2,2,256,128]{3,2,1,0:T(8,128)(2,1)}, bf16[2,2,256,128]{3,2,1,0:T(8,128)(2,1)S(1)}, u32[]{:S(2)}, u32[]{:S(2)}) collective-permute-start(bf16[2,2,256,128]{3,2,1,0:T(8,128)(2,1)} %get-tuple-element.91), channel_id=1, source_target_pairs={{0,112},{16,64},{32,80},{48,96},{64,48},{80,0},{96,16},{112,32},{1... | collective-permute-start | bytes 786440 | tf_op jit(solution)/shard_map/ppermute | solution.py:365

commit v5 on v4

--- a/solution.py
+++ b/solution.py
@@ -10,7 +10,8 @@
 ZS, Y = 2, 4
 CHUNKS = (4, 2, 2)
 FLIPPED = (False, True, True)
-TIES = {2: ((0, (0, 1, 2, 3, 4, 5, 7)),), 3: ((0, (6,)), (1, range(8)))}
+TIES = {2: ((0, (0, 1, 2, 3, 4, 5, 7)),), 3: ((0, (6,)), (1, range(8)), (2, range(8)))}
+UNITS = ((0, 0, 4), (1, 0, 1), (1, 1, 1), (2, 0, 1), (2, 1, 1))
 ORDER = (6, 2, 5, 7, 1, 3, 4)
 STEP = 16
 BF16, F32 = jnp.bfloat16, jnp.float32
@@ -150,14 +151,14 @@
         spread(full, (0,), meta_ref, outs)
 
 
-def transform(got, legendre, meta, first, flipped, by_hop):
-    srcs, count, _, lats, rows = got.shape
+def transform(got, legendre, meta, first, offset, count, flipped):
+    srcs, _, _, lats, rows = got.shape
     degrees = legendre.shape[2]
     if flipped:
         kernel = transform_kernel
         depth, width = srcs // 2 * lats, degrees
         got_spec = pl.BlockSpec(
-            (srcs // 2, 1, 2, lats, rows), lambda s, t, m: (t ^ m[0], s, 0, 0, 0)
+            (srcs // 2, 1, 2, lats, rows), lambda s, t, m: (t ^ m[0], offset + s, 0, 0, 0)
         )
         table_spec = pl.BlockSpec((1, depth, width), lambda s, t, m: (first + s, t ^ m[0], 0))
         shape, block = (2, count, rows, 128), (1, 1, rows, 128)
@@ -165,16 +166,12 @@
     else:
         kernel = transform_whole_kernel
         depth, width = srcs * lats, degrees // 2
-        got_spec = pl.BlockSpec((srcs, 1, 2, lats, rows), lambda s, t, m: (0, s, 0, 0, 0))
+        got_spec = pl.BlockSpec((srcs, 1, 2, lats, rows), lambda s, t, m: (0, offset + s, 0, 0, 0))
         table_spec = pl.BlockSpec((1, depth, width), lambda s, t, m: (first + s, 0, t))
         shape, block = (count, rows, 128), (1, rows, 128)
         where = lambda s, t, m: (s, 0, 0)
-    if by_hop:
-        out_specs = [pl.BlockSpec(block, where)] * 8
-        out_shape = [pltpu.HBM(shape, BF16)] * 8
-    else:
-        out_specs = pl.BlockSpec((8,) + block, lambda s, t, m: (0, *where(s, t, m)))
-        out_shape = pltpu.HBM((8,) + shape, BF16)
+    out_specs = [pl.BlockSpec(block, where)] * 8
+    out_shape = [pltpu.HBM(shape, BF16)] * 8
     return pl.pallas_call(
         kernel,
         grid_spec=pltpu.PrefetchScalarGridSpec(
@@ -311,17 +308,17 @@
 
     out, gots, moves = None, [], []
 
-    final = len(starts) - 1
-
-    def put(k):
+    def put(u):
+        chunk, offset, count = UNITS[u]
         return settle(
-            moves[k],
+            moves[u],
             spectral_state,
             inverses,
             block_index,
             place,
-            *starts[k],
-            FLIPPED[k],
+            starts[chunk][0] + offset,
+            count,
+            FLIPPED[chunk],
             out,
         )
 
@@ -329,9 +326,9 @@
         keep = {}
         if k > 0:
             keep["got", k - 1] = gots[k - 1]
-        for chunk, hops_of in TIES.get(k, ()):
+        for unit, hops_of in TIES.get(k, ()):
             for h in hops_of:
-                keep["move", chunk, h] = moves[chunk][h]
+                keep["move", unit, h] = moves[unit][h]
         if k > 2:
             keep["out"] = out
         if k < len(starts):
@@ -353,22 +350,30 @@
                 )
             else:
                 gots.append(lax.all_to_all(send, "lat", 0, 0, tiled=True))
-        if k > 0:
-            first, n = starts[k - 1]
-            meta = jnp.concatenate([(lat // 8)[None], blocks, lengths[first : first + n]])
-            meta = meta.astype(jnp.int32)
-            by_hop = True
-            parts = transform(gots[k - 1], legendre, meta, first, FLIPPED[k - 1], by_hop)
-            if by_hop:
+        for chunk, offset, count in UNITS:
+            if chunk == k - 1:
+                first = starts[chunk][0] + offset
+                meta = jnp.concatenate([(lat // 8)[None], blocks, lengths[first : first + count]])
+                parts = transform(
+                    gots[chunk],
+                    legendre,
+                    meta.astype(jnp.int32),
+                    first,
+                    offset,
+                    count,
+                    FLIPPED[chunk],
+                )
                 moved = {0: parts[0]}
                 for h in ORDER:
                     moved[h] = lax.ppermute(parts[h], "rad", rad_targets(h // Y, h % Y))
                 moves.append([moved[h] for h in range(8)])
-            else:
-                moves.append([lax.all_to_all(parts, "rad", 0, 0, tiled=True)])
-        if k > 1:
-            out = put(k - 2)
-    return put(final)
+        for u, (chunk, _, _) in enumerate(UNITS):
+            if chunk == k - 2:
+                out = put(u)
+    for u, (chunk, _, _) in enumerate(UNITS):
+        if chunk == len(starts) - 1:
+            out = put(u)
+    return out
 
 
 def solution(mesh):

time: 241 us -> 253 us (1.050); the launches traced: 236 us -> 252 us
  starting transfers between devices: 50.3 us -> 74.1 us
  waiting for transfers between devices: 41.1 us -> 21.6 us
  Pallas kernels: 60.5 us -> 69.2 us
  other arithmetic: 1.17 us -> 3.74 us
    ppermute x21 -> x35, starting transfers between devices: 37.9 us -> 61 us  [on_device(): moved[h] = lax.ppermute(parts[h], 'rad', rad_targets(h // Y, h % Y))]
    ppermute x21 -> x35, waiting for transfers between devices: 39.8 us -> 20.2 us  [on_device(): moved[h] = lax.ppermute(parts[h], 'rad', rad_targets(h // Y, h % Y))]
    pallas_call x3 -> x5, Pallas kernels: 15.2 us -> 19.7 us  [settle(): pl.pallas_call(functools.partial(kernel, first, flipped), grid_spec=pltpu...]
    pallas_call x3 -> x5, Pallas kernels: 29.4 us -> 33.5 us  [transform(): pl.pallas_call(kernel, grid_spec=pltpu.PrefetchScalarGridSpec(num_scalar_...]
    concatenate x2 -> x3, other arithmetic: 0.16 us -> 2.72 us  [on_device(): jnp.concatenate([(lat // 8)[None], blocks, lengths[first:first + count]])]
    unnamed x46 -> x84, local copies, waits for them, and re-layouts: 5.71 us -> 5.41 us
  transfers between devices with their start and end apart: 23 -> 37, of which waited for: 13 -> 6; matrix products, arithmetic and copies ran while one was open for 0% -> 1% of each run, Pallas kernels for 14% -> 18%
where the time goes in v5:
time: 253 us; the launch traced here: 252 us
  blocking collectives  76.8 us (30%)
  starting transfers between devices  74.1 us (29%)
  Pallas kernels  69.2 us (27%)
  waiting for transfers between devices  21.6 us (9%)
  local copies, waits for them, and re-layouts  6.21 us (2%)
  other arithmetic  3.74 us (1%)
    all_to_all x1, blocking collectives, on_device(): gots.append(lax.all_to_all(send, 'lat', 0, 0, tiled=True))  76.8 us
    ppermute x35, starting transfers between devices, on_device(): moved[h] = lax.ppermute(parts[h], 'rad', rad_targets(h // Y, h % Y))  61 us
    pallas_call x5, Pallas kernels, transform(): pl.pallas_call(kernel, grid_spec=pltpu.PrefetchScalarGridSpec(num_scalar_...  33.5 us
    ppermute x35, waiting for transfers between devices, on_device(): moved[h] = lax.ppermute(parts[h], 'rad', rad_targets(h // Y, h % Y))  20.2 us
    pallas_call x5, Pallas kernels, settle(): pl.pallas_call(functools.partial(kernel, first, flipped), grid_spec=pltpu...  19.7 us
    pallas_call x1, Pallas kernels, prep(): pl.pallas_call(functools.partial(prep_kernel, starts, per_dev), grid=(lat...  15.9 us
    all_to_all x2, starting transfers between devices, on_device(): lax.all_to_all(send, ('rad', 'lat'), 0, 0, tiled=True, axis_index_groups=...  13.1 us
    unnamed x84, local copies, waits for them, and re-layouts  5.41 us
  transfers between devices with their start and end apart: 37, of which 6 were waited for; matrix products, arithmetic and copies ran while one was open for 1% of the time, Pallas kernels for 18%

profile of v5, /device:TPU:74, one launch (start us, length us, event | category | flops | bytes accessed | tf_op | source)
XLA Modules:
  0.0 252.0 jit_solution(10541765173864073175)
XLA Ops:
  0.0 0.7 broadcast_multiply_fusion
  0.7 0.1 iota_add_fusion
  0.7 0.1 add.69.key_ref
  0.9 15.9 %prep.1 = (bf16[16,4,2,96,256]{4,3,2,1,0:T(8,128)(2,1)}, bf16[16,2,2,96,256]{4,3,2,1,0:T(8,128)(2,1)}, bf16[16,2,2,96,256]{4,3,2,1,0:T(8,128)(2,1)}) custom-call(s32[1,256]{1,0:T(1,128)S(1)} %add.69.key_ref, bf16[256,96,256]{2,1,0:T(8,128)(2,1)} %bitcast.8), custom_call_target="tpu_custom_call" | custom-call | flops 9663676416 | bytes 25165824 | tf_op jit(solution)/shard_map/prep/pallas_call | solution.py:73
  16.8 76.8 %all_to_all.15.got_ref = bf16[16,4,2,96,256]{4,3,2,1,0:T(8,128)(2,1)} all-to-all(bf16[16,4,2,96,256]{4,3,2,1,0:T(8,128)(2,1)} %get-tuple-element.77), channel_id=1, replica_groups=mesh['rad'=8,'lat'=16] {'lat'}, dimensions={0} | all-to-all | bytes 12582912 | tf_op jit(solution)/shard_map/all_to_all | solution.py:352
  93.7 8.7 %all-to-all-start.1 = ((bf16[16,2,2,96,256]{4,3,2,1,0:T(8,128)(2,1)}), bf16[16,2,2,96,256]{4,3,2,1,0:T(8,128)(2,1)}, u32[]{:S(2)}, u32[]{:S(2)}) async-start(bf16[16,2,2,96,256]{4,3,2,1,0:T(8,128)(2,1)} %get-tuple-element.79), calls=%async_computation.1 | async-start | bytes 6291456 | tf_op jit(solution)/shard_map/all_to_all | solution.py:347
  102.4 0.2 select_reduce_fusion
  102.6 0.1 pad_add_fusion.3.meta_ref
  102.7 13.7 %transform.5 = (bf16[4,256,128]{2,1,0:T(8,128)(2,1)}, bf16[4,256,128]{2,1,0:T(8,128)(2,1)}, bf16[4,256,128]{2,1,0:T(8,128)(2,1)}, bf16[4,256,128]{2,1,0:T(8,128)...) custom-call(s32[13]{0:T(128)S(1)} %pad_add_fusion.3.meta_ref, ...), custom_call_target="tpu_custom_call" | custom-call | flops 4831838208 | bytes 18874368 | tf_op jit(solution)/shard_map/transform/pallas_call | solution.py:175
  116.3 1.6 collective-permute-start
  118.0 0.9 collective-permute-start.1
  118.9 2.4 collective-permute-start.2
  121.3 1.6 collective-permute-start.3
  122.9 7.2 %collective-permute-done.refs_1_ = bf16[4,256,128]{2,1,0:T(8,128)(2,1)S(1)} collective-permute-done((bf16[4,256,128]{2,1,0:T(8,128)(2,1)}, bf16[4,256,128]{2,1,0:T(8,128)(2,1)S(1)}, u32[]{:S(2)}, u32[]{:S(2)}) %collective-permute-start) | collective-permute-done | bytes 262176 | tf_op jit(solution)/shard_map/ppermute | solution.py:368
  130.2 3.4 %collective-permute-done.2.refs_3_ = bf16[4,256,128]{2,1,0:T(8,128)(2,1)S(1)} collective-permute-done((bf16[4,256,128]{2,1,0:T(8,128)(2,1)}, bf16[4,256,128]{2,1,0:T(8,128)(2,1)S(1)}, u32[]{:S(2)}, u32[]{:S(2)}) %collective-permute-start.2) | collective-permute-done | bytes 262176 | tf_op jit(solution)/shard_map/ppermute | solution.py:368
  133.5 7.6 %collective-permute-done.4.refs_5_ = bf16[4,256,128]{2,1,0:T(8,128)(2,1)S(1)} collective-permute-done((bf16[4,256,128]{2,1,0:T(8,128)(2,1)}, bf16[4,256,128]{2,1,0:T(8,128)(2,1)S(1)}, u32[]{:S(2)}, u32[]{:S(2)}) %collective-permute-start.4) | collective-permute-done | bytes 262176 | tf_op jit(solution)/shard_map/ppermute | solution.py:368
  141.1 1.8 collective-permute-done.5.refs_7_
  142.9 0.7 copy-done.2
  143.6 1.4 all-to-all-done.1.got_ref
  145.1 4.4 %all-to-all-start.2 = ((bf16[16,2,2,96,256]{4,3,2,1,0:T(8,128)(2,1)}), bf16[16,2,2,96,256]{4,3,2,1,0:T(8,128)(2,1)}, u32[]{:S(2)}, u32[]{:S(2)}) async-start(bf16[16,2,2,96,256]{4,3,2,1,0:T(8,128)(2,1)} %get-tuple-element.89), calls=%async_computation.2 | async-start | bytes 6291456 | tf_op jit(solution)/shard_map/all_to_all | solution.py:347
  149.5 0.7 fusion.4
  150.1 0.7 pad_add_fusion.6
  150.8 4.4 %collective-permute-start.6 = (bf16[4,256,128]{2,1,0:T(8,128)(2,1)}, bf16[4,256,128]{2,1,0:T(8,128)(2,1)S(1)}, u32[]{:S(2)}, u32[]{:S(2)}) collective-permute-start(bf16[4,256,128]{2,1,0:T(8,128)(2,1)} %get-tuple-element.90), channel_id=1, source_target_pairs={{0,96},{16,112},{32,64},{48,80},{64,32},{80,48},{96,0},{112,16},{1... | collective-permute-start | bytes 786440 | tf_op jit(solution)/shard_map/ppermute | solution.py:368
  155.2 1.9 pad_add_fusion.5
  157.1 4.8 %transform.7 = (bf16[2,1,256,128]{3,2,1,0:T(8,128)(2,1)}, bf16[2,1,256,128]{3,2,1,0:T(8,128)(2,1)}, bf16[2,1,256,128]{3,2,1,0:T(8,128)(2,1)}, bf16[2,1,256,128]{...) custom-call(s32[10]{0:T(128)S(1)} %get-tuple-element.151.meta_ref, ...), custom_call_target="tpu_custom_call" | custom-call | flops 1207959552 | bytes 4718592 | tf_op jit(solution)/shard_map/transform/pallas_call | solution.py:175
  162.0 3.4 %collective-permute-start.15 = (bf16[2,1,256,128]{3,2,1,0:T(8,128)(2,1)}, bf16[2,1,256,128]{3,2,1,0:T(8,128)(2,1)S(1)}, u32[]{:S(2)}, u32[]{:S(2)}) collective-permute-start(bf16[2,1,256,128]{3,2,1,0:T(8,128)(2,1)} %get-tuple-element.102), channel_id=1, source_target_pairs={{0,32},{16,48},{32,0},{48,16},{64,96},{80,112},{96,64},{112,80},{1... | collective-permute-start | bytes 393224 | tf_op jit(solution)/shard_map/ppermute | solution.py:368
  165.4 0.5 collective-permute-start.16
  166.0 5.2 %transform.6 = (bf16[2,1,256,128]{3,2,1,0:T(8,128)(2,1)}, bf16[2,1,256,128]{3,2,1,0:T(8,128)(2,1)}, bf16[2,1,256,128]{3,2,1,0:T(8,128)(2,1)}, bf16[2,1,256,128]{...) custom-call(s32[10]{0:T(128)S(1)} %get-tuple-element.152.meta_ref, ...), custom_call_target="tpu_custom_call" | custom-call | flops 1207959552 | bytes 4718592 | tf_op jit(solution)/shard_map/transform/pallas_call | solution.py:175
  171.2 3.1 %collective-permute-start.18 = (bf16[2,1,256,128]{3,2,1,0:T(8,128)(2,1)S(1)}, bf16[2,1,256,128]{3,2,1,0:T(8,128)(2,1)S(1)}, u32[]{:S(2)}, u32[]{:S(2)}) collective-permute-start(bf16[2,1,256,128]{3,2,1,0:T(8,128)(2,1)S(1)} %copy-done.39), channel_id=1, source_target_pairs={{0,80},{16,96},{32,112},{48,64},{64,16},{80,32},{96,48},{112,0},{1... | collective-permute-start | bytes 393224 | tf_op jit(solution)/shard_map/ppermute | solution.py:368
  174.3 0.8 collective-permute-start.19
  175.2 2.3 collective-permute-start.20
  177.4 0.6 copy-done.7
  178.1 1.3 collective-permute-start.7
  179.4 3.3 %collective-permute-start.8 = (bf16[2,1,256,128]{3,2,1,0:T(8,128)(2,1)}, bf16[2,1,256,128]{3,2,1,0:T(8,128)(2,1)S(1)}, u32[]{:S(2)}, u32[]{:S(2)}) collective-permute-start(bf16[2,1,256,128]{3,2,1,0:T(8,128)(2,1)} %get-tuple-element.94), channel_id=1, source_target_pairs={{0,32},{16,48},{32,0},{48,16},{64,96},{80,112},{96,64},{112,80},{1... | collective-permute-start | bytes 393224 | tf_op jit(solution)/shard_map/ppermute | solution.py:368
  182.8 0.1 collective-permute-done.19.refs_6_
  182.9 3.6 %collective-permute-start.10 = (bf16[2,1,256,128]{3,2,1,0:T(8,128)(2,1)}, bf16[2,1,256,128]{3,2,1,0:T(8,128)(2,1)S(1)}, u32[]{:S(2)}, u32[]{:S(2)}) collective-permute-start(bf16[2,1,256,128]{3,2,1,0:T(8,128)(2,1)} %get-tuple-element.96), channel_id=1, source_target_pairs={{0,64},{16,80},{32,96},{48,112},{64,0},{80,16},{96,32},{112,48},{1... | collective-permute-start | bytes 393224 | tf_op jit(solution)/shard_map/ppermute | solution.py:368
  186.5 0.7 copy-done.18
  187.2 3.2 %collective-permute-start.12 = (bf16[2,1,256,128]{3,2,1,0:T(8,128)(2,1)}, bf16[2,1,256,128]{3,2,1,0:T(8,128)(2,1)S(1)}, u32[]{:S(2)}, u32[]{:S(2)}) collective-permute-start(bf16[2,1,256,128]{3,2,1,0:T(8,128)(2,1)} %get-tuple-element.98), channel_id=1, source_target_pairs={{0,96},{16,112},{32,64},{48,80},{64,32},{80,48},{96,0},{112,16},{1... | collective-permute-start | bytes 393224 | tf_op jit(solution)/shard_map/ppermute | solution.py:368
  190.4 1.4 collective-permute-start.13
  191.9 6.4 %settle.5.refs_11_ = bf16[8,8,256,128]{3,2,1,0:T(8,128)(2,1)} custom-call(s32[2]{0:T(128)S(1)} %pad_add_fusion.meta_ref, bf16[4,256,128]{2,1,0:T(8,128)(2,1)S(1)} %copy-done.1, bf16[4,256,128]{2,1,0:T(8,128)(2,1)S(1)} %collective-permute-done.refs_1_, bf16[4,256,128]{2,1,0:T(8,128)(2,1)S(1)} %collective-permute-done.1.refs_2_, ...), custom_call_target="tpu_custom_call" | custom-call | flops 2147483648 | bytes 10485760 | tf_op jit(solution)/shard_map/settle/pallas_call | solution.py:256
  198.3 0.6 copy-done.22
  198.9 0.6 copy-done.24
  199.6 0.6 copy-done.26
  200.2 0.7 copy-done.28
  200.9 0.7 copy-done.30
  201.5 4.9 %transform.9 = (bf16[2,1,256,128]{3,2,1,0:T(8,128)(2,1)}, bf16[2,1,256,128]{3,2,1,0:T(8,128)(2,1)}, bf16[2,1,256,128]{3,2,1,0:T(8,128)(2,1)}, bf16[2,1,256,128]{...) custom-call(s32[10]{0:T(128)S(1)} %get-tuple-element.149.meta_ref, ...), custom_call_target="tpu_custom_call" | custom-call | flops 1207959552 | bytes 4718592 | tf_op jit(solution)/shard_map/transform/pallas_call | solution.py:175
  206.4 0.2 collective-permute-start.28
  206.6 2.9 %collective-permute-start.29 = (bf16[2,1,256,128]{3,2,1,0:T(8,128)(2,1)}, bf16[2,1,256,128]{3,2,1,0:T(8,128)(2,1)S(1)}, u32[]{:S(2)}, u32[]{:S(2)}) collective-permute-start(bf16[2,1,256,128]{3,2,1,0:T(8,128)(2,1)} %get-tuple-element.126), channel_id=1, source_target_pairs={{0,32},{16,48},{32,0},{48,16},{64,96},{80,112},{96,64},{112,80},{1... | collective-permute-start | bytes 393224 | tf_op jit(solution)/shard_map/ppermute | solution.py:368
  209.5 2.0 collective-permute-start.30
  211.5 0.2 collective-permute-start.31
  211.9 4.9 %transform.8 = (bf16[2,1,256,128]{3,2,1,0:T(8,128)(2,1)}, bf16[2,1,256,128]{3,2,1,0:T(8,128)(2,1)}, bf16[2,1,256,128]{3,2,1,0:T(8,128)(2,1)}, bf16[2,1,256,128]{...) custom-call(s32[10]{0:T(128)S(1)} %get-tuple-element.153.meta_ref, ...), custom_call_target="tpu_custom_call" | custom-call | flops 1207959552 | bytes 4718592 | tf_op jit(solution)/shard_map/transform/pallas_call | solution.py:175
  216.7 1.3 collective-permute-start.32
  218.1 3.2 %collective-permute-start.33 = (bf16[2,1,256,128]{3,2,1,0:T(8,128)(2,1)S(1)}, bf16[2,1,256,128]{3,2,1,0:T(8,128)(2,1)S(1)}, u32[]{:S(2)}, u32[]{:S(2)}) collective-permute-start(bf16[2,1,256,128]{3,2,1,0:T(8,128)(2,1)S(1)} %copy-done.38), channel_id=1, source_target_pairs={{0,96},{16,112},{32,64},{48,80},{64,32},{80,48},{96,0},{112,16},{1... | collective-permute-start | bytes 393224 | tf_op jit(solution)/shard_map/ppermute | solution.py:368
  221.3 0.2 collective-permute-start.34
  221.5 1.5 collective-permute-start.21
  223.0 2.7 %collective-permute-start.22 = (bf16[2,1,256,128]{3,2,1,0:T(8,128)(2,1)}, bf16[2,1,256,128]{3,2,1,0:T(8,128)(2,1)S(1)}, u32[]{:S(2)}, u32[]{:S(2)}) collective-permute-start(bf16[2,1,256,128]{3,2,1,0:T(8,128)(2,1)} %get-tuple-element.118), channel_id=1, source_target_pairs={{0,32},{16,48},{32,0},{48,16},{64,96},{80,112},{96,64},{112,80},{1... | collective-permute-start | bytes 393224 | tf_op jit(solution)/shard_map/ppermute | solution.py:368
  225.7 2.0 collective-permute-start.23
  227.7 3.0 %collective-permute-start.24 = (bf16[2,1,256,128]{3,2,1,0:T(8,128)(2,1)}, bf16[2,1,256,128]{3,2,1,0:T(8,128)(2,1)S(1)}, u32[]{:S(2)}, u32[]{:S(2)}) collective-permute-start(bf16[2,1,256,128]{3,2,1,0:T(8,128)(2,1)} %get-tuple-element.120), channel_id=1, source_target_pairs={{0,64},{16,80},{32,96},{48,112},{64,0},{80,16},{96,32},{112,48},{1... | collective-permute-start | bytes 393224 | tf_op jit(solution)/shard_map/ppermute | solution.py:368
  230.8 3.9 %collective-permute-start.26 = (bf16[2,1,256,128]{3,2,1,0:T(8,128)(2,1)}, bf16[2,1,256,128]{3,2,1,0:T(8,128)(2,1)S(1)}, u32[]{:S(2)}, u32[]{:S(2)}) collective-permute-start(bf16[2,1,256,128]{3,2,1,0:T(8,128)(2,1)} %get-tuple-element.122), channel_id=1, source_target_pairs={{0,96},{16,112},{32,64},{48,80},{64,32},{80,48},{96,0},{112,16},{1... | collective-permute-start | bytes 393224 | tf_op jit(solution)/shard_map/ppermute | solution.py:368
  234.7 3.8 %collective-permute-start.27 = (bf16[2,1,256,128]{3,2,1,0:T(8,128)(2,1)}, bf16[2,1,256,128]{3,2,1,0:T(8,128)(2,1)S(1)}, u32[]{:S(2)}, u32[]{:S(2)}) collective-permute-start(bf16[2,1,256,128]{3,2,1,0:T(8,128)(2,1)} %get-tuple-element.123), channel_id=1, source_target_pairs={{0,112},{16,64},{32,80},{48,96},{64,48},{80,0},{96,16},{112,32},{1... | collective-permute-start | bytes 393224 | tf_op jit(solution)/shard_map/ppermute | solution.py:368
  238.6 3.3 %settle.6.refs_11_ = bf16[8,8,256,128]{3,2,1,0:T(8,128)(2,1)} custom-call(s32[2]{0:T(128)S(1)} %pad_add_fusion.meta_ref, bf16[2,1,256,128]{3,2,1,0:T(8,128)(2,1)S(1)} %copy-done.13, bf16[2,1,256,128]{3,2,1,0:T(8,128)(2,1)S(1)} %copy-done.19, bf16[2,1,256,128]{3,2,1,0:T(8,128)(2,1)S(1)} %copy-done.21, ...), custom_call_target="tpu_custom_call", output_to_operand_aliasing={{}: (12, {})} | custom-call | flops 536870912 | bytes 4194304 | tf_op jit(solution)/shard_map/settle/pallas_call | solution.py:256
  242.0 3.3 %settle.7.refs_11_ = bf16[8,8,256,128]{3,2,1,0:T(8,128)(2,1)} custom-call(s32[2]{0:T(128)S(1)} %pad_add_fusion.meta_ref, bf16[2,1,256,128]{3,2,1,0:T(8,128)(2,1)S(1)} %copy-done.4, bf16[2,1,256,128]{3,2,1,0:T(8,128)(2,1)S(1)} %collective-permute-done.14.refs_1_, bf16[2,1,256,128]{3,2,1,0:T(8,128)(2,1)S(1)} %copy-done.6, ...), custom_call_target="tpu_custom_call", output_to_operand_aliasing={{}: (12, {})} | custom-call | flops 536870912 | bytes 4194304 | tf_op jit(solution)/shard_map/settle/pallas_call | solution.py:256
  245.3 3.3 %settle.8.refs_11_ = bf16[8,8,256,128]{3,2,1,0:T(8,128)(2,1)} custom-call(s32[2]{0:T(128)S(1)} %pad_add_fusion.meta_ref, bf16[2,1,256,128]{3,2,1,0:T(8,128)(2,1)S(1)} %copy-done.33, bf16[2,1,256,128]{3,2,1,0:T(8,128)(2,1)S(1)} %collective-permute-done.28.refs_1_, ...), custom_call_target="tpu_custom_call", output_to_operand_aliasing={{}: (12, {})} | custom-call | flops 536870912 | bytes 4194304 | tf_op jit(solution)/shard_map/settle/pallas_call | solution.py:256
  248.7 3.3 %settle.9 = bf16[8,8,256,128]{3,2,1,0:T(8,128)(2,1)} custom-call(s32[2]{0:T(128)S(1)} %pad_add_fusion.meta_ref, bf16[2,1,256,128]{3,2,1,0:T(8,128)(2,1)S(1)} %copy-done.32, bf16[2,1,256,128]{3,2,1,0:T(8,128)(2,1)S(1)} %collective-permute-done.21.refs_1_, ...), custom_call_target="tpu_custom_call", output_to_operand_aliasing={{}: (12, {})} | custom-call | flops 536870912 | bytes 4194304 | tf_op jit(solution)/shard_map/settle/pallas_call | solution.py:256
  (118 shorter events, 0.4 us)
Async XLA Ops:
  93.7 8.7 %copy-start.41 = (s32[128]{0:T(128)S(1)}, s32[128]{0:T(128)}, u32[]{:S(2)}) copy-start(s32[128]{0:T(128)} %param.7) | copy-start | bytes 1540
  93.7 51.4 %all-to-all-start.1 = ((bf16[16,2,2,96,256]{4,3,2,1,0:T(8,128)(2,1)}), bf16[16,2,2,96,256]{4,3,2,1,0:T(8,128)(2,1)}, u32[]{:S(2)}, u32[]{:S(2)}) async-start(bf16[16,2,2,96,256]{4,3,2,1,0:T(8,128)(2,1)} %get-tuple-element.79), calls=%async_computation.1 | async-start | bytes 6291456 | tf_op jit(solution)/shard_map/all_to_all | solution.py:347
  116.3 13.8 %collective-permute-start = (bf16[4,256,128]{2,1,0:T(8,128)(2,1)}, bf16[4,256,128]{2,1,0:T(8,128)(2,1)S(1)}, u32[]{:S(2)}, u32[]{:S(2)}) collective-permute-start(bf16[4,256,128]{2,1,0:T(8,128)(2,1)} %get-tuple-element.82), channel_id=1, source_target_pairs={{0,16},{16,32},{32,48},{48,0},{64,80},{80,96},{96,112},{112,64},{1... | collective-permute-start | bytes 786440 | tf_op jit(solution)/shard_map/ppermute | solution.py:368
  118.0 12.2 %collective-permute-start.1 = (bf16[4,256,128]{2,1,0:T(8,128)(2,1)}, bf16[4,256,128]{2,1,0:T(8,128)(2,1)S(1)}, u32[]{:S(2)}, u32[]{:S(2)}) collective-permute-start(bf16[4,256,128]{2,1,0:T(8,128)(2,1)} %get-tuple-element.83), channel_id=1, source_target_pairs={{0,32},{16,48},{32,0},{48,16},{64,96},{80,112},{96,64},{112,80},{1... | collective-permute-start | bytes 786440 | tf_op jit(solution)/shard_map/ppermute | solution.py:368
  118.9 14.6 %collective-permute-start.2 = (bf16[4,256,128]{2,1,0:T(8,128)(2,1)}, bf16[4,256,128]{2,1,0:T(8,128)(2,1)S(1)}, u32[]{:S(2)}, u32[]{:S(2)}) collective-permute-start(bf16[4,256,128]{2,1,0:T(8,128)(2,1)} %get-tuple-element.84), channel_id=1, source_target_pairs={{0,48},{16,0},{32,16},{48,32},{64,112},{80,64},{96,80},{112,96},{1... | collective-permute-start | bytes 786440 | tf_op jit(solution)/shard_map/ppermute | solution.py:368
  121.3 12.2 %collective-permute-start.3 = (bf16[4,256,128]{2,1,0:T(8,128)(2,1)}, bf16[4,256,128]{2,1,0:T(8,128)(2,1)S(1)}, u32[]{:S(2)}, u32[]{:S(2)}) collective-permute-start(bf16[4,256,128]{2,1,0:T(8,128)(2,1)} %get-tuple-element.85), channel_id=1, source_target_pairs={{0,64},{16,80},{32,96},{48,112},{64,0},{80,16},{96,32},{112,48},{1... | collective-permute-start | bytes 786440 | tf_op jit(solution)/shard_map/ppermute | solution.py:368
  122.9 18.1 %collective-permute-start.4 = (bf16[4,256,128]{2,1,0:T(8,128)(2,1)}, bf16[4,256,128]{2,1,0:T(8,128)(2,1)S(1)}, u32[]{:S(2)}, u32[]{:S(2)}) collective-permute-start(bf16[4,256,128]{2,1,0:T(8,128)(2,1)} %get-tuple-element.86), channel_id=1, source_target_pairs={{0,80},{16,96},{32,112},{48,64},{64,16},{80,32},{96,48},{112,0},{1... | collective-permute-start | bytes 786440 | tf_op jit(solution)/shard_map/ppermute | solution.py:368
  130.2 12.8 %collective-permute-start.5 = (bf16[4,256,128]{2,1,0:T(8,128)(2,1)}, bf16[4,256,128]{2,1,0:T(8,128)(2,1)S(1)}, u32[]{:S(2)}, u32[]{:S(2)}) collective-permute-start(bf16[4,256,128]{2,1,0:T(8,128)(2,1)} %get-tuple-element.87), channel_id=1, source_target_pairs={{0,112},{16,64},{32,80},{48,96},{64,48},{80,0},{96,16},{112,32},{1... | collective-permute-start | bytes 786440 | tf_op jit(solution)/shard_map/ppermute | solution.py:368
  145.1 56.5 %all-to-all-start.2 = ((bf16[16,2,2,96,256]{4,3,2,1,0:T(8,128)(2,1)}), bf16[16,2,2,96,256]{4,3,2,1,0:T(8,128)(2,1)}, u32[]{:S(2)}, u32[]{:S(2)}) async-start(bf16[16,2,2,96,256]{4,3,2,1,0:T(8,128)(2,1)} %get-tuple-element.89), calls=%async_computation.2 | async-start | bytes 6291456 | tf_op jit(solution)/shard_map/all_to_all | solution.py:347
  150.8 20.4 %collective-permute-start.6 = (bf16[4,256,128]{2,1,0:T(8,128)(2,1)}, bf16[4,256,128]{2,1,0:T(8,128)(2,1)S(1)}, u32[]{:S(2)}, u32[]{:S(2)}) collective-permute-start(bf16[4,256,128]{2,1,0:T(8,128)(2,1)} %get-tuple-element.90), channel_id=1, source_target_pairs={{0,96},{16,112},{32,64},{48,80},{64,32},{80,48},{96,0},{112,16},{1... | collective-permute-start | bytes 786440 | tf_op jit(solution)/shard_map/ppermute | solution.py:368
  162.0 12.4 %collective-permute-start.14 = (bf16[2,1,256,128]{3,2,1,0:T(8,128)(2,1)}, bf16[2,1,256,128]{3,2,1,0:T(8,128)(2,1)S(1)}, u32[]{:S(2)}, u32[]{:S(2)}) collective-permute-start(bf16[2,1,256,128]{3,2,1,0:T(8,128)(2,1)} %get-tuple-element.101), channel_id=1, source_target_pairs={{0,16},{16,32},{32,48},{48,0},{64,80},{80,96},{96,112},{112,64},{1... | collective-permute-start | bytes 393224 | tf_op jit(solution)/shard_map/ppermute | solution.py:368
  162.0 13.1 %collective-permute-start.15 = (bf16[2,1,256,128]{3,2,1,0:T(8,128)(2,1)}, bf16[2,1,256,128]{3,2,1,0:T(8,128)(2,1)S(1)}, u32[]{:S(2)}, u32[]{:S(2)}) collective-permute-start(bf16[2,1,256,128]{3,2,1,0:T(8,128)(2,1)} %get-tuple-element.102), channel_id=1, source_target_pairs={{0,32},{16,48},{32,0},{48,16},{64,96},{80,112},{96,64},{112,80},{1... | collective-permute-start | bytes 393224 | tf_op jit(solution)/shard_map/ppermute | solution.py:368
  165.4 12.0 %collective-permute-start.16 = (bf16[2,1,256,128]{3,2,1,0:T(8,128)(2,1)}, bf16[2,1,256,128]{3,2,1,0:T(8,128)(2,1)S(1)}, u32[]{:S(2)}, u32[]{:S(2)}) collective-permute-start(bf16[2,1,256,128]{3,2,1,0:T(8,128)(2,1)} %get-tuple-element.103), channel_id=1, source_target_pairs={{0,48},{16,0},{32,16},{48,32},{64,112},{80,64},{96,80},{112,96},{1... | collective-permute-start | bytes 393224 | tf_op jit(solution)/shard_map/ppermute | solution.py:368
  165.9 13.5 %collective-permute-start.17 = (bf16[2,1,256,128]{3,2,1,0:T(8,128)(2,1)}, bf16[2,1,256,128]{3,2,1,0:T(8,128)(2,1)S(1)}, u32[]{:S(2)}, u32[]{:S(2)}) collective-permute-start(bf16[2,1,256,128]{3,2,1,0:T(8,128)(2,1)} %get-tuple-element.104), channel_id=1, source_target_pairs={{0,64},{16,80},{32,96},{48,112},{64,0},{80,16},{96,32},{112,48},{1... | collective-permute-start | bytes 393224 | tf_op jit(solution)/shard_map/ppermute | solution.py:368
  165.9 8.4 %copy-start.37 = (bf16[2,1,256,128]{3,2,1,0:T(8,128)(2,1)S(1)}, bf16[2,1,256,128]{3,2,1,0:T(8,128)(2,1)}, u32[]{:S(2)}) copy-start(bf16[2,1,256,128]{3,2,1,0:T(8,128)(2,1)} %get-tuple-element.106) | copy-start | bytes 393220
  165.9 9.3 %copy-start.35 = (bf16[2,1,256,128]{3,2,1,0:T(8,128)(2,1)S(1)}, bf16[2,1,256,128]{3,2,1,0:T(8,128)(2,1)}, u32[]{:S(2)}) copy-start(bf16[2,1,256,128]{3,2,1,0:T(8,128)(2,1)} %get-tuple-element.107) | copy-start | bytes 393220
  165.9 25.9 %copy-start = (bf16[4,4,256,256]{3,2,1,0:T(8,128)(2,1)S(1)}, bf16[4,4,256,256]{3,2,1,0:T(8,128)(2,1)}, u32[]{:S(2)}) copy-start(bf16[4,4,256,256]{3,2,1,0:T(8,128)(2,1)} %refs_10_.9) | copy-start | bytes 6291460
  165.9 25.9 %copy-start.1 = (bf16[4,256,128]{2,1,0:T(8,128)(2,1)S(1)}, bf16[4,256,128]{2,1,0:T(8,128)(2,1)}, u32[]{:S(2)}) copy-start(bf16[4,256,128]{2,1,0:T(8,128)(2,1)} %get-tuple-element.108.refs_0_) | copy-start | bytes 786436
  165.9 25.9 %copy-start.3 = (bf16[4,256,128]{2,1,0:T(8,128)(2,1)S(1)}, bf16[4,256,128]{2,1,0:T(8,128)(2,1)}, u32[]{:S(2)}) copy-start(bf16[4,256,128]{2,1,0:T(8,128)(2,1)} %copy-done.2) | copy-start | bytes 786436
  165.9 25.9 %copy-start.34 = (s32[8,128]{1,0:T(8,128)S(1)}, s32[8,128]{1,0:T(8,128)}, u32[]{:S(2)}) copy-start(s32[8,128]{1,0:T(8,128)} %refs_9_.9) | copy-start | bytes 12292
  171.2 11.6 %collective-permute-start.18 = (bf16[2,1,256,128]{3,2,1,0:T(8,128)(2,1)S(1)}, bf16[2,1,256,128]{3,2,1,0:T(8,128)(2,1)S(1)}, u32[]{:S(2)}, u32[]{:S(2)}) collective-permute-start(bf16[2,1,256,128]{3,2,1,0:T(8,128)(2,1)S(1)} %copy-done.39), channel_id=1, source_target_pairs={{0,80},{16,96},{32,112},{48,64},{64,16},{80,32},{96,48},{112,0},{1... | collective-permute-start | bytes 393224 | tf_op jit(solution)/shard_map/ppermute | solution.py:368
  174.3 8.6 %collective-permute-start.19 = (bf16[2,1,256,128]{3,2,1,0:T(8,128)(2,1)S(1)}, bf16[2,1,256,128]{3,2,1,0:T(8,128)(2,1)S(1)}, u32[]{:S(2)}, u32[]{:S(2)}) collective-permute-start(bf16[2,1,256,128]{3,2,1,0:T(8,128)(2,1)S(1)} %copy-done.37), channel_id=1, source_target_pairs={{0,96},{16,112},{32,64},{48,80},{64,32},{80,48},{96,0},{112,16},{1... | collective-permute-start | bytes 393224 | tf_op jit(solution)/shard_map/ppermute | solution.py:368
  175.2 23.1 %copy-start.5 = (bf16[2,1,256,128]{3,2,1,0:T(8,128)(2,1)}, bf16[2,1,256,128]{3,2,1,0:T(8,128)(2,1)S(1)}, u32[]{:S(2)}) copy-start(bf16[2,1,256,128]{3,2,1,0:T(8,128)(2,1)S(1)} %collective-permute-done.15.refs_2_) | copy-start | bytes 393220
  175.2 11.3 %collective-permute-start.20 = (bf16[2,1,256,128]{3,2,1,0:T(8,128)(2,1)S(1)}, bf16[2,1,256,128]{3,2,1,0:T(8,128)(2,1)S(1)}, u32[]{:S(2)}, u32[]{:S(2)}) collective-permute-start(bf16[2,1,256,128]{3,2,1,0:T(8,128)(2,1)S(1)} %copy-done.35), channel_id=1, source_target_pairs={{0,112},{16,64},{32,80},{48,96},{64,48},{80,0},{96,16},{112,32},{1... | collective-permute-start | bytes 393224 | tf_op jit(solution)/shard_map/ppermute | solution.py:368
  178.1 8.4 %collective-permute-start.7 = (bf16[2,1,256,128]{3,2,1,0:T(8,128)(2,1)}, bf16[2,1,256,128]{3,2,1,0:T(8,128)(2,1)S(1)}, u32[]{:S(2)}, u32[]{:S(2)}) collective-permute-start(bf16[2,1,256,128]{3,2,1,0:T(8,128)(2,1)} %get-tuple-element.93), channel_id=1, source_target_pairs={{0,16},{16,32},{32,48},{48,0},{64,80},{80,96},{96,112},{112,64},{1... | collective-permute-start | bytes 393224 | tf_op jit(solution)/shard_map/ppermute | solution.py:368
  179.4 18.8 %copy-start.9 = (bf16[2,1,256,128]{3,2,1,0:T(8,128)(2,1)}, bf16[2,1,256,128]{3,2,1,0:T(8,128)(2,1)S(1)}, u32[]{:S(2)}) copy-start(bf16[2,1,256,128]{3,2,1,0:T(8,128)(2,1)S(1)} %collective-permute-done.17.refs_4_) | copy-start | bytes 393220
  179.4 11.0 %collective-permute-start.8 = (bf16[2,1,256,128]{3,2,1,0:T(8,128)(2,1)}, bf16[2,1,256,128]{3,2,1,0:T(8,128)(2,1)S(1)}, u32[]{:S(2)}, u32[]{:S(2)}) collective-permute-start(bf16[2,1,256,128]{3,2,1,0:T(8,128)(2,1)} %get-tuple-element.94), channel_id=1, source_target_pairs={{0,32},{16,48},{32,0},{48,16},{64,96},{80,112},{96,64},{112,80},{1... | collective-permute-start | bytes 393224 | tf_op jit(solution)/shard_map/ppermute | solution.py:368
  182.8 15.4 %copy-start.11 = (bf16[2,1,256,128]{3,2,1,0:T(8,128)(2,1)}, bf16[2,1,256,128]{3,2,1,0:T(8,128)(2,1)S(1)}, u32[]{:S(2)}) copy-start(bf16[2,1,256,128]{3,2,1,0:T(8,128)(2,1)S(1)} %collective-permute-done.18.refs_5_) | copy-start | bytes 393220
  182.8 15.5 %collective-permute-start.9 = (bf16[2,1,256,128]{3,2,1,0:T(8,128)(2,1)}, bf16[2,1,256,128]{3,2,1,0:T(8,128)(2,1)S(1)}, u32[]{:S(2)}, u32[]{:S(2)}) collective-permute-start(bf16[2,1,256,128]{3,2,1,0:T(8,128)(2,1)} %get-tuple-element.95), channel_id=1, source_target_pairs={{0,48},{16,0},{32,16},{48,32},{64,112},{80,64},{96,80},{112,96},{1... | collective-permute-start | bytes 393224 | tf_op jit(solution)/shard_map/ppermute | solution.py:368
  182.9 15.3 %copy-start.14 = (bf16[2,1,256,128]{3,2,1,0:T(8,128)(2,1)}, bf16[2,1,256,128]{3,2,1,0:T(8,128)(2,1)S(1)}, u32[]{:S(2)}) copy-start(bf16[2,1,256,128]{3,2,1,0:T(8,128)(2,1)S(1)} %collective-permute-done.19.refs_6_) | copy-start | bytes 393220
  182.9 16.0 %collective-permute-start.10 = (bf16[2,1,256,128]{3,2,1,0:T(8,128)(2,1)}, bf16[2,1,256,128]{3,2,1,0:T(8,128)(2,1)S(1)}, u32[]{:S(2)}, u32[]{:S(2)}) collective-permute-start(bf16[2,1,256,128]{3,2,1,0:T(8,128)(2,1)} %get-tuple-element.96), channel_id=1, source_target_pairs={{0,64},{16,80},{32,96},{48,112},{64,0},{80,16},{96,32},{112,48},{1... | collective-permute-start | bytes 393224 | tf_op jit(solution)/shard_map/ppermute | solution.py:368
  186.5 11.7 %copy-start.16 = (bf16[2,1,256,128]{3,2,1,0:T(8,128)(2,1)}, bf16[2,1,256,128]{3,2,1,0:T(8,128)(2,1)S(1)}, u32[]{:S(2)}) copy-start(bf16[2,1,256,128]{3,2,1,0:T(8,128)(2,1)S(1)} %collective-permute-done.20.refs_7_) | copy-start | bytes 393220
  186.5 13.1 %collective-permute-start.11 = (bf16[2,1,256,128]{3,2,1,0:T(8,128)(2,1)}, bf16[2,1,256,128]{3,2,1,0:T(8,128)(2,1)S(1)}, u32[]{:S(2)}, u32[]{:S(2)}) collective-permute-start(bf16[2,1,256,128]{3,2,1,0:T(8,128)(2,1)} %get-tuple-element.97), channel_id=1, source_target_pairs={{0,80},{16,96},{32,112},{48,64},{64,16},{80,32},{96,48},{112,0},{1... | collective-permute-start | bytes 393224 | tf_op jit(solution)/shard_map/ppermute | solution.py:368
  187.2 13.0 %collective-permute-start.12 = (bf16[2,1,256,128]{3,2,1,0:T(8,128)(2,1)}, bf16[2,1,256,128]{3,2,1,0:T(8,128)(2,1)S(1)}, u32[]{:S(2)}, u32[]{:S(2)}) collective-permute-start(bf16[2,1,256,128]{3,2,1,0:T(8,128)(2,1)} %get-tuple-element.98), channel_id=1, source_target_pairs={{0,96},{16,112},{32,64},{48,80},{64,32},{80,48},{96,0},{112,16},{1... | collective-permute-start | bytes 393224 | tf_op jit(solution)/shard_map/ppermute | solution.py:368
  190.4 7.8 %copy-start.20 = (bf16[2,1,256,128]{3,2,1,0:T(8,128)(2,1)}, bf16[2,1,256,128]{3,2,1,0:T(8,128)(2,1)S(1)}, u32[]{:S(2)}) copy-start(bf16[2,1,256,128]{3,2,1,0:T(8,128)(2,1)S(1)} %collective-permute-done.8.refs_2_) | copy-start | bytes 393220
  190.4 10.5 %collective-permute-start.13 = (bf16[2,1,256,128]{3,2,1,0:T(8,128)(2,1)}, bf16[2,1,256,128]{3,2,1,0:T(8,128)(2,1)S(1)}, u32[]{:S(2)}, u32[]{:S(2)}) collective-permute-start(bf16[2,1,256,128]{3,2,1,0:T(8,128)(2,1)} %get-tuple-element.99), channel_id=1, source_target_pairs={{0,112},{16,64},{32,80},{48,96},{64,48},{80,0},{96,16},{112,32},{1... | collective-permute-start | bytes 393224 | tf_op jit(solution)/shard_map/ppermute | solution.py:368
  206.4 11.6 %collective-permute-start.28 = (bf16[2,1,256,128]{3,2,1,0:T(8,128)(2,1)}, bf16[2,1,256,128]{3,2,1,0:T(8,128)(2,1)S(1)}, u32[]{:S(2)}, u32[]{:S(2)}) collective-permute-start(bf16[2,1,256,128]{3,2,1,0:T(8,128)(2,1)} %get-tuple-element.125), channel_id=1, source_target_pairs={{0,16},{16,32},{32,48},{48,0},{64,80},{80,96},{96,112},{112,64},{1... | collective-permute-start | bytes 393224 | tf_op jit(solution)/shard_map/ppermute | solution.py:368
  206.6 14.7 %collective-permute-start.29 = (bf16[2,1,256,128]{3,2,1,0:T(8,128)(2,1)}, bf16[2,1,256,128]{3,2,1,0:T(8,128)(2,1)S(1)}, u32[]{:S(2)}, u32[]{:S(2)}) collective-permute-start(bf16[2,1,256,128]{3,2,1,0:T(8,128)(2,1)} %get-tuple-element.126), channel_id=1, source_target_pairs={{0,32},{16,48},{32,0},{48,16},{64,96},{80,112},{96,64},{112,80},{1... | collective-permute-start | bytes 393224 | tf_op jit(solution)/shard_map/ppermute | solution.py:368
  209.5 12.0 %collective-permute-start.30 = (bf16[2,1,256,128]{3,2,1,0:T(8,128)(2,1)}, bf16[2,1,256,128]{3,2,1,0:T(8,128)(2,1)S(1)}, u32[]{:S(2)}, u32[]{:S(2)}) collective-permute-start(bf16[2,1,256,128]{3,2,1,0:T(8,128)(2,1)} %get-tuple-element.127), channel_id=1, source_target_pairs={{0,48},{16,0},{32,16},{48,32},{64,112},{80,64},{96,80},{112,96},{1... | collective-permute-start | bytes 393224 | tf_op jit(solution)/shard_map/ppermute | solution.py:368
  211.5 11.5 %collective-permute-start.31 = (bf16[2,1,256,128]{3,2,1,0:T(8,128)(2,1)}, bf16[2,1,256,128]{3,2,1,0:T(8,128)(2,1)S(1)}, u32[]{:S(2)}, u32[]{:S(2)}) collective-permute-start(bf16[2,1,256,128]{3,2,1,0:T(8,128)(2,1)} %get-tuple-element.128), channel_id=1, source_target_pairs={{0,64},{16,80},{32,96},{48,112},{64,0},{80,16},{96,32},{112,48},{1... | collective-permute-start | bytes 393224 | tf_op jit(solution)/shard_map/ppermute | solution.py:368
  211.8 9.5 %copy-start.36 = (bf16[2,1,256,128]{3,2,1,0:T(8,128)(2,1)S(1)}, bf16[2,1,256,128]{3,2,1,0:T(8,128)(2,1)}, u32[]{:S(2)}) copy-start(bf16[2,1,256,128]{3,2,1,0:T(8,128)(2,1)} %get-tuple-element.131) | copy-start | bytes 393220
  211.8 26.8 %copy-start.13 = (bf16[2,1,256,128]{3,2,1,0:T(8,128)(2,1)S(1)}, bf16[2,1,256,128]{3,2,1,0:T(8,128)(2,1)}, u32[]{:S(2)}) copy-start(bf16[2,1,256,128]{3,2,1,0:T(8,128)(2,1)} %get-tuple-element.140.refs_0_) | copy-start | bytes 393220
  211.8 26.8 %copy-start.19 = (bf16[2,1,256,128]{3,2,1,0:T(8,128)(2,1)S(1)}, bf16[2,1,256,128]{3,2,1,0:T(8,128)(2,1)}, u32[]{:S(2)}) copy-start(bf16[2,1,256,128]{3,2,1,0:T(8,128)(2,1)} %copy-done.18) | copy-start | bytes 393220
  211.8 26.7 %copy-start.21 = (bf16[2,1,256,128]{3,2,1,0:T(8,128)(2,1)S(1)}, bf16[2,1,256,128]{3,2,1,0:T(8,128)(2,1)}, u32[]{:S(2)}) copy-start(bf16[2,1,256,128]{3,2,1,0:T(8,128)(2,1)} %copy-done.20) | copy-start | bytes 393220
  211.8 26.7 %copy-start.23 = (bf16[2,1,256,128]{3,2,1,0:T(8,128)(2,1)S(1)}, bf16[2,1,256,128]{3,2,1,0:T(8,128)(2,1)}, u32[]{:S(2)}) copy-start(bf16[2,1,256,128]{3,2,1,0:T(8,128)(2,1)} %copy-done.22) | copy-start | bytes 393220
  211.8 26.7 %copy-start.25 = (bf16[2,1,256,128]{3,2,1,0:T(8,128)(2,1)S(1)}, bf16[2,1,256,128]{3,2,1,0:T(8,128)(2,1)}, u32[]{:S(2)}) copy-start(bf16[2,1,256,128]{3,2,1,0:T(8,128)(2,1)} %copy-done.24) | copy-start | bytes 393220
  211.8 26.7 %copy-start.27 = (bf16[2,1,256,128]{3,2,1,0:T(8,128)(2,1)S(1)}, bf16[2,1,256,128]{3,2,1,0:T(8,128)(2,1)}, u32[]{:S(2)}) copy-start(bf16[2,1,256,128]{3,2,1,0:T(8,128)(2,1)} %copy-done.26) | copy-start | bytes 393220
  211.8 26.7 %copy-start.29 = (bf16[2,1,256,128]{3,2,1,0:T(8,128)(2,1)S(1)}, bf16[2,1,256,128]{3,2,1,0:T(8,128)(2,1)}, u32[]{:S(2)}) copy-start(bf16[2,1,256,128]{3,2,1,0:T(8,128)(2,1)} %copy-done.28) | copy-start | bytes 393220
  211.8 26.7 %copy-start.31 = (bf16[2,1,256,128]{3,2,1,0:T(8,128)(2,1)S(1)}, bf16[2,1,256,128]{3,2,1,0:T(8,128)(2,1)}, u32[]{:S(2)}) copy-start(bf16[2,1,256,128]{3,2,1,0:T(8,128)(2,1)} %copy-done.30) | copy-start | bytes 393220
  216.7 9.0 %collective-permute-start.32 = (bf16[2,1,256,128]{3,2,1,0:T(8,128)(2,1)S(1)}, bf16[2,1,256,128]{3,2,1,0:T(8,128)(2,1)S(1)}, u32[]{:S(2)}, u32[]{:S(2)}) collective-permute-start(bf16[2,1,256,128]{3,2,1,0:T(8,128)(2,1)S(1)} %copy-done.40), channel_id=1, source_target_pairs={{0,80},{16,96},{32,112},{48,64},{64,16},{80,32},{96,48},{112,0},{1... | collective-permute-start | bytes 393224 | tf_op jit(solution)/shard_map/ppermute | solution.py:368
  218.1 9.7 %collective-permute-start.33 = (bf16[2,1,256,128]{3,2,1,0:T(8,128)(2,1)S(1)}, bf16[2,1,256,128]{3,2,1,0:T(8,128)(2,1)S(1)}, u32[]{:S(2)}, u32[]{:S(2)}) collective-permute-start(bf16[2,1,256,128]{3,2,1,0:T(8,128)(2,1)S(1)} %copy-done.38), channel_id=1, source_target_pairs={{0,96},{16,112},{32,64},{48,80},{64,32},{80,48},{96,0},{112,16},{1... | collective-permute-start | bytes 393224 | tf_op jit(solution)/shard_map/ppermute | solution.py:368
  221.3 9.5 %collective-permute-start.34 = (bf16[2,1,256,128]{3,2,1,0:T(8,128)(2,1)S(1)}, bf16[2,1,256,128]{3,2,1,0:T(8,128)(2,1)S(1)}, u32[]{:S(2)}, u32[]{:S(2)}) collective-permute-start(bf16[2,1,256,128]{3,2,1,0:T(8,128)(2,1)S(1)} %copy-done.36), channel_id=1, source_target_pairs={{0,112},{16,64},{32,80},{48,96},{64,48},{80,0},{96,16},{112,32},{1... | collective-permute-start | bytes 393224 | tf_op jit(solution)/shard_map/ppermute | solution.py:368
  221.5 9.3 %collective-permute-start.21 = (bf16[2,1,256,128]{3,2,1,0:T(8,128)(2,1)}, bf16[2,1,256,128]{3,2,1,0:T(8,128)(2,1)S(1)}, u32[]{:S(2)}, u32[]{:S(2)}) collective-permute-start(bf16[2,1,256,128]{3,2,1,0:T(8,128)(2,1)} %get-tuple-element.117), channel_id=1, source_target_pairs={{0,16},{16,32},{32,48},{48,0},{64,80},{80,96},{96,112},{112,64},{1... | collective-permute-start | bytes 393224 | tf_op jit(solution)/shard_map/ppermute | solution.py:368
  223.0 11.6 %collective-permute-start.22 = (bf16[2,1,256,128]{3,2,1,0:T(8,128)(2,1)}, bf16[2,1,256,128]{3,2,1,0:T(8,128)(2,1)S(1)}, u32[]{:S(2)}, u32[]{:S(2)}) collective-permute-start(bf16[2,1,256,128]{3,2,1,0:T(8,128)(2,1)} %get-tuple-element.118), channel_id=1, source_target_pairs={{0,32},{16,48},{32,0},{48,16},{64,96},{80,112},{96,64},{112,80},{1... | collective-permute-start | bytes 393224 | tf_op jit(solution)/shard_map/ppermute | solution.py:368
  225.7 22.9 %collective-permute-start.23 = (bf16[2,1,256,128]{3,2,1,0:T(8,128)(2,1)}, bf16[2,1,256,128]{3,2,1,0:T(8,128)(2,1)S(1)}, u32[]{:S(2)}, u32[]{:S(2)}) collective-permute-start(bf16[2,1,256,128]{3,2,1,0:T(8,128)(2,1)} %get-tuple-element.119), channel_id=1, source_target_pairs={{0,48},{16,0},{32,16},{48,32},{64,112},{80,64},{96,80},{112,96},{1... | collective-permute-start | bytes 393224 | tf_op jit(solution)/shard_map/ppermute | solution.py:368
  227.7 20.9 %collective-permute-start.24 = (bf16[2,1,256,128]{3,2,1,0:T(8,128)(2,1)}, bf16[2,1,256,128]{3,2,1,0:T(8,128)(2,1)S(1)}, u32[]{:S(2)}, u32[]{:S(2)}) collective-permute-start(bf16[2,1,256,128]{3,2,1,0:T(8,128)(2,1)} %get-tuple-element.120), channel_id=1, source_target_pairs={{0,64},{16,80},{32,96},{48,112},{64,0},{80,16},{96,32},{112,48},{1... | collective-permute-start | bytes 393224 | tf_op jit(solution)/shard_map/ppermute | solution.py:368
  230.7 17.9 %collective-permute-start.25 = (bf16[2,1,256,128]{3,2,1,0:T(8,128)(2,1)}, bf16[2,1,256,128]{3,2,1,0:T(8,128)(2,1)S(1)}, u32[]{:S(2)}, u32[]{:S(2)}) collective-permute-start(bf16[2,1,256,128]{3,2,1,0:T(8,128)(2,1)} %get-tuple-element.121), channel_id=1, source_target_pairs={{0,80},{16,96},{32,112},{48,64},{64,16},{80,32},{96,48},{112,0},{1... | collective-permute-start | bytes 393224 | tf_op jit(solution)/shard_map/ppermute | solution.py:368
  230.8 17.9 %collective-permute-start.26 = (bf16[2,1,256,128]{3,2,1,0:T(8,128)(2,1)}, bf16[2,1,256,128]{3,2,1,0:T(8,128)(2,1)S(1)}, u32[]{:S(2)}, u32[]{:S(2)}) collective-permute-start(bf16[2,1,256,128]{3,2,1,0:T(8,128)(2,1)} %get-tuple-element.122), channel_id=1, source_target_pairs={{0,96},{16,112},{32,64},{48,80},{64,32},{80,48},{96,0},{112,16},{1... | collective-permute-start | bytes 393224 | tf_op jit(solution)/shard_map/ppermute | solution.py:368
  234.7 7.3 %copy-start.8 = (bf16[2,1,256,128]{3,2,1,0:T(8,128)(2,1)S(1)}, bf16[2,1,256,128]{3,2,1,0:T(8,128)(2,1)}, u32[]{:S(2)}) copy-start(bf16[2,1,256,128]{3,2,1,0:T(8,128)(2,1)} %copy-done.7) | copy-start | bytes 393220
  234.7 7.3 %copy-start.10 = (bf16[2,1,256,128]{3,2,1,0:T(8,128)(2,1)S(1)}, bf16[2,1,256,128]{3,2,1,0:T(8,128)(2,1)}, u32[]{:S(2)}) copy-start(bf16[2,1,256,128]{3,2,1,0:T(8,128)(2,1)} %copy-done.9) | copy-start | bytes 393220
  234.7 7.3 %copy-start.12 = (bf16[2,1,256,128]{3,2,1,0:T(8,128)(2,1)S(1)}, bf16[2,1,256,128]{3,2,1,0:T(8,128)(2,1)}, u32[]{:S(2)}) copy-start(bf16[2,1,256,128]{3,2,1,0:T(8,128)(2,1)} %copy-done.11) | copy-start | bytes 393220
  234.7 7.3 %copy-start.15 = (bf16[2,1,256,128]{3,2,1,0:T(8,128)(2,1)S(1)}, bf16[2,1,256,128]{3,2,1,0:T(8,128)(2,1)}, u32[]{:S(2)}) copy-start(bf16[2,1,256,128]{3,2,1,0:T(8,128)(2,1)} %copy-done.14) | copy-start | bytes 393220
  234.7 7.3 %copy-start.17 = (bf16[2,1,256,128]{3,2,1,0:T(8,128)(2,1)S(1)}, bf16[2,1,256,128]{3,2,1,0:T(8,128)(2,1)}, u32[]{:S(2)}) copy-start(bf16[2,1,256,128]{3,2,1,0:T(8,128)(2,1)} %copy-done.16) | copy-start | bytes 393220
  234.7 14.0 %collective-permute-start.27 = (bf16[2,1,256,128]{3,2,1,0:T(8,128)(2,1)}, bf16[2,1,256,128]{3,2,1,0:T(8,128)(2,1)S(1)}, u32[]{:S(2)}, u32[]{:S(2)}) collective-permute-start(bf16[2,1,256,128]{3,2,1,0:T(8,128)(2,1)} %get-tuple-element.123), channel_id=1, source_target_pairs={{0,112},{16,64},{32,80},{48,96},{64,48},{80,0},{96,16},{112,32},{1... | collective-permute-start | bytes 393224 | tf_op jit(solution)/shard_map/ppermute | solution.py:368
  (15 other events, 43.1 us)

commit v6 on v4

--- a/solution.py
+++ b/solution.py
@@ -9,8 +9,8 @@
 
 ZS, Y = 2, 4
 CHUNKS = (4, 2, 2)
-FLIPPED = (False, True, True)
-TIES = {2: ((0, (0, 1, 2, 3, 4, 5, 7)),), 3: ((0, (6,)), (1, range(8)))}
+FLIPPED = (False, True, False)
+TIES = {2: ((0, (0, 1, 2, 3, 4, 5, 7)),), 3: ((0, (6,)), (1, (0, 1, 2, 3)))}
 ORDER = (6, 2, 5, 7, 1, 3, 4)
 STEP = 16
 BF16, F32 = jnp.bfloat16, jnp.float32

time: 241 us -> 245 us (1.017)
  waiting for transfers between devices: 41.1 us -> 51.2 us
  starting transfers between devices: 50.3 us -> 45.7 us
    all_to_all x0 -> x1, waiting for transfers between devices: none -> 27.9 us  [on_device(): gots.append(lax.all_to_all(send, 'lat', 0, 0, tiled=True))]
    ppermute x21, waiting for transfers between devices: 39.8 us -> 22 us  [on_device(): moved[h] = lax.ppermute(parts[h], 'rad', rad_targets(h // Y, h % Y))]
    ppermute x21, starting transfers between devices: 37.9 us -> 31.7 us  [on_device(): moved[h] = lax.ppermute(parts[h], 'rad', rad_targets(h // Y, h % Y))]
    all_to_all x0 -> x1, starting transfers between devices: none -> 5.92 us  [on_device(): gots.append(lax.all_to_all(send, 'lat', 0, 0, tiled=True))]
    all_to_all x2 -> x1, starting transfers between devices: 12.4 us -> 8.03 us  [on_device(): lax.all_to_all(send, ('rad', 'lat'), 0, 0, tiled=True, axis_index_groups=...]
    unnamed x46 -> x38, local copies, waits for them, and re-layouts: 5.71 us -> 4.32 us
  transfers between devices with their start and end apart: 23 -> 23, of which waited for: 13 -> 8; matrix products, arithmetic and copies ran while one was open for 0% -> 0% of each run, Pallas kernels for 14% -> 17%
where the time goes in v6:
time: 245 us; the launch traced here: 240 us
  blocking collectives  76.8 us (31%)
  Pallas kernels  60.8 us (25%)
  waiting for transfers between devices  51.2 us (21%)
  starting transfers between devices  45.7 us (19%)
  local copies, waits for them, and re-layouts  4.53 us (2%)
    all_to_all x1, blocking collectives, on_device(): gots.append(lax.all_to_all(send, 'lat', 0, 0, tiled=True))  76.8 us
    ppermute x21, starting transfers between devices, on_device(): moved[h] = lax.ppermute(parts[h], 'rad', rad_targets(h // Y, h % Y))  31.7 us
    pallas_call x3, Pallas kernels, transform(): pl.pallas_call(kernel, grid_spec=pltpu.PrefetchScalarGridSpec(num_scalar_...  29.7 us
    all_to_all x1, waiting for transfers between devices, on_device(): gots.append(lax.all_to_all(send, 'lat', 0, 0, tiled=True))  27.9 us
    ppermute x21, waiting for transfers between devices, on_device(): moved[h] = lax.ppermute(parts[h], 'rad', rad_targets(h // Y, h % Y))  22 us
    pallas_call x1, Pallas kernels, prep(): pl.pallas_call(functools.partial(prep_kernel, starts, per_dev), grid=(lat...  15.9 us
    pallas_call x3, Pallas kernels, settle(): pl.pallas_call(functools.partial(kernel, first, flipped), grid_spec=pltpu...  15.1 us
    all_to_all x1, starting transfers between devices, on_device(): lax.all_to_all(send, ('rad', 'lat'), 0, 0, tiled=True, axis_index_groups=...  8.03 us
  transfers between devices with their start and end apart: 23, of which 8 were waited for; matrix products, arithmetic and copies ran while one was open for 0% of the time, Pallas kernels for 17%

profile of v6, /device:TPU:74, one launch (start us, length us, event | category | flops | bytes accessed | tf_op | source)
XLA Modules:
  0.0 240.4 jit_solution(12366950626920740194)
XLA Ops:
  0.0 0.7 broadcast_multiply_fusion
  0.7 0.1 iota_add_fusion
  0.7 0.1 add.69.key_ref
  0.9 15.9 %prep.1 = (bf16[16,4,2,96,256]{4,3,2,1,0:T(8,128)(2,1)}, bf16[16,2,2,96,256]{4,3,2,1,0:T(8,128)(2,1)}, bf16[16,2,2,96,256]{4,3,2,1,0:T(8,128)(2,1)}) custom-call(s32[1,256]{1,0:T(1,128)S(1)} %add.69.key_ref, bf16[256,96,256]{2,1,0:T(8,128)(2,1)} %bitcast.8), custom_call_target="tpu_custom_call" | custom-call | flops 9663676416 | bytes 25165824 | tf_op jit(solution)/shard_map/prep/pallas_call | solution.py:72
  16.8 76.8 %all_to_all.15.got_ref = bf16[16,4,2,96,256]{4,3,2,1,0:T(8,128)(2,1)} all-to-all(bf16[16,4,2,96,256]{4,3,2,1,0:T(8,128)(2,1)} %get-tuple-element.49), channel_id=1, replica_groups=mesh['rad'=8,'lat'=16] {'lat'}, dimensions={0} | all-to-all | bytes 12582912 | tf_op jit(solution)/shard_map/all_to_all | solution.py:355
  93.7 8.0 %all-to-all-start.1 = ((bf16[16,2,2,96,256]{4,3,2,1,0:T(8,128)(2,1)}), bf16[16,2,2,96,256]{4,3,2,1,0:T(8,128)(2,1)S(1)}, u32[]{:S(2)}, u32[]{:S(2)}) async-start(bf16[16,2,2,96,256]{4,3,2,1,0:T(8,128)(2,1)} %get-tuple-element.51), calls=%async_computation.1 | async-start | bytes 6291456 | tf_op jit(solution)/shard_map/all_to_all | solution.py:350
  101.7 0.2 select_reduce_fusion
  101.9 0.1 pad_add_fusion.3.meta_ref
  102.0 13.7 %transform.3 = (bf16[4,256,128]{2,1,0:T(8,128)(2,1)}, bf16[4,256,128]{2,1,0:T(8,128)(2,1)}, bf16[4,256,128]{2,1,0:T(8,128)(2,1)}, bf16[4,256,128]{2,1,0:T(8,128)...) custom-call(s32[13]{0:T(128)S(1)} %pad_add_fusion.3.meta_ref, ...), custom_call_target="tpu_custom_call" | custom-call | flops 4831838208 | bytes 18874368 | tf_op jit(solution)/shard_map/transform/pallas_call | solution.py:178
  115.7 1.6 collective-permute-start
  117.3 0.9 collective-permute-start.1
  118.2 2.4 %collective-permute-start.2 = (bf16[4,256,128]{2,1,0:T(8,128)(2,1)}, bf16[4,256,128]{2,1,0:T(8,128)(2,1)S(1)}, u32[]{:S(2)}, u32[]{:S(2)}) collective-permute-start(bf16[4,256,128]{2,1,0:T(8,128)(2,1)} %get-tuple-element.56), channel_id=1, source_target_pairs={{0,48},{16,0},{32,16},{48,32},{64,112},{80,64},{96,80},{112,96},{1... | collective-permute-start | bytes 786440 | tf_op jit(solution)/shard_map/ppermute | solution.py:365
  120.7 1.6 collective-permute-start.3
  122.3 0.0 collective-permute-start.4
  122.3 7.2 %collective-permute-done.refs_1_ = bf16[4,256,128]{2,1,0:T(8,128)(2,1)S(1)} collective-permute-done((bf16[4,256,128]{2,1,0:T(8,128)(2,1)}, bf16[4,256,128]{2,1,0:T(8,128)(2,1)S(1)}, u32[]{:S(2)}, u32[]{:S(2)}) %collective-permute-start) | collective-permute-done | bytes 262176 | tf_op jit(solution)/shard_map/ppermute | solution.py:365
  129.5 0.7 copy-done.3
  130.2 0.0 collective-permute-start.5
  130.2 0.0 collective-permute-done.1.refs_2_
  130.2 0.7 copy-done.5
  130.9 1.9 collective-permute-done.2.refs_3_
  132.8 0.7 copy-done.7
  133.5 0.0 collective-permute-done.3.refs_4_
  133.6 0.7 copy-done.9
  134.3 6.1 %collective-permute-done.4.refs_5_ = bf16[4,256,128]{2,1,0:T(8,128)(2,1)S(1)} collective-permute-done((bf16[4,256,128]{2,1,0:T(8,128)(2,1)}, bf16[4,256,128]{2,1,0:T(8,128)(2,1)S(1)}, u32[]{:S(2)}, u32[]{:S(2)}) %collective-permute-start.4) | collective-permute-done | bytes 262176 | tf_op jit(solution)/shard_map/ppermute | solution.py:365
  140.4 0.7 copy-done.11
  141.1 1.1 collective-permute-done.5.refs_7_
  142.2 0.7 copy-done.13
  142.9 1.3 all-to-all-done.1.got_ref
  144.3 5.9 %all-to-all-start.2 = ((bf16[16,2,2,96,256]{4,3,2,1,0:T(8,128)(2,1)}), bf16[16,2,2,96,256]{4,3,2,1,0:T(8,128)(2,1)}, u32[]{:S(2)}, u32[]{:S(2)}) async-start(bf16[16,2,2,96,256]{4,3,2,1,0:T(8,128)(2,1)} %get-tuple-element.61), calls=%async_computation.2 | async-start | bytes 6291456 | tf_op jit(solution)/shard_map/all_to_all | solution.py:355
  150.2 0.1 fusion.4
  150.3 0.1 pad_add_fusion.4
  150.3 3.2 %collective-permute-start.6 = (bf16[4,256,128]{2,1,0:T(8,128)(2,1)}, bf16[4,256,128]{2,1,0:T(8,128)(2,1)S(1)}, u32[]{:S(2)}, u32[]{:S(2)}) collective-permute-start(bf16[4,256,128]{2,1,0:T(8,128)(2,1)} %get-tuple-element.62), channel_id=1, source_target_pairs={{0,96},{16,112},{32,64},{48,80},{64,32},{80,48},{96,0},{112,16},{1... | collective-permute-start | bytes 786440 | tf_op jit(solution)/shard_map/ppermute | solution.py:365
  153.6 0.0 copy-start.16
  153.6 8.0 %transform.4 = (bf16[2,2,256,128]{3,2,1,0:T(8,128)(2,1)}, bf16[2,2,256,128]{3,2,1,0:T(8,128)(2,1)}, bf16[2,2,256,128]{3,2,1,0:T(8,128)(2,1)}, bf16[2,2,256,128]{...) custom-call(s32[11]{0:T(128)S(1)} %get-tuple-element.93.meta_ref, ...), custom_call_target="tpu_custom_call" | custom-call | flops 2415919104 | bytes 9437184 | tf_op jit(solution)/shard_map/transform/pallas_call | solution.py:178
  161.6 0.1 collective-permute-start.7
  161.7 3.4 %collective-permute-start.8 = (bf16[2,2,256,128]{3,2,1,0:T(8,128)(2,1)}, bf16[2,2,256,128]{3,2,1,0:T(8,128)(2,1)S(1)}, u32[]{:S(2)}, u32[]{:S(2)}) collective-permute-start(bf16[2,2,256,128]{3,2,1,0:T(8,128)(2,1)} %get-tuple-element.66), channel_id=1, source_target_pairs={{0,32},{16,48},{32,0},{48,16},{64,96},{80,112},{96,64},{112,80},{1... | collective-permute-start | bytes 786440 | tf_op jit(solution)/shard_map/ppermute | solution.py:365
  165.1 0.5 collective-permute-start.9
  165.5 0.1 pad_add_fusion.meta_ref
  165.6 0.6 collective-permute-start.17
  166.2 5.4 %collective-permute-done.6.refs_6_ = bf16[4,256,128]{2,1,0:T(8,128)(2,1)S(1)} collective-permute-done((bf16[4,256,128]{2,1,0:T(8,128)(2,1)}, bf16[4,256,128]{2,1,0:T(8,128)(2,1)S(1)}, u32[]{:S(2)}, u32[]{:S(2)}) %collective-permute-start.6) | collective-permute-done | bytes 262176 | tf_op jit(solution)/shard_map/ppermute | solution.py:365
  171.7 1.8 collective-permute-start.18
  173.6 6.4 %settle.3.refs_11_ = bf16[8,8,256,128]{3,2,1,0:T(8,128)(2,1)} custom-call(s32[2]{0:T(128)S(1)} %pad_add_fusion.meta_ref, bf16[4,256,128]{2,1,0:T(8,128)(2,1)S(1)} %copy-done.2, bf16[4,256,128]{2,1,0:T(8,128)(2,1)S(1)} %copy-done.4, bf16[4,256,128]{2,1,0:T(8,128)(2,1)S(1)} %copy-done.6, bf16[4,256,128]{2,1,0:T(8,128)(2,1)S(1)} %copy-done.8, ...), custom_call_target="tpu_custom_call" | custom-call | flops 2147483648 | bytes 10485760 | tf_op jit(solution)/shard_map/settle/pallas_call | solution.py:259
  179.9 0.0 collective-permute-done.7.refs_1_
  179.9 0.0 collective-permute-start.19
  179.9 0.0 collective-permute-done.8.refs_2_
  179.9 2.5 %collective-permute-start.20 = (bf16[2,2,256,128]{3,2,1,0:T(8,128)(2,1)}, bf16[2,2,256,128]{3,2,1,0:T(8,128)(2,1)}, u32[]{:S(2)}, u32[]{:S(2)}) collective-permute-start(bf16[2,2,256,128]{3,2,1,0:T(8,128)(2,1)} %get-tuple-element.91), channel_id=1, source_target_pairs={{0,112},{16,64},{32,80},{48,96},{64,48},{80,0},{96,16},{112,32},{1... | collective-permute-start | bytes 786440 | tf_op jit(solution)/shard_map/ppermute | solution.py:365
  182.5 0.0 collective-permute-done.9.refs_3_
  182.5 27.9 %all-to-all-done.2.got_ref = bf16[16,2,2,96,256]{4,3,2,1,0:T(8,128)(2,1)} async-done(((bf16[16,2,2,96,256]{4,3,2,1,0:T(8,128)(2,1)}), bf16[16,2,2,96,256]{4,3,2,1,0:T(8,128)(2,1)}, u32[]{:S(2)}, u32[]{:S(2)}) %all-to-all-start.2) | async-done | bytes 3145760 | tf_op jit(solution)/shard_map/all_to_all | solution.py:355
  210.4 8.0 %transform.5 = (bf16[2,256,128]{2,1,0:T(8,128)(2,1)}, bf16[2,256,128]{2,1,0:T(8,128)(2,1)}, bf16[2,256,128]{2,1,0:T(8,128)(2,1)}, bf16[2,256,128]{2,1,0:T(8,128)...) custom-call(s32[11]{0:T(128)S(1)} %get-tuple-element.94.meta_ref, ...), custom_call_target="tpu_custom_call" | custom-call | flops 2415919104 | bytes 9437184 | tf_op jit(solution)/shard_map/transform/pallas_call | solution.py:178
  218.4 0.1 collective-permute-start.10
  218.5 0.0 collective-permute-done.17.refs_4_
  218.5 3.9 %collective-permute-start.11 = (bf16[2,256,128]{2,1,0:T(8,128)(2,1)}, bf16[2,256,128]{2,1,0:T(8,128)(2,1)S(1)}, u32[]{:S(2)}, u32[]{:S(2)}) collective-permute-start(bf16[2,256,128]{2,1,0:T(8,128)(2,1)} %get-tuple-element.78), channel_id=1, source_target_pairs={{0,32},{16,48},{32,0},{48,16},{64,96},{80,112},{96,64},{112,80},{1... | collective-permute-start | bytes 393224 | tf_op jit(solution)/shard_map/ppermute | solution.py:365
  222.3 0.0 collective-permute-done.18.refs_5_
  222.4 0.0 collective-permute-start.12
  222.4 0.0 collective-permute-done.19.refs_6_
  222.4 1.5 collective-permute-start.13
  223.8 0.0 collective-permute-done.20.refs_7_
  223.8 2.0 collective-permute-start.14
  225.9 4.1 %collective-permute-start.15 = (bf16[2,256,128]{2,1,0:T(8,128)(2,1)}, bf16[2,256,128]{2,1,0:T(8,128)(2,1)S(1)}, u32[]{:S(2)}, u32[]{:S(2)}) collective-permute-start(bf16[2,256,128]{2,1,0:T(8,128)(2,1)} %get-tuple-element.82), channel_id=1, source_target_pairs={{0,96},{16,112},{32,64},{48,80},{64,32},{80,48},{96,0},{112,16},{1... | collective-permute-start | bytes 393224 | tf_op jit(solution)/shard_map/ppermute | solution.py:365
  229.9 1.6 collective-permute-start.16
  231.5 4.6 %settle.4.refs_11_ = bf16[8,8,256,128]{3,2,1,0:T(8,128)(2,1)} custom-call(s32[2]{0:T(128)S(1)} %pad_add_fusion.meta_ref, bf16[2,2,256,128]{3,2,1,0:T(8,128)(2,1)S(1)} %copy-done.1, bf16[2,2,256,128]{3,2,1,0:T(8,128)(2,1)S(1)} %collective-permute-done.7.refs_1_, ...), custom_call_target="tpu_custom_call", output_to_operand_aliasing={{}: (12, {})} | custom-call | flops 1073741824 | bytes 6291456 | tf_op jit(solution)/shard_map/settle/pallas_call | solution.py:259
  236.1 0.0 collective-permute-done.14.refs_5_
  236.1 0.1 collective-permute-done.16.refs_7_
  236.2 4.2 %settle.5 = bf16[8,8,256,128]{3,2,1,0:T(8,128)(2,1)} custom-call(s32[2]{0:T(128)S(1)} %pad_add_fusion.meta_ref, bf16[2,256,128]{2,1,0:T(8,128)(2,1)S(1)} %copy-done.15, bf16[2,256,128]{2,1,0:T(8,128)(2,1)S(1)} %collective-permute-done.10.refs_1_, bf16[2,256,128]{2,1,0:T(8,128)(2,1)S(1)} %collective-permute-done.11.refs_2_, ...), custom_call_target="tpu_custom_call", output_to_operand_aliasing={{}: (12, {})} | custom-call | flops 1073741824 | bytes 6291456 | tf_op jit(solution)/shard_map/settle/pallas_call | solution.py:259
  (39 shorter events, 0.1 us)
Async XLA Ops:
  93.7 8.1 %copy-start.18 = (s32[128]{0:T(128)S(1)}, s32[128]{0:T(128)}, u32[]{:S(2)}) copy-start(s32[128]{0:T(128)} %param.7) | copy-start | bytes 1540
  93.7 50.6 %all-to-all-start.1 = ((bf16[16,2,2,96,256]{4,3,2,1,0:T(8,128)(2,1)}), bf16[16,2,2,96,256]{4,3,2,1,0:T(8,128)(2,1)S(1)}, u32[]{:S(2)}, u32[]{:S(2)}) async-start(bf16[16,2,2,96,256]{4,3,2,1,0:T(8,128)(2,1)} %get-tuple-element.51), calls=%async_computation.1 | async-start | bytes 6291456 | tf_op jit(solution)/shard_map/all_to_all | solution.py:350
  115.7 13.8 %collective-permute-start = (bf16[4,256,128]{2,1,0:T(8,128)(2,1)}, bf16[4,256,128]{2,1,0:T(8,128)(2,1)S(1)}, u32[]{:S(2)}, u32[]{:S(2)}) collective-permute-start(bf16[4,256,128]{2,1,0:T(8,128)(2,1)} %get-tuple-element.54), channel_id=1, source_target_pairs={{0,16},{16,32},{32,48},{48,0},{64,80},{80,96},{96,112},{112,64},{1... | collective-permute-start | bytes 786440 | tf_op jit(solution)/shard_map/ppermute | solution.py:365
  117.3 12.9 %collective-permute-start.1 = (bf16[4,256,128]{2,1,0:T(8,128)(2,1)}, bf16[4,256,128]{2,1,0:T(8,128)(2,1)S(1)}, u32[]{:S(2)}, u32[]{:S(2)}) collective-permute-start(bf16[4,256,128]{2,1,0:T(8,128)(2,1)} %get-tuple-element.55), channel_id=1, source_target_pairs={{0,32},{16,48},{32,0},{48,16},{64,96},{80,112},{96,64},{112,80},{1... | collective-permute-start | bytes 786440 | tf_op jit(solution)/shard_map/ppermute | solution.py:365
  118.2 14.6 %collective-permute-start.2 = (bf16[4,256,128]{2,1,0:T(8,128)(2,1)}, bf16[4,256,128]{2,1,0:T(8,128)(2,1)S(1)}, u32[]{:S(2)}, u32[]{:S(2)}) collective-permute-start(bf16[4,256,128]{2,1,0:T(8,128)(2,1)} %get-tuple-element.56), channel_id=1, source_target_pairs={{0,48},{16,0},{32,16},{48,32},{64,112},{80,64},{96,80},{112,96},{1... | collective-permute-start | bytes 786440 | tf_op jit(solution)/shard_map/ppermute | solution.py:365
  120.7 12.9 %collective-permute-start.3 = (bf16[4,256,128]{2,1,0:T(8,128)(2,1)}, bf16[4,256,128]{2,1,0:T(8,128)(2,1)S(1)}, u32[]{:S(2)}, u32[]{:S(2)}) collective-permute-start(bf16[4,256,128]{2,1,0:T(8,128)(2,1)} %get-tuple-element.57), channel_id=1, source_target_pairs={{0,64},{16,80},{32,96},{48,112},{64,0},{80,16},{96,32},{112,48},{1... | collective-permute-start | bytes 786440 | tf_op jit(solution)/shard_map/ppermute | solution.py:365
  122.3 18.1 %collective-permute-start.4 = (bf16[4,256,128]{2,1,0:T(8,128)(2,1)}, bf16[4,256,128]{2,1,0:T(8,128)(2,1)S(1)}, u32[]{:S(2)}, u32[]{:S(2)}) collective-permute-start(bf16[4,256,128]{2,1,0:T(8,128)(2,1)} %get-tuple-element.58), channel_id=1, source_target_pairs={{0,80},{16,96},{32,112},{48,64},{64,16},{80,32},{96,48},{112,0},{1... | collective-permute-start | bytes 786440 | tf_op jit(solution)/shard_map/ppermute | solution.py:365
  129.5 0.7 copy-start.3
  130.2 12.0 %collective-permute-start.5 = (bf16[4,256,128]{2,1,0:T(8,128)(2,1)}, bf16[4,256,128]{2,1,0:T(8,128)(2,1)S(1)}, u32[]{:S(2)}, u32[]{:S(2)}) collective-permute-start(bf16[4,256,128]{2,1,0:T(8,128)(2,1)} %get-tuple-element.59), channel_id=1, source_target_pairs={{0,112},{16,64},{32,80},{48,96},{64,48},{80,0},{96,16},{112,32},{1... | collective-permute-start | bytes 786440 | tf_op jit(solution)/shard_map/ppermute | solution.py:365
  130.2 0.7 copy-start.5
  132.8 0.7 copy-start.7
  133.6 0.7 copy-start.9
  140.4 0.7 copy-start.11
  142.2 0.7 copy-start.13
  144.3 9.2 %copy-start.17 = (bf16[16,2,2,96,256]{4,3,2,1,0:T(8,128)(2,1)}, bf16[16,2,2,96,256]{4,3,2,1,0:T(8,128)(2,1)S(1)}, u32[]{:S(2)}) copy-start(bf16[16,2,2,96,256]{4,3,2,1,0:T(8,128)(2,1)S(1)} %all-to-all-done.1.got_ref) | copy-start | bytes 9437188
  144.3 66.1 %all-to-all-start.2 = ((bf16[16,2,2,96,256]{4,3,2,1,0:T(8,128)(2,1)}), bf16[16,2,2,96,256]{4,3,2,1,0:T(8,128)(2,1)}, u32[]{:S(2)}, u32[]{:S(2)}) async-start(bf16[16,2,2,96,256]{4,3,2,1,0:T(8,128)(2,1)} %get-tuple-element.61), calls=%async_computation.2 | async-start | bytes 6291456 | tf_op jit(solution)/shard_map/all_to_all | solution.py:355
  150.3 21.3 %collective-permute-start.6 = (bf16[4,256,128]{2,1,0:T(8,128)(2,1)}, bf16[4,256,128]{2,1,0:T(8,128)(2,1)S(1)}, u32[]{:S(2)}, u32[]{:S(2)}) collective-permute-start(bf16[4,256,128]{2,1,0:T(8,128)(2,1)} %get-tuple-element.62), channel_id=1, source_target_pairs={{0,96},{16,112},{32,64},{48,80},{64,32},{80,48},{96,0},{112,16},{1... | collective-permute-start | bytes 786440 | tf_op jit(solution)/shard_map/ppermute | solution.py:365
  153.5 20.0 %copy-start = (bf16[4,4,256,256]{3,2,1,0:T(8,128)(2,1)S(1)}, bf16[4,4,256,256]{3,2,1,0:T(8,128)(2,1)}, u32[]{:S(2)}) copy-start(bf16[4,4,256,256]{3,2,1,0:T(8,128)(2,1)} %refs_10_.5) | copy-start | bytes 6291460
  153.5 20.0 %copy-start.2 = (bf16[4,256,128]{2,1,0:T(8,128)(2,1)S(1)}, bf16[4,256,128]{2,1,0:T(8,128)(2,1)}, u32[]{:S(2)}) copy-start(bf16[4,256,128]{2,1,0:T(8,128)(2,1)} %get-tuple-element.68.refs_0_) | copy-start | bytes 786436
  153.5 20.0 %copy-start.4 = (bf16[4,256,128]{2,1,0:T(8,128)(2,1)S(1)}, bf16[4,256,128]{2,1,0:T(8,128)(2,1)}, u32[]{:S(2)}) copy-start(bf16[4,256,128]{2,1,0:T(8,128)(2,1)} %copy-done.3) | copy-start | bytes 786436
  153.5 20.0 %copy-start.6 = (bf16[4,256,128]{2,1,0:T(8,128)(2,1)S(1)}, bf16[4,256,128]{2,1,0:T(8,128)(2,1)}, u32[]{:S(2)}) copy-start(bf16[4,256,128]{2,1,0:T(8,128)(2,1)} %copy-done.5) | copy-start | bytes 786436
  153.5 20.0 %copy-start.8 = (bf16[4,256,128]{2,1,0:T(8,128)(2,1)S(1)}, bf16[4,256,128]{2,1,0:T(8,128)(2,1)}, u32[]{:S(2)}) copy-start(bf16[4,256,128]{2,1,0:T(8,128)(2,1)} %copy-done.7) | copy-start | bytes 786436
  153.5 20.0 %copy-start.10 = (bf16[4,256,128]{2,1,0:T(8,128)(2,1)S(1)}, bf16[4,256,128]{2,1,0:T(8,128)(2,1)}, u32[]{:S(2)}) copy-start(bf16[4,256,128]{2,1,0:T(8,128)(2,1)} %copy-done.9) | copy-start | bytes 786436
  153.5 20.0 %copy-start.12 = (bf16[4,256,128]{2,1,0:T(8,128)(2,1)S(1)}, bf16[4,256,128]{2,1,0:T(8,128)(2,1)}, u32[]{:S(2)}) copy-start(bf16[4,256,128]{2,1,0:T(8,128)(2,1)} %copy-done.11) | copy-start | bytes 786436
  153.6 20.0 %copy-start.14 = (bf16[4,256,128]{2,1,0:T(8,128)(2,1)S(1)}, bf16[4,256,128]{2,1,0:T(8,128)(2,1)}, u32[]{:S(2)}) copy-start(bf16[4,256,128]{2,1,0:T(8,128)(2,1)} %copy-done.13) | copy-start | bytes 786436
  153.6 20.0 %copy-start.16 = (s32[8,128]{1,0:T(8,128)S(1)}, s32[8,128]{1,0:T(8,128)}, u32[]{:S(2)}) copy-start(s32[8,128]{1,0:T(8,128)} %refs_9_.5) | copy-start | bytes 12292
  161.6 18.3 %collective-permute-start.7 = (bf16[2,2,256,128]{3,2,1,0:T(8,128)(2,1)}, bf16[2,2,256,128]{3,2,1,0:T(8,128)(2,1)S(1)}, u32[]{:S(2)}, u32[]{:S(2)}) collective-permute-start(bf16[2,2,256,128]{3,2,1,0:T(8,128)(2,1)} %get-tuple-element.65), channel_id=1, source_target_pairs={{0,16},{16,32},{32,48},{48,0},{64,80},{80,96},{96,112},{112,64},{1... | collective-permute-start | bytes 786440 | tf_op jit(solution)/shard_map/ppermute | solution.py:365
  161.7 18.3 %collective-permute-start.8 = (bf16[2,2,256,128]{3,2,1,0:T(8,128)(2,1)}, bf16[2,2,256,128]{3,2,1,0:T(8,128)(2,1)S(1)}, u32[]{:S(2)}, u32[]{:S(2)}) collective-permute-start(bf16[2,2,256,128]{3,2,1,0:T(8,128)(2,1)} %get-tuple-element.66), channel_id=1, source_target_pairs={{0,32},{16,48},{32,0},{48,16},{64,96},{80,112},{96,64},{112,80},{1... | collective-permute-start | bytes 786440 | tf_op jit(solution)/shard_map/ppermute | solution.py:365
  165.1 17.4 %collective-permute-start.9 = (bf16[2,2,256,128]{3,2,1,0:T(8,128)(2,1)}, bf16[2,2,256,128]{3,2,1,0:T(8,128)(2,1)S(1)}, u32[]{:S(2)}, u32[]{:S(2)}) collective-permute-start(bf16[2,2,256,128]{3,2,1,0:T(8,128)(2,1)} %get-tuple-element.67), channel_id=1, source_target_pairs={{0,48},{16,0},{32,16},{48,32},{64,112},{80,64},{96,80},{112,96},{1... | collective-permute-start | bytes 786440 | tf_op jit(solution)/shard_map/ppermute | solution.py:365
  165.6 52.9 %collective-permute-start.17 = (bf16[2,2,256,128]{3,2,1,0:T(8,128)(2,1)}, bf16[2,2,256,128]{3,2,1,0:T(8,128)(2,1)S(1)}, u32[]{:S(2)}, u32[]{:S(2)}) collective-permute-start(bf16[2,2,256,128]{3,2,1,0:T(8,128)(2,1)} %get-tuple-element.88), channel_id=1, source_target_pairs={{0,64},{16,80},{32,96},{48,112},{64,0},{80,16},{96,32},{112,48},{1... | collective-permute-start | bytes 786440 | tf_op jit(solution)/shard_map/ppermute | solution.py:365
  171.7 50.7 %collective-permute-start.18 = (bf16[2,2,256,128]{3,2,1,0:T(8,128)(2,1)}, bf16[2,2,256,128]{3,2,1,0:T(8,128)(2,1)S(1)}, u32[]{:S(2)}, u32[]{:S(2)}) collective-permute-start(bf16[2,2,256,128]{3,2,1,0:T(8,128)(2,1)} %get-tuple-element.89), channel_id=1, source_target_pairs={{0,80},{16,96},{32,112},{48,64},{64,16},{80,32},{96,48},{112,0},{1... | collective-permute-start | bytes 786440 | tf_op jit(solution)/shard_map/ppermute | solution.py:365
  179.9 42.4 %collective-permute-start.19 = (bf16[2,2,256,128]{3,2,1,0:T(8,128)(2,1)}, bf16[2,2,256,128]{3,2,1,0:T(8,128)(2,1)}, u32[]{:S(2)}, u32[]{:S(2)}) collective-permute-start(bf16[2,2,256,128]{3,2,1,0:T(8,128)(2,1)} %get-tuple-element.90), channel_id=1, source_target_pairs={{0,96},{16,112},{32,64},{48,80},{64,32},{80,48},{96,0},{112,16},{1... | collective-permute-start | bytes 786440 | tf_op jit(solution)/shard_map/ppermute | solution.py:365
  179.9 43.9 %collective-permute-start.20 = (bf16[2,2,256,128]{3,2,1,0:T(8,128)(2,1)}, bf16[2,2,256,128]{3,2,1,0:T(8,128)(2,1)}, u32[]{:S(2)}, u32[]{:S(2)}) collective-permute-start(bf16[2,2,256,128]{3,2,1,0:T(8,128)(2,1)} %get-tuple-element.91), channel_id=1, source_target_pairs={{0,112},{16,64},{32,80},{48,96},{64,48},{80,0},{96,16},{112,32},{1... | collective-permute-start | bytes 786440 | tf_op jit(solution)/shard_map/ppermute | solution.py:365
  210.4 21.2 %copy-start.1 = (bf16[2,2,256,128]{3,2,1,0:T(8,128)(2,1)S(1)}, bf16[2,2,256,128]{3,2,1,0:T(8,128)(2,1)}, u32[]{:S(2)}) copy-start(bf16[2,2,256,128]{3,2,1,0:T(8,128)(2,1)} %get-tuple-element.84.refs_0_) | copy-start | bytes 786436
  218.4 7.4 %collective-permute-start.10 = (bf16[2,256,128]{2,1,0:T(8,128)(2,1)}, bf16[2,256,128]{2,1,0:T(8,128)(2,1)S(1)}, u32[]{:S(2)}, u32[]{:S(2)}) collective-permute-start(bf16[2,256,128]{2,1,0:T(8,128)(2,1)} %get-tuple-element.77), channel_id=1, source_target_pairs={{0,16},{16,32},{32,48},{48,0},{64,80},{80,96},{96,112},{112,64},{1... | collective-permute-start | bytes 393224 | tf_op jit(solution)/shard_map/ppermute | solution.py:365
  218.5 11.4 %collective-permute-start.11 = (bf16[2,256,128]{2,1,0:T(8,128)(2,1)}, bf16[2,256,128]{2,1,0:T(8,128)(2,1)S(1)}, u32[]{:S(2)}, u32[]{:S(2)}) collective-permute-start(bf16[2,256,128]{2,1,0:T(8,128)(2,1)} %get-tuple-element.78), channel_id=1, source_target_pairs={{0,32},{16,48},{32,0},{48,16},{64,96},{80,112},{96,64},{112,80},{1... | collective-permute-start | bytes 393224 | tf_op jit(solution)/shard_map/ppermute | solution.py:365
  222.4 13.7 %collective-permute-start.12 = (bf16[2,256,128]{2,1,0:T(8,128)(2,1)}, bf16[2,256,128]{2,1,0:T(8,128)(2,1)S(1)}, u32[]{:S(2)}, u32[]{:S(2)}) collective-permute-start(bf16[2,256,128]{2,1,0:T(8,128)(2,1)} %get-tuple-element.79), channel_id=1, source_target_pairs={{0,48},{16,0},{32,16},{48,32},{64,112},{80,64},{96,80},{112,96},{1... | collective-permute-start | bytes 393224 | tf_op jit(solution)/shard_map/ppermute | solution.py:365
  222.4 13.7 %collective-permute-start.13 = (bf16[2,256,128]{2,1,0:T(8,128)(2,1)}, bf16[2,256,128]{2,1,0:T(8,128)(2,1)S(1)}, u32[]{:S(2)}, u32[]{:S(2)}) collective-permute-start(bf16[2,256,128]{2,1,0:T(8,128)(2,1)} %get-tuple-element.80), channel_id=1, source_target_pairs={{0,64},{16,80},{32,96},{48,112},{64,0},{80,16},{96,32},{112,48},{1... | collective-permute-start | bytes 393224 | tf_op jit(solution)/shard_map/ppermute | solution.py:365
  223.8 12.3 %collective-permute-start.14 = (bf16[2,256,128]{2,1,0:T(8,128)(2,1)}, bf16[2,256,128]{2,1,0:T(8,128)(2,1)S(1)}, u32[]{:S(2)}, u32[]{:S(2)}) collective-permute-start(bf16[2,256,128]{2,1,0:T(8,128)(2,1)} %get-tuple-element.81), channel_id=1, source_target_pairs={{0,80},{16,96},{32,112},{48,64},{64,16},{80,32},{96,48},{112,0},{1... | collective-permute-start | bytes 393224 | tf_op jit(solution)/shard_map/ppermute | solution.py:365
  225.9 10.3 %collective-permute-start.15 = (bf16[2,256,128]{2,1,0:T(8,128)(2,1)}, bf16[2,256,128]{2,1,0:T(8,128)(2,1)S(1)}, u32[]{:S(2)}, u32[]{:S(2)}) collective-permute-start(bf16[2,256,128]{2,1,0:T(8,128)(2,1)} %get-tuple-element.82), channel_id=1, source_target_pairs={{0,96},{16,112},{32,64},{48,80},{64,32},{80,48},{96,0},{112,16},{1... | collective-permute-start | bytes 393224 | tf_op jit(solution)/shard_map/ppermute | solution.py:365
  229.9 6.3 %copy-start.15 = (bf16[2,256,128]{2,1,0:T(8,128)(2,1)S(1)}, bf16[2,256,128]{2,1,0:T(8,128)(2,1)}, u32[]{:S(2)}) copy-start(bf16[2,256,128]{2,1,0:T(8,128)(2,1)} %get-tuple-element.76.refs_0_) | copy-start | bytes 393220
  229.9 6.3 %collective-permute-start.16 = (bf16[2,256,128]{2,1,0:T(8,128)(2,1)}, bf16[2,256,128]{2,1,0:T(8,128)(2,1)S(1)}, u32[]{:S(2)}, u32[]{:S(2)}) collective-permute-start(bf16[2,256,128]{2,1,0:T(8,128)(2,1)} %get-tuple-element.83), channel_id=1, source_target_pairs={{0,112},{16,64},{32,80},{48,96},{64,48},{80,0},{96,16},{112,32},{1... | collective-permute-start | bytes 393224 | tf_op jit(solution)/shard_map/ppermute | solution.py:365

commit v7 on v4

--- a/solution.py
+++ b/solution.py
@@ -10,7 +10,7 @@
 ZS, Y = 2, 4
 CHUNKS = (4, 2, 2)
 FLIPPED = (False, True, True)
-TIES = {2: ((0, (0, 1, 2, 3, 4, 5, 7)),), 3: ((0, (6,)), (1, range(8)))}
+TIES = {2: ((0, (0, 1, 2, 3, 4, 5, 7)),), 3: ((0, (6,)), (1, (0, 1, 2, 3, 5, 6, 7)))}
 ORDER = (6, 2, 5, 7, 1, 3, 4)
 STEP = 16
 BF16, F32 = jnp.bfloat16, jnp.float32

time: 241 us -> 240 us (level)
  starting transfers between devices: 50.3 us -> 54.4 us
  waiting for transfers between devices: 41.1 us -> 37.6 us
    ppermute x21, starting transfers between devices: 37.9 us -> 42 us  [on_device(): moved[h] = lax.ppermute(parts[h], 'rad', rad_targets(h // Y, h % Y))]
    ppermute x21, waiting for transfers between devices: 39.8 us -> 36.3 us  [on_device(): moved[h] = lax.ppermute(parts[h], 'rad', rad_targets(h // Y, h % Y))]
    unnamed x46 -> x42, local copies, waits for them, and re-layouts: 5.71 us -> 5 us
  transfers between devices with their start and end apart: 23 -> 23, of which waited for: 13 -> 12; matrix products, arithmetic and copies ran while one was open for 0% -> 0% of each run, Pallas kernels for 14% -> 17%
where the time goes in v7:
time: 240 us; the launch traced here: 236 us
  blocking collectives  76.8 us (32%)
  Pallas kernels  60.5 us (25%)
  starting transfers between devices  54.4 us (23%)
  waiting for transfers between devices  37.6 us (16%)
  local copies, waits for them, and re-layouts  5.21 us (2%)
    all_to_all x1, blocking collectives, on_device(): gots.append(lax.all_to_all(send, 'lat', 0, 0, tiled=True))  76.8 us
    ppermute x21, starting transfers between devices, on_device(): moved[h] = lax.ppermute(parts[h], 'rad', rad_targets(h // Y, h % Y))  42 us
    ppermute x21, waiting for transfers between devices, on_device(): moved[h] = lax.ppermute(parts[h], 'rad', rad_targets(h // Y, h % Y))  36.3 us
    pallas_call x3, Pallas kernels, transform(): pl.pallas_call(kernel, grid_spec=pltpu.PrefetchScalarGridSpec(num_scalar_...  29.3 us
    pallas_call x1, Pallas kernels, prep(): pl.pallas_call(functools.partial(prep_kernel, starts, per_dev), grid=(lat...  16 us
    pallas_call x3, Pallas kernels, settle(): pl.pallas_call(functools.partial(kernel, first, flipped), grid_spec=pltpu...  15.3 us
    all_to_all x2, starting transfers between devices, on_device(): lax.all_to_all(send, ('rad', 'lat'), 0, 0, tiled=True, axis_index_groups=...  12.4 us
    unnamed x42, local copies, waits for them, and re-layouts  5 us
  transfers between devices with their start and end apart: 23, of which 12 were waited for; matrix products, arithmetic and copies ran while one was open for 0% of the time, Pallas kernels for 17%

profile of v7, /device:TPU:74, one launch (start us, length us, event | category | flops | bytes accessed | tf_op | source)
XLA Modules:
  0.0 235.9 jit_solution(10703513264331256587)
XLA Ops:
  0.0 0.7 broadcast_multiply_fusion
  0.7 0.1 iota_add_fusion
  0.7 0.1 add.69.key_ref
  0.9 16.0 %prep.1 = (bf16[16,4,2,96,256]{4,3,2,1,0:T(8,128)(2,1)}, bf16[16,2,2,96,256]{4,3,2,1,0:T(8,128)(2,1)}, bf16[16,2,2,96,256]{4,3,2,1,0:T(8,128)(2,1)}) custom-call(s32[1,256]{1,0:T(1,128)S(1)} %add.69.key_ref, bf16[256,96,256]{2,1,0:T(8,128)(2,1)} %bitcast.8), custom_call_target="tpu_custom_call" | custom-call | flops 9663676416 | bytes 25165824 | tf_op jit(solution)/shard_map/prep/pallas_call | solution.py:72
  16.8 76.8 %all_to_all.15.got_ref = bf16[16,4,2,96,256]{4,3,2,1,0:T(8,128)(2,1)} all-to-all(bf16[16,4,2,96,256]{4,3,2,1,0:T(8,128)(2,1)} %get-tuple-element.52), channel_id=1, replica_groups=mesh['rad'=8,'lat'=16] {'lat'}, dimensions={0} | all-to-all | bytes 12582912 | tf_op jit(solution)/shard_map/all_to_all | solution.py:355
  93.7 8.0 %all-to-all-start.1 = ((bf16[16,2,2,96,256]{4,3,2,1,0:T(8,128)(2,1)}), bf16[16,2,2,96,256]{4,3,2,1,0:T(8,128)(2,1)S(1)}, u32[]{:S(2)}, u32[]{:S(2)}) async-start(bf16[16,2,2,96,256]{4,3,2,1,0:T(8,128)(2,1)} %get-tuple-element.54), calls=%async_computation.1 | async-start | bytes 6291456 | tf_op jit(solution)/shard_map/all_to_all | solution.py:350
  101.8 0.2 select_reduce_fusion
  102.0 0.1 pad_add_fusion.3.meta_ref
  102.0 13.6 %transform.3 = (bf16[4,256,128]{2,1,0:T(8,128)(2,1)}, bf16[4,256,128]{2,1,0:T(8,128)(2,1)}, bf16[4,256,128]{2,1,0:T(8,128)(2,1)}, bf16[4,256,128]{2,1,0:T(8,128)...) custom-call(s32[13]{0:T(128)S(1)} %pad_add_fusion.3.meta_ref, ...), custom_call_target="tpu_custom_call" | custom-call | flops 4831838208 | bytes 18874368 | tf_op jit(solution)/shard_map/transform/pallas_call | solution.py:178
  115.7 1.6 collective-permute-start
  117.3 0.9 collective-permute-start.1
  118.2 2.4 %collective-permute-start.2 = (bf16[4,256,128]{2,1,0:T(8,128)(2,1)}, bf16[4,256,128]{2,1,0:T(8,128)(2,1)S(1)}, u32[]{:S(2)}, u32[]{:S(2)}) collective-permute-start(bf16[4,256,128]{2,1,0:T(8,128)(2,1)} %get-tuple-element.59), channel_id=1, source_target_pairs={{0,48},{16,0},{32,16},{48,32},{64,112},{80,64},{96,80},{112,96},{1... | collective-permute-start | bytes 786440 | tf_op jit(solution)/shard_map/ppermute | solution.py:365
  120.7 1.6 collective-permute-start.3
  122.3 7.2 %collective-permute-done.refs_1_ = bf16[4,256,128]{2,1,0:T(8,128)(2,1)S(1)} collective-permute-done((bf16[4,256,128]{2,1,0:T(8,128)(2,1)}, bf16[4,256,128]{2,1,0:T(8,128)(2,1)S(1)}, u32[]{:S(2)}, u32[]{:S(2)}) %collective-permute-start) | collective-permute-done | bytes 262176 | tf_op jit(solution)/shard_map/ppermute | solution.py:365
  129.5 0.7 copy-done.6
  130.2 0.0 collective-permute-start.5
  130.2 0.0 collective-permute-done.1.refs_2_
  130.2 0.7 copy-done.8
  130.9 1.9 collective-permute-done.2.refs_3_
  132.8 0.7 copy-done.10
  133.5 0.7 copy-done.12
  134.3 6.1 %collective-permute-done.4.refs_5_ = bf16[4,256,128]{2,1,0:T(8,128)(2,1)S(1)} collective-permute-done((bf16[4,256,128]{2,1,0:T(8,128)(2,1)}, bf16[4,256,128]{2,1,0:T(8,128)(2,1)S(1)}, u32[]{:S(2)}, u32[]{:S(2)}) %collective-permute-start.4) | collective-permute-done | bytes 262176 | tf_op jit(solution)/shard_map/ppermute | solution.py:365
  140.4 0.7 copy-done.14
  141.1 1.1 collective-permute-done.5.refs_7_
  142.2 0.7 copy-done.16
  142.9 1.3 all-to-all-done.1.got_ref
  144.3 4.4 %all-to-all-start.2 = ((bf16[16,2,2,96,256]{4,3,2,1,0:T(8,128)(2,1)}), bf16[16,2,2,96,256]{4,3,2,1,0:T(8,128)(2,1)}, u32[]{:S(2)}, u32[]{:S(2)}) async-start(bf16[16,2,2,96,256]{4,3,2,1,0:T(8,128)(2,1)} %get-tuple-element.64), calls=%async_computation.2 | async-start | bytes 6291456 | tf_op jit(solution)/shard_map/all_to_all | solution.py:350
  148.7 0.1 fusion.4
  148.8 0.1 pad_add_fusion.4
  148.8 4.4 %collective-permute-start.6 = (bf16[4,256,128]{2,1,0:T(8,128)(2,1)}, bf16[4,256,128]{2,1,0:T(8,128)(2,1)S(1)}, u32[]{:S(2)}, u32[]{:S(2)}) collective-permute-start(bf16[4,256,128]{2,1,0:T(8,128)(2,1)} %get-tuple-element.65), channel_id=1, source_target_pairs={{0,96},{16,112},{32,64},{48,80},{64,32},{80,48},{96,0},{112,16},{1... | collective-permute-start | bytes 786440 | tf_op jit(solution)/shard_map/ppermute | solution.py:365
  153.3 0.0 copy-start.18
  153.3 8.0 %transform.4 = (bf16[2,2,256,128]{3,2,1,0:T(8,128)(2,1)}, bf16[2,2,256,128]{3,2,1,0:T(8,128)(2,1)}, bf16[2,2,256,128]{3,2,1,0:T(8,128)(2,1)}, bf16[2,2,256,128]{...) custom-call(s32[11]{0:T(128)S(1)} %get-tuple-element.99.meta_ref, ...), custom_call_target="tpu_custom_call" | custom-call | flops 2415919104 | bytes 9437184 | tf_op jit(solution)/shard_map/transform/pallas_call | solution.py:178
  161.3 0.1 collective-permute-start.7
  161.4 3.4 %collective-permute-start.8 = (bf16[2,2,256,128]{3,2,1,0:T(8,128)(2,1)}, bf16[2,2,256,128]{3,2,1,0:T(8,128)(2,1)S(1)}, u32[]{:S(2)}, u32[]{:S(2)}) collective-permute-start(bf16[2,2,256,128]{3,2,1,0:T(8,128)(2,1)} %get-tuple-element.69), channel_id=1, source_target_pairs={{0,32},{16,48},{32,0},{48,16},{64,96},{80,112},{96,64},{112,80},{1... | collective-permute-start | bytes 786440 | tf_op jit(solution)/shard_map/ppermute | solution.py:365
  164.8 0.5 collective-permute-start.9
  165.2 0.4 collective-permute-start.10
  165.6 0.0 collective-permute-done.6.refs_6_
  165.6 3.5 %collective-permute-start.11 = (bf16[2,2,256,128]{3,2,1,0:T(8,128)(2,1)}, bf16[2,2,256,128]{3,2,1,0:T(8,128)(2,1)S(1)}, u32[]{:S(2)}, u32[]{:S(2)}) collective-permute-start(bf16[2,2,256,128]{3,2,1,0:T(8,128)(2,1)} %get-tuple-element.72), channel_id=1, source_target_pairs={{0,96},{16,112},{32,64},{48,80},{64,32},{80,48},{96,0},{112,16},{1... | collective-permute-start | bytes 786440 | tf_op jit(solution)/shard_map/ppermute | solution.py:365
  169.1 1.6 collective-permute-done.7.refs_1_
  170.8 6.6 %collective-permute-start.12 = (bf16[2,2,256,128]{3,2,1,0:T(8,128)(2,1)}, bf16[2,2,256,128]{3,2,1,0:T(8,128)(2,1)S(1)}, u32[]{:S(2)}, u32[]{:S(2)}) collective-permute-start(bf16[2,2,256,128]{3,2,1,0:T(8,128)(2,1)} %get-tuple-element.73), channel_id=1, source_target_pairs={{0,112},{16,64},{32,80},{48,96},{64,48},{80,0},{96,16},{112,32},{1... | collective-permute-start | bytes 786440 | tf_op jit(solution)/shard_map/ppermute | solution.py:365
  177.4 0.1 pad_add_fusion.meta_ref
  177.5 6.4 %settle.3.refs_11_ = bf16[8,8,256,128]{3,2,1,0:T(8,128)(2,1)} custom-call(s32[2]{0:T(128)S(1)} %pad_add_fusion.meta_ref, bf16[4,256,128]{2,1,0:T(8,128)(2,1)S(1)} %copy-done.5, bf16[4,256,128]{2,1,0:T(8,128)(2,1)S(1)} %copy-done.7, bf16[4,256,128]{2,1,0:T(8,128)(2,1)S(1)} %copy-done.9, bf16[4,256,128]{2,1,0:T(8,128)(2,1)S(1)} %copy-done.11, ...), custom_call_target="tpu_custom_call" | custom-call | flops 2147483648 | bytes 10485760 | tf_op jit(solution)/shard_map/settle/pallas_call | solution.py:259
  183.9 0.0 collective-permute-done.8.refs_2_
  183.9 3.0 %collective-permute-start.20 = (bf16[2,2,256,128]{3,2,1,0:T(8,128)(2,1)}, bf16[2,2,256,128]{3,2,1,0:T(8,128)(2,1)}, u32[]{:S(2)}, u32[]{:S(2)}) collective-permute-start(bf16[2,2,256,128]{3,2,1,0:T(8,128)(2,1)} %get-tuple-element.94), channel_id=1, source_target_pairs={{0,64},{16,80},{32,96},{48,112},{64,0},{80,16},{96,32},{112,48},{1... | collective-permute-start | bytes 786440 | tf_op jit(solution)/shard_map/ppermute | solution.py:365
  186.9 0.0 collective-permute-done.9.refs_3_
  186.9 1.4 collective-permute-done.10.refs_5_
  188.3 0.8 collective-permute-done.11.refs_6_
  189.1 3.3 %collective-permute-done.12.refs_7_ = bf16[2,2,256,128]{3,2,1,0:T(8,128)(2,1)S(1)} collective-permute-done((bf16[2,2,256,128]{3,2,1,0:T(8,128)(2,1)}, bf16[2,2,256,128]{3,2,1,0:T(8,128)(2,1)S(1)}, u32[]{:S(2)}, u32[]{:S(2)}) %collective-permute-start.12) | collective-permute-done | bytes 262176 | tf_op jit(solution)/shard_map/ppermute | solution.py:365
  192.3 0.7 copy-done.2
  193.0 0.0 all-to-all-done.2.got_ref
  193.1 7.7 %transform.5 = (bf16[2,2,256,128]{3,2,1,0:T(8,128)(2,1)}, bf16[2,2,256,128]{3,2,1,0:T(8,128)(2,1)}, bf16[2,2,256,128]{3,2,1,0:T(8,128)(2,1)}, bf16[2,2,256,128]{...) custom-call(s32[11]{0:T(128)S(1)} %get-tuple-element.100.meta_ref, ...), custom_call_target="tpu_custom_call" | custom-call | flops 2415919104 | bytes 9437184 | tf_op jit(solution)/shard_map/transform/pallas_call | solution.py:178
  200.7 4.0 %collective-permute-start.13 = (bf16[2,2,256,128]{3,2,1,0:T(8,128)(2,1)}, bf16[2,2,256,128]{3,2,1,0:T(8,128)(2,1)S(1)}, u32[]{:S(2)}, u32[]{:S(2)}) collective-permute-start(bf16[2,2,256,128]{3,2,1,0:T(8,128)(2,1)} %get-tuple-element.83), channel_id=1, source_target_pairs={{0,16},{16,32},{32,48},{48,0},{64,80},{80,96},{96,112},{112,64},{1... | collective-permute-start | bytes 786440 | tf_op jit(solution)/shard_map/ppermute | solution.py:365
  204.8 0.0 collective-permute-start.14
  204.8 2.2 collective-permute-start.15
  206.9 2.0 collective-permute-start.16
  208.9 0.0 collective-permute-done.20.refs_4_
  208.9 8.1 %collective-permute-done.13.refs_1_ = bf16[2,2,256,128]{3,2,1,0:T(8,128)(2,1)S(1)} collective-permute-done((bf16[2,2,256,128]{3,2,1,0:T(8,128)(2,1)}, bf16[2,2,256,128]{3,2,1,0:T(8,128)(2,1)S(1)}, u32[]{:S(2)}, u32[]{:S(2)}) %collective-permute-start.13) | collective-permute-done | bytes 262176 | tf_op jit(solution)/shard_map/ppermute | solution.py:365
  217.0 0.0 collective-permute-start.18
  217.0 0.0 collective-permute-done.14.refs_2_
  217.0 5.3 %collective-permute-start.19 = (bf16[2,2,256,128]{3,2,1,0:T(8,128)(2,1)}, bf16[2,2,256,128]{3,2,1,0:T(8,128)(2,1)S(1)}, u32[]{:S(2)}, u32[]{:S(2)}) collective-permute-start(bf16[2,2,256,128]{3,2,1,0:T(8,128)(2,1)} %get-tuple-element.89), channel_id=1, source_target_pairs={{0,112},{16,64},{32,80},{48,96},{64,48},{80,0},{96,16},{112,32},{1... | collective-permute-start | bytes 786440 | tf_op jit(solution)/shard_map/ppermute | solution.py:365
  222.4 4.5 %settle.4.refs_11_ = bf16[8,8,256,128]{3,2,1,0:T(8,128)(2,1)} custom-call(s32[2]{0:T(128)S(1)} %pad_add_fusion.meta_ref, bf16[2,2,256,128]{3,2,1,0:T(8,128)(2,1)S(1)} %copy-done.1, bf16[2,2,256,128]{3,2,1,0:T(8,128)(2,1)S(1)} %collective-permute-done.7.refs_1_, ...), custom_call_target="tpu_custom_call", output_to_operand_aliasing={{}: (12, {})} | custom-call | flops 1073741824 | bytes 6291456 | tf_op jit(solution)/shard_map/settle/pallas_call | solution.py:259
  226.8 3.1 %collective-permute-done.16.refs_4_ = bf16[2,2,256,128]{3,2,1,0:T(8,128)(2,1)S(1)} collective-permute-done((bf16[2,2,256,128]{3,2,1,0:T(8,128)(2,1)}, bf16[2,2,256,128]{3,2,1,0:T(8,128)(2,1)S(1)}, u32[]{:S(2)}, u32[]{:S(2)}) %collective-permute-start.16) | collective-permute-done | bytes 262176 | tf_op jit(solution)/shard_map/ppermute | solution.py:365
  230.0 1.5 collective-permute-done.19.refs_7_
  231.5 4.4 %settle.5 = bf16[8,8,256,128]{3,2,1,0:T(8,128)(2,1)} custom-call(s32[2]{0:T(128)S(1)} %pad_add_fusion.meta_ref, bf16[2,2,256,128]{3,2,1,0:T(8,128)(2,1)S(1)} %copy-done.4, bf16[2,2,256,128]{3,2,1,0:T(8,128)(2,1)S(1)} %collective-permute-done.13.refs_1_, ...), custom_call_target="tpu_custom_call", output_to_operand_aliasing={{}: (12, {})} | custom-call | flops 1073741824 | bytes 6291456 | tf_op jit(solution)/shard_map/settle/pallas_call | solution.py:259
  (43 shorter events, 0.1 us)
Async XLA Ops:
  93.7 8.1 %copy-start.20 = (s32[128]{0:T(128)S(1)}, s32[128]{0:T(128)}, u32[]{:S(2)}) copy-start(s32[128]{0:T(128)} %param.7) | copy-start | bytes 1540
  93.7 50.6 %all-to-all-start.1 = ((bf16[16,2,2,96,256]{4,3,2,1,0:T(8,128)(2,1)}), bf16[16,2,2,96,256]{4,3,2,1,0:T(8,128)(2,1)S(1)}, u32[]{:S(2)}, u32[]{:S(2)}) async-start(bf16[16,2,2,96,256]{4,3,2,1,0:T(8,128)(2,1)} %get-tuple-element.54), calls=%async_computation.1 | async-start | bytes 6291456 | tf_op jit(solution)/shard_map/all_to_all | solution.py:350
  115.7 13.8 %collective-permute-start = (bf16[4,256,128]{2,1,0:T(8,128)(2,1)}, bf16[4,256,128]{2,1,0:T(8,128)(2,1)S(1)}, u32[]{:S(2)}, u32[]{:S(2)}) collective-permute-start(bf16[4,256,128]{2,1,0:T(8,128)(2,1)} %get-tuple-element.57), channel_id=1, source_target_pairs={{0,16},{16,32},{32,48},{48,0},{64,80},{80,96},{96,112},{112,64},{1... | collective-permute-start | bytes 786440 | tf_op jit(solution)/shard_map/ppermute | solution.py:365
  117.3 12.9 %collective-permute-start.1 = (bf16[4,256,128]{2,1,0:T(8,128)(2,1)}, bf16[4,256,128]{2,1,0:T(8,128)(2,1)S(1)}, u32[]{:S(2)}, u32[]{:S(2)}) collective-permute-start(bf16[4,256,128]{2,1,0:T(8,128)(2,1)} %get-tuple-element.58), channel_id=1, source_target_pairs={{0,32},{16,48},{32,0},{48,16},{64,96},{80,112},{96,64},{112,80},{1... | collective-permute-start | bytes 786440 | tf_op jit(solution)/shard_map/ppermute | solution.py:365
  118.2 14.6 %collective-permute-start.2 = (bf16[4,256,128]{2,1,0:T(8,128)(2,1)}, bf16[4,256,128]{2,1,0:T(8,128)(2,1)S(1)}, u32[]{:S(2)}, u32[]{:S(2)}) collective-permute-start(bf16[4,256,128]{2,1,0:T(8,128)(2,1)} %get-tuple-element.59), channel_id=1, source_target_pairs={{0,48},{16,0},{32,16},{48,32},{64,112},{80,64},{96,80},{112,96},{1... | collective-permute-start | bytes 786440 | tf_op jit(solution)/shard_map/ppermute | solution.py:365
  120.7 12.9 %collective-permute-start.3 = (bf16[4,256,128]{2,1,0:T(8,128)(2,1)}, bf16[4,256,128]{2,1,0:T(8,128)(2,1)S(1)}, u32[]{:S(2)}, u32[]{:S(2)}) collective-permute-start(bf16[4,256,128]{2,1,0:T(8,128)(2,1)} %get-tuple-element.60), channel_id=1, source_target_pairs={{0,64},{16,80},{32,96},{48,112},{64,0},{80,16},{96,32},{112,48},{1... | collective-permute-start | bytes 786440 | tf_op jit(solution)/shard_map/ppermute | solution.py:365
  122.3 18.1 %collective-permute-start.4 = (bf16[4,256,128]{2,1,0:T(8,128)(2,1)}, bf16[4,256,128]{2,1,0:T(8,128)(2,1)S(1)}, u32[]{:S(2)}, u32[]{:S(2)}) collective-permute-start(bf16[4,256,128]{2,1,0:T(8,128)(2,1)} %get-tuple-element.61), channel_id=1, source_target_pairs={{0,80},{16,96},{32,112},{48,64},{64,16},{80,32},{96,48},{112,0},{1... | collective-permute-start | bytes 786440 | tf_op jit(solution)/shard_map/ppermute | solution.py:365
  129.5 0.7 copy-start.6
  130.2 12.0 %collective-permute-start.5 = (bf16[4,256,128]{2,1,0:T(8,128)(2,1)}, bf16[4,256,128]{2,1,0:T(8,128)(2,1)S(1)}, u32[]{:S(2)}, u32[]{:S(2)}) collective-permute-start(bf16[4,256,128]{2,1,0:T(8,128)(2,1)} %get-tuple-element.62), channel_id=1, source_target_pairs={{0,112},{16,64},{32,80},{48,96},{64,48},{80,0},{96,16},{112,32},{1... | collective-permute-start | bytes 786440 | tf_op jit(solution)/shard_map/ppermute | solution.py:365
  130.2 0.7 copy-start.8
  132.8 0.7 copy-start.10
  133.5 0.7 copy-start.12
  140.4 0.7 copy-start.14
  142.2 0.7 copy-start.16
  144.3 8.9 %copy-start.19 = (bf16[16,2,2,96,256]{4,3,2,1,0:T(8,128)(2,1)}, bf16[16,2,2,96,256]{4,3,2,1,0:T(8,128)(2,1)S(1)}, u32[]{:S(2)}) copy-start(bf16[16,2,2,96,256]{4,3,2,1,0:T(8,128)(2,1)S(1)} %all-to-all-done.1.got_ref) | copy-start | bytes 9437188
  144.3 48.8 %all-to-all-start.2 = ((bf16[16,2,2,96,256]{4,3,2,1,0:T(8,128)(2,1)}), bf16[16,2,2,96,256]{4,3,2,1,0:T(8,128)(2,1)}, u32[]{:S(2)}, u32[]{:S(2)}) async-start(bf16[16,2,2,96,256]{4,3,2,1,0:T(8,128)(2,1)} %get-tuple-element.64), calls=%async_computation.2 | async-start | bytes 6291456 | tf_op jit(solution)/shard_map/all_to_all | solution.py:350
  148.8 16.8 %collective-permute-start.6 = (bf16[4,256,128]{2,1,0:T(8,128)(2,1)}, bf16[4,256,128]{2,1,0:T(8,128)(2,1)S(1)}, u32[]{:S(2)}, u32[]{:S(2)}) collective-permute-start(bf16[4,256,128]{2,1,0:T(8,128)(2,1)} %get-tuple-element.65), channel_id=1, source_target_pairs={{0,96},{16,112},{32,64},{48,80},{64,32},{80,48},{96,0},{112,16},{1... | collective-permute-start | bytes 786440 | tf_op jit(solution)/shard_map/ppermute | solution.py:365
  153.2 24.2 %copy-start = (bf16[4,4,256,256]{3,2,1,0:T(8,128)(2,1)S(1)}, bf16[4,4,256,256]{3,2,1,0:T(8,128)(2,1)}, u32[]{:S(2)}) copy-start(bf16[4,4,256,256]{3,2,1,0:T(8,128)(2,1)} %refs_10_.5) | copy-start | bytes 6291460
  153.2 24.2 %copy-start.5 = (bf16[4,256,128]{2,1,0:T(8,128)(2,1)S(1)}, bf16[4,256,128]{2,1,0:T(8,128)(2,1)}, u32[]{:S(2)}) copy-start(bf16[4,256,128]{2,1,0:T(8,128)(2,1)} %get-tuple-element.74.refs_0_) | copy-start | bytes 786436
  153.2 24.2 %copy-start.7 = (bf16[4,256,128]{2,1,0:T(8,128)(2,1)S(1)}, bf16[4,256,128]{2,1,0:T(8,128)(2,1)}, u32[]{:S(2)}) copy-start(bf16[4,256,128]{2,1,0:T(8,128)(2,1)} %copy-done.6) | copy-start | bytes 786436
  153.2 24.2 %copy-start.9 = (bf16[4,256,128]{2,1,0:T(8,128)(2,1)S(1)}, bf16[4,256,128]{2,1,0:T(8,128)(2,1)}, u32[]{:S(2)}) copy-start(bf16[4,256,128]{2,1,0:T(8,128)(2,1)} %copy-done.8) | copy-start | bytes 786436
  153.3 24.2 %copy-start.11 = (bf16[4,256,128]{2,1,0:T(8,128)(2,1)S(1)}, bf16[4,256,128]{2,1,0:T(8,128)(2,1)}, u32[]{:S(2)}) copy-start(bf16[4,256,128]{2,1,0:T(8,128)(2,1)} %copy-done.10) | copy-start | bytes 786436
  153.3 24.2 %copy-start.13 = (bf16[4,256,128]{2,1,0:T(8,128)(2,1)S(1)}, bf16[4,256,128]{2,1,0:T(8,128)(2,1)}, u32[]{:S(2)}) copy-start(bf16[4,256,128]{2,1,0:T(8,128)(2,1)} %copy-done.12) | copy-start | bytes 786436
  153.3 24.2 %copy-start.15 = (bf16[4,256,128]{2,1,0:T(8,128)(2,1)S(1)}, bf16[4,256,128]{2,1,0:T(8,128)(2,1)}, u32[]{:S(2)}) copy-start(bf16[4,256,128]{2,1,0:T(8,128)(2,1)} %copy-done.14) | copy-start | bytes 786436
  153.3 24.2 %copy-start.17 = (bf16[4,256,128]{2,1,0:T(8,128)(2,1)S(1)}, bf16[4,256,128]{2,1,0:T(8,128)(2,1)}, u32[]{:S(2)}) copy-start(bf16[4,256,128]{2,1,0:T(8,128)(2,1)} %copy-done.16) | copy-start | bytes 786436
  153.3 24.2 %copy-start.18 = (s32[8,128]{1,0:T(8,128)S(1)}, s32[8,128]{1,0:T(8,128)}, u32[]{:S(2)}) copy-start(s32[8,128]{1,0:T(8,128)} %refs_9_.5) | copy-start | bytes 12292
  161.3 9.4 %collective-permute-start.7 = (bf16[2,2,256,128]{3,2,1,0:T(8,128)(2,1)}, bf16[2,2,256,128]{3,2,1,0:T(8,128)(2,1)S(1)}, u32[]{:S(2)}, u32[]{:S(2)}) collective-permute-start(bf16[2,2,256,128]{3,2,1,0:T(8,128)(2,1)} %get-tuple-element.68), channel_id=1, source_target_pairs={{0,16},{16,32},{32,48},{48,0},{64,80},{80,96},{96,112},{112,64},{1... | collective-permute-start | bytes 786440 | tf_op jit(solution)/shard_map/ppermute | solution.py:365
  161.4 22.5 %collective-permute-start.8 = (bf16[2,2,256,128]{3,2,1,0:T(8,128)(2,1)}, bf16[2,2,256,128]{3,2,1,0:T(8,128)(2,1)S(1)}, u32[]{:S(2)}, u32[]{:S(2)}) collective-permute-start(bf16[2,2,256,128]{3,2,1,0:T(8,128)(2,1)} %get-tuple-element.69), channel_id=1, source_target_pairs={{0,32},{16,48},{32,0},{48,16},{64,96},{80,112},{96,64},{112,80},{1... | collective-permute-start | bytes 786440 | tf_op jit(solution)/shard_map/ppermute | solution.py:365
  164.8 22.1 %collective-permute-start.9 = (bf16[2,2,256,128]{3,2,1,0:T(8,128)(2,1)}, bf16[2,2,256,128]{3,2,1,0:T(8,128)(2,1)S(1)}, u32[]{:S(2)}, u32[]{:S(2)}) collective-permute-start(bf16[2,2,256,128]{3,2,1,0:T(8,128)(2,1)} %get-tuple-element.70), channel_id=1, source_target_pairs={{0,48},{16,0},{32,16},{48,32},{64,112},{80,64},{96,80},{112,96},{1... | collective-permute-start | bytes 786440 | tf_op jit(solution)/shard_map/ppermute | solution.py:365
  165.2 23.0 %collective-permute-start.10 = (bf16[2,2,256,128]{3,2,1,0:T(8,128)(2,1)}, bf16[2,2,256,128]{3,2,1,0:T(8,128)(2,1)S(1)}, u32[]{:S(2)}, u32[]{:S(2)}) collective-permute-start(bf16[2,2,256,128]{3,2,1,0:T(8,128)(2,1)} %get-tuple-element.71), channel_id=1, source_target_pairs={{0,80},{16,96},{32,112},{48,64},{64,16},{80,32},{96,48},{112,0},{1... | collective-permute-start | bytes 786440 | tf_op jit(solution)/shard_map/ppermute | solution.py:365
  165.6 23.4 %collective-permute-start.11 = (bf16[2,2,256,128]{3,2,1,0:T(8,128)(2,1)}, bf16[2,2,256,128]{3,2,1,0:T(8,128)(2,1)S(1)}, u32[]{:S(2)}, u32[]{:S(2)}) collective-permute-start(bf16[2,2,256,128]{3,2,1,0:T(8,128)(2,1)} %get-tuple-element.72), channel_id=1, source_target_pairs={{0,96},{16,112},{32,64},{48,80},{64,32},{80,48},{96,0},{112,16},{1... | collective-permute-start | bytes 786440 | tf_op jit(solution)/shard_map/ppermute | solution.py:365
  170.8 21.6 %collective-permute-start.12 = (bf16[2,2,256,128]{3,2,1,0:T(8,128)(2,1)}, bf16[2,2,256,128]{3,2,1,0:T(8,128)(2,1)S(1)}, u32[]{:S(2)}, u32[]{:S(2)}) collective-permute-start(bf16[2,2,256,128]{3,2,1,0:T(8,128)(2,1)} %get-tuple-element.73), channel_id=1, source_target_pairs={{0,112},{16,64},{32,80},{48,96},{64,48},{80,0},{96,16},{112,32},{1... | collective-permute-start | bytes 786440 | tf_op jit(solution)/shard_map/ppermute | solution.py:365
  183.9 25.0 %collective-permute-start.20 = (bf16[2,2,256,128]{3,2,1,0:T(8,128)(2,1)}, bf16[2,2,256,128]{3,2,1,0:T(8,128)(2,1)}, u32[]{:S(2)}, u32[]{:S(2)}) collective-permute-start(bf16[2,2,256,128]{3,2,1,0:T(8,128)(2,1)} %get-tuple-element.94), channel_id=1, source_target_pairs={{0,64},{16,80},{32,96},{48,112},{64,0},{80,16},{96,32},{112,48},{1... | collective-permute-start | bytes 786440 | tf_op jit(solution)/shard_map/ppermute | solution.py:365
  192.3 0.7 copy-start.2
  193.0 29.3 %copy-start.1 = (bf16[2,2,256,128]{3,2,1,0:T(8,128)(2,1)S(1)}, bf16[2,2,256,128]{3,2,1,0:T(8,128)(2,1)}, u32[]{:S(2)}) copy-start(bf16[2,2,256,128]{3,2,1,0:T(8,128)(2,1)} %get-tuple-element.90.refs_0_) | copy-start | bytes 786436
  193.0 29.3 %copy-start.3 = (bf16[2,2,256,128]{3,2,1,0:T(8,128)(2,1)S(1)}, bf16[2,2,256,128]{3,2,1,0:T(8,128)(2,1)}, u32[]{:S(2)}) copy-start(bf16[2,2,256,128]{3,2,1,0:T(8,128)(2,1)} %copy-done.2) | copy-start | bytes 786436
  200.7 16.3 %collective-permute-start.13 = (bf16[2,2,256,128]{3,2,1,0:T(8,128)(2,1)}, bf16[2,2,256,128]{3,2,1,0:T(8,128)(2,1)S(1)}, u32[]{:S(2)}, u32[]{:S(2)}) collective-permute-start(bf16[2,2,256,128]{3,2,1,0:T(8,128)(2,1)} %get-tuple-element.83), channel_id=1, source_target_pairs={{0,16},{16,32},{32,48},{48,0},{64,80},{80,96},{96,112},{112,64},{1... | collective-permute-start | bytes 786440 | tf_op jit(solution)/shard_map/ppermute | solution.py:365
  204.8 12.2 %collective-permute-start.14 = (bf16[2,2,256,128]{3,2,1,0:T(8,128)(2,1)}, bf16[2,2,256,128]{3,2,1,0:T(8,128)(2,1)S(1)}, u32[]{:S(2)}, u32[]{:S(2)}) collective-permute-start(bf16[2,2,256,128]{3,2,1,0:T(8,128)(2,1)} %get-tuple-element.84), channel_id=1, source_target_pairs={{0,32},{16,48},{32,0},{48,16},{64,96},{80,112},{96,64},{112,80},{1... | collective-permute-start | bytes 786440 | tf_op jit(solution)/shard_map/ppermute | solution.py:365
  204.8 22.1 %collective-permute-start.15 = (bf16[2,2,256,128]{3,2,1,0:T(8,128)(2,1)}, bf16[2,2,256,128]{3,2,1,0:T(8,128)(2,1)S(1)}, u32[]{:S(2)}, u32[]{:S(2)}) collective-permute-start(bf16[2,2,256,128]{3,2,1,0:T(8,128)(2,1)} %get-tuple-element.85), channel_id=1, source_target_pairs={{0,48},{16,0},{32,16},{48,32},{64,112},{80,64},{96,80},{112,96},{1... | collective-permute-start | bytes 786440 | tf_op jit(solution)/shard_map/ppermute | solution.py:365
  206.9 23.1 %collective-permute-start.16 = (bf16[2,2,256,128]{3,2,1,0:T(8,128)(2,1)}, bf16[2,2,256,128]{3,2,1,0:T(8,128)(2,1)S(1)}, u32[]{:S(2)}, u32[]{:S(2)}) collective-permute-start(bf16[2,2,256,128]{3,2,1,0:T(8,128)(2,1)} %get-tuple-element.86), channel_id=1, source_target_pairs={{0,64},{16,80},{32,96},{48,112},{64,0},{80,16},{96,32},{112,48},{1... | collective-permute-start | bytes 786440 | tf_op jit(solution)/shard_map/ppermute | solution.py:365
  208.9 21.1 %collective-permute-start.17 = (bf16[2,2,256,128]{3,2,1,0:T(8,128)(2,1)}, bf16[2,2,256,128]{3,2,1,0:T(8,128)(2,1)S(1)}, u32[]{:S(2)}, u32[]{:S(2)}) collective-permute-start(bf16[2,2,256,128]{3,2,1,0:T(8,128)(2,1)} %get-tuple-element.87), channel_id=1, source_target_pairs={{0,80},{16,96},{32,112},{48,64},{64,16},{80,32},{96,48},{112,0},{1... | collective-permute-start | bytes 786440 | tf_op jit(solution)/shard_map/ppermute | solution.py:365
  217.0 13.0 %collective-permute-start.18 = (bf16[2,2,256,128]{3,2,1,0:T(8,128)(2,1)}, bf16[2,2,256,128]{3,2,1,0:T(8,128)(2,1)S(1)}, u32[]{:S(2)}, u32[]{:S(2)}) collective-permute-start(bf16[2,2,256,128]{3,2,1,0:T(8,128)(2,1)} %get-tuple-element.88), channel_id=1, source_target_pairs={{0,96},{16,112},{32,64},{48,80},{64,32},{80,48},{96,0},{112,16},{1... | collective-permute-start | bytes 786440 | tf_op jit(solution)/shard_map/ppermute | solution.py:365
  217.0 14.5 %copy-start.4 = (bf16[2,2,256,128]{3,2,1,0:T(8,128)(2,1)S(1)}, bf16[2,2,256,128]{3,2,1,0:T(8,128)(2,1)}, u32[]{:S(2)}) copy-start(bf16[2,2,256,128]{3,2,1,0:T(8,128)(2,1)} %get-tuple-element.82.refs_0_) | copy-start | bytes 786436
  217.0 14.5 %collective-permute-start.19 = (bf16[2,2,256,128]{3,2,1,0:T(8,128)(2,1)}, bf16[2,2,256,128]{3,2,1,0:T(8,128)(2,1)S(1)}, u32[]{:S(2)}, u32[]{:S(2)}) collective-permute-start(bf16[2,2,256,128]{3,2,1,0:T(8,128)(2,1)} %get-tuple-element.89), channel_id=1, source_target_pairs={{0,112},{16,64},{32,80},{48,96},{64,48},{80,0},{96,16},{112,32},{1... | collective-permute-start | bytes 786440 | tf_op jit(solution)/shard_map/ppermute | solution.py:365
